TPU v7x, 256 devices: a whole 4x4x8 slice. The times are simulated.
256 devices in a mesh: row: 4 (over y), col: 2 (over z_lo), depth: 32 (over z_hi, x, core).
Axes of the slice: x: 4, y: 4, z: 8 (z_hi: 4, z_lo: 2; z = z_hi * 2 + z_lo), core: 2. Of those that a mesh axis runs over, the one named last changes fastest.
Arguments:
- inputs: bfloat16 [1024, 12288], P(('col', 'depth'), 'row'), may hold values from -6 to 6
- weight: bfloat16 [12288, 49152], P('row', ('col', 'depth')), may hold values from -0.0546875 to 0.0546875
- out_grad: bfloat16 [1024, 49152], P('row', ('col', 'depth')), may hold values from -16 to 16
Outputs:
- activated: bfloat16 [1024, 49152], P('row', ('col', 'depth'))
- input_grad: bfloat16 [1024, 12288], P(('col', 'depth'), 'row')
- weight_grad: bfloat16 [12288, 49152], P('row', ('col', 'depth'))
All inputs are finite; a program needn't handle non-finite values.
Results may differ from a plain program's by a relative error of at most 0.0049.
Values may be sent and summed in bfloat16 or wider, within the bound.
No kernel may reach another device: no remote copies, remote signals or barrier semaphores. Data moves between devices by JAX's collectives and lax.ppermute only.
A program may use at most 128 MiB of HBM per device.

v0:
```python
import math

import jax
import jax.numpy as jnp
from jax import lax
from jax.sharding import PartitionSpec as P

gelu_coef = 0.044715


def gelu_pair(pre, cotangent):
    scale = math.sqrt(2.0 / math.pi)
    inner = scale * (pre + gelu_coef * pre * pre * pre)
    tanh_val = jnp.tanh(inner)
    activated = (0.5 * pre * (1.0 + tanh_val)).astype(jnp.bfloat16)
    slope = 0.5 * (1.0 + tanh_val) + 0.5 * pre * (1.0 - tanh_val * tanh_val) * scale * (
        1.0 + 3.0 * gelu_coef * pre * pre
    )
    pre_grad = (cotangent.astype(jnp.float32) * slope).astype(jnp.bfloat16)
    return (activated, pre_grad)


def body(inputs, weight, out_grad):
    gathered = lax.all_gather(inputs, ("col", "depth"), axis=0, tiled=True)
    partial_pre = jnp.dot(gathered, weight, preferred_element_type=jnp.float32)
    pre = lax.psum_scatter(partial_pre, "row", scatter_dimension=0, tiled=True)
    activated, pre_grad = gelu_pair(pre, out_grad)
    grad_all = lax.all_gather(pre_grad, "row", axis=0, tiled=True)
    weight_grad = lax.dot_general(
        gathered, grad_all, (((0,), (0,)), ((), ())), preferred_element_type=jnp.float32
    ).astype(jnp.bfloat16)
    input_grad = lax.psum_scatter(
        lax.dot_general(
            grad_all, weight, (((1,), (1,)), ((), ())), preferred_element_type=jnp.float32
        ),
        ("col", "depth"),
        scatter_dimension=0,
        tiled=True,
    )
    return (activated, input_grad.astype(jnp.bfloat16), weight_grad)


def solution(mesh):
    return jax.shard_map(
        body,
        mesh=mesh,
        in_specs=(
            P(("col", "depth"), "row"),
            P("row", ("col", "depth")),
            P("row", ("col", "depth")),
        ),
        out_specs=(
            P("row", ("col", "depth")),
            P(("col", "depth"), "row"),
            P("row", ("col", "depth")),
        ),
        check_vma=False,
    )
```

profile of v0, /device:TPU:56, one launch (start us, length us, event | category | flops | bytes accessed | tf_op | source)
XLA Modules:
  0.0 573.7 jit_solution(2355312599847938495)
XLA Ops:
  7.2 0.0 all-gather.3.cloned.1.call-start
  7.2 0.7 all-gather.3.cloned.1.call-update
  7.9 0.0 copy-start
  7.9 0.0 reduce-scatter.3.cloned.1.call-start
  8.0 122.6 %all-gather.3.cloned.1.call-done = bf16[1024,3072]{1,0:T(8,128)(2,1)} async-done(((bf16[16,3072]{1,0:T(8,128)(2,1)}), bf16[1024,3072]{1,0:T(8,128)(2,1)}) %all-gather.3.cloned.1.call-update) | async-done | bytes 6291472 | tf_op jit(solution)/shard_map/all_gather | solution.py:24
  130.6 9.6 %fusion.8 = f32[1024,768]{1,0:T(8,128)} fusion(bf16[1024,3072]{1,0:T(8,128)(2,1)} %all-gather.3.cloned.1.call-done, bf16[3072,768]{1,0:T(8,128)(2,1)} %param.4), kind=kOutput, calls=%fused_computation.12 | convolution fusion | flops 4831838208 | bytes 14155776 | tf_op jit(solution)/shard_map/dot_general | solution.py:25
  140.2 0.0 reduce-scatter.3.cloned.1.call-update
  140.3 0.0 all-gather.5.cloned.1.call-start
  140.3 37.2 %reduce-scatter.3.cloned.1.call-done = f32[256,768]{1,0:T(8,128)} async-done(((f32[1024,768]{1,0:T(8,128)}), f32[256,768]{1,0:T(8,128)}) %reduce-scatter.3.cloned.1.call-update) | async-done | bytes 786448 | tf_op jit(solution)/shard_map/reduce_scatter | solution.py:26
  177.5 0.0 copy-done
  177.5 2.6 fusion.7
  180.1 0.0 all-gather.5.cloned.1.call-update
  180.1 0.0 reduce-scatter.5.cloned.1.call-start
  180.1 29.8 %all-gather.5.cloned.1.call-done = bf16[1024,768]{1,0:T(8,128)(2,1)} async-done(((bf16[256,768]{1,0:T(8,128)(2,1)}), bf16[1024,768]{1,0:T(8,128)(2,1)}) %all-gather.5.cloned.1.call-update) | async-done | bytes 1572880 | tf_op jit(solution)/shard_map/all_gather | solution.py:28
  209.9 10.1 %fusion.9 = f32[1024,3072]{1,0:T(8,128)} fusion(bf16[1024,768]{1,0:T(8,128)(2,1)} %all-gather.5.cloned.1.call-done, bf16[3072,768]{1,0:T(8,128)(2,1)} %param.4), kind=kOutput, calls=%fused_computation.13 | convolution fusion | flops 4831838208 | bytes 18874368 | tf_op jit(solution)/shard_map/dot_general | solution.py:33
  220.0 0.0 copy-start.1
  220.0 0.0 reduce-scatter.5.cloned.1.call-update
  220.1 1.4 copy-done.1
  221.4 9.6 %fusion = bf16[3072,768]{0,1:T(8,128)(2,1)} fusion(bf16[1024,768]{1,0:T(8,128)(2,1)S(1)} %copy-done.1, bf16[1024,3072]{1,0:T(8,128)(2,1)} %all-gather.3.cloned.1.call-done), kind=kOutput, calls=%fused_computation.1 | convolution fusion | flops 4834197504 | bytes 12582912 | tf_op jit(solution)/shard_map/dot_general | solution.py:29
  231.0 6.6 %copy.6 = bf16[3072,768]{1,0:T(8,128)(2,1)} copy(bf16[3072,768]{0,1:T(8,128)(2,1)} %fusion) | data formatting | bytes 9437184
  237.6 328.0 %reduce-scatter.5.cloned.1.call-done = f32[16,3072]{1,0:T(8,128)} async-done(((f32[1024,3072]{1,0:T(8,128)}), f32[16,3072]{1,0:T(8,128)}) %reduce-scatter.5.cloned.1.call-update) | async-done | bytes 196624 | tf_op jit(solution)/shard_map/reduce_scatter | solution.py:32
  565.6 1.6 convert_element_type.21
Async XLA Ops:
  7.2 123.4 %all-gather.3.cloned.1.call-start = ((), (), s32[]{:S(2)}) async-start(), calls=%async_computation.2 | async-start | bytes 6389760 | tf_op jit(solution)/shard_map/all_gather | solution.py:24
  7.9 169.6 %copy-start = (bf16[256,768]{1,0:T(8,128)(2,1)S(1)}, bf16[256,768]{1,0:T(8,128)(2,1)}, u32[]{:S(2)}) copy-start(bf16[256,768]{1,0:T(8,128)(2,1)} %param.5) | copy-start | bytes 1179652
  7.9 169.6 %reduce-scatter.3.cloned.1.call-start = ((), (), s32[]{:S(2)}) async-start(), calls=%async_computation.3 | async-start | bytes 3932160 | tf_op jit(solution)/shard_map/reduce_scatter | solution.py:26
  140.3 69.6 %all-gather.5.cloned.1.call-start = ((), (), s32[]{:S(2)}) async-start(), calls=%async_computation.4 | async-start | bytes 1966080 | tf_op jit(solution)/shard_map/all_gather | solution.py:28
  180.1 385.5 %reduce-scatter.5.cloned.1.call-start = ((), (), s32[]{:S(2)}) async-start(), calls=%async_computation.5 | async-start | bytes 12779520 | tf_op jit(solution)/shard_map/reduce_scatter | solution.py:32
  220.0 1.4 copy-start.1
Sparse Core Ops, SparseCore 0:
  9.9 120.7 all-gather.2
  140.4 37.0 reduce-scatter.2
  180.2 29.6 all-gather.4
  220.2 345.3 reduce-scatter.4
where the time goes:
time: 576 us; the launch traced here: 574 us
  waiting for transfers between devices  518 us (90%)
  matrix products  29.4 us (5%)
  between operations  13.8 us (2%)
  local copies, waits for them, and re-layouts  8 us (1%)
    reduce_scatter x1, waiting for transfers between devices, body(): lax.psum_scatter(lax.dot_general(grad_all, weight, (((1,), (1,)), ((), ()...  328 us
    all_gather x1, waiting for transfers between devices, body(): gathered = lax.all_gather(inputs, ('col', 'depth'), axis=0, tiled=True)  123 us
    reduce_scatter x1, waiting for transfers between devices, body(): pre = lax.psum_scatter(partial_pre, 'row', scatter_dimension=0, tiled=True)  37.2 us
    all_gather x1, waiting for transfers between devices, body(): grad_all = lax.all_gather(pre_grad, 'row', axis=0, tiled=True)  29.8 us
  transfers between devices with their start and end apart: 4, of which 4 were waited for; matrix products, arithmetic and copies ran while one was open for 3% of the time, Pallas kernels for 0%

commit v1 on v0

v1 whole, which is shorter than its diff:
```python
import functools
import math

import jax
import jax.numpy as jnp
import numpy as np
from jax import lax
from jax.experimental import pallas as pl
from jax.experimental.pallas import tpu as pltpu
from jax.sharding import Mesh
from jax.sharding import PartitionSpec as P

gelu_coef = 0.044715

AXES = ("y", "zl", "zh", "x", "core")
SIZES = (4, 2, 4, 4, 2)
Z = ("zl", "zh")
BF = jnp.bfloat16
F32 = jnp.float32


def permute(array, move):
    pairs = []
    for y, zl, zh, x, core in np.ndindex(*SIZES):
        y2, x2, core2 = move(y, x, core)
        source = np.ravel_multi_index((y, zl, zh, x, core), SIZES)
        target = np.ravel_multi_index((y2, zl, zh, x2, core2), SIZES)
        pairs.append((int(source), int(target)))
    return lax.ppermute(array, AXES, pairs)


first = lambda core: 3 if core else 1
second = lambda core: 1 if core else 3
swap_core = lambda y, x, core: (y, x, 1 - core)
x_first = lambda y, x, core: (y, x ^ first(core), core)
x_second = lambda y, x, core: (y, x ^ second(core), core)
y_first = lambda y, x, core: (y ^ first(core), x, core)
y_second = lambda y, x, core: (y ^ second(core), x, core)


def gelu_pair(pre, cotangent):
    scale = math.sqrt(2.0 / math.pi)
    inner = scale * (pre + gelu_coef * pre * pre * pre)
    tanh_val = jnp.tanh(inner)
    activated = (0.5 * pre * (1.0 + tanh_val)).astype(BF)
    slope = 0.5 * (1.0 + tanh_val) + 0.5 * pre * (1.0 - tanh_val * tanh_val) * scale * (
        1.0 + 3.0 * gelu_coef * pre * pre
    )
    return activated, (cotangent.astype(F32) * slope).astype(BF)


def gelu_kernel(place_ref, own_ref, other_ref, cot_ref, act_ref, grad_ref):
    pre = own_ref[0] + other_ref[0].astype(F32)
    activated, grad = gelu_pair(pre, cot_ref[:, 0])
    act_ref[:, 0] = activated
    grad_ref[0] = grad


def gelu_call(place, own, other, cotangent):
    slots, two, t, f = own.shape
    local = pl.BlockSpec((1, two, t, f), lambda s, place: (s, 0, 0, 0))
    placed = pl.BlockSpec((two, 1, t, f), lambda s, place: (0, place[s], 0, 0))
    return pl.pallas_call(
        gelu_kernel,
        grid_spec=pltpu.PrefetchScalarGridSpec(
            num_scalar_prefetch=1,
            grid=(slots,),
            in_specs=[local, local, placed],
            out_specs=[placed, local],
        ),
        out_shape=[
            jax.ShapeDtypeStruct(cotangent.shape, BF),
            jax.ShapeDtypeStruct(own.shape, BF),
        ],
        cost_estimate=pl.CostEstimate(flops=30 * own.size, bytes_accessed=12 * own.size, transcendentals=own.size),
        name="gelu",
    )(place, own, other, cotangent)


def order_kernel(place_ref, a_ref, b_ref, c_ref, out_ref):
    out_ref[:, pl.ds(place_ref[0], 1)] = a_ref[...][:, None]
    out_ref[:, pl.ds(place_ref[1], 1)] = b_ref[...][:, None]
    out_ref[:, pl.ds(place_ref[2], 1)] = c_ref[0][:, None]
    out_ref[:, pl.ds(place_ref[3], 1)] = c_ref[1][:, None]


def order_call(place, a, b, c):
    slots, rows, f = a.shape
    whole = pl.BlockSpec(memory_space=pltpu.VMEM)
    return pl.pallas_call(
        order_kernel,
        in_specs=[pl.BlockSpec(memory_space=pltpu.SMEM), whole, whole, whole],
        out_specs=whole,
        out_shape=jax.ShapeDtypeStruct((slots, 4, rows, f), BF),
        compiler_params=pltpu.CompilerParams(vmem_limit_bytes=16 * 2**20),
        cost_estimate=pl.CostEstimate(flops=0, bytes_accessed=16 * a.size, transcendentals=0),
        name="order",
    )(place, a, b, c)


def body(inputs, weight, out_grad):
    y, x, core = lax.axis_index("y"), lax.axis_index("x"), lax.axis_index("core")
    t, d = inputs.shape
    f = weight.shape[1]
    near = jnp.where(core == 0, 1, 3)
    far = jnp.where(core == 0, 3, 1)
    pick = lambda a, i: lax.dynamic_index_in_dim(a, i, 1, keepdims=False)

    own = lax.all_to_all(jnp.broadcast_to(inputs[None], (8, t, d)), Z, 0, 0, tiled=True)
    one = permute(own, x_first)
    two = permute(own, x_second)
    three = permute(one, x_second)
    o0, o1, o2, o3 = (permute(p, swap_core) for p in (own, one, two, three))
    tokens = jnp.concatenate([own, o0, one, o2, two, o1, three, o3], 0).reshape(64 * t, d)

    part = jnp.dot(tokens, weight, preferred_element_type=F32).reshape(8, 4, 2 * t, f)
    send = jnp.stack([pick(part, y ^ near), pick(part, y ^ 2)]).astype(BF)
    got = permute(send, y_first).astype(F32)
    mine = pick(part, y) + got[0]
    theirs = pick(part, y ^ far) + got[1]
    got = permute(theirs.astype(BF), y_second)

    steps = jnp.stack([jnp.int32(0), near, far, jnp.int32(2)]).astype(jnp.int32)
    place = ((x ^ steps)[:, None] * 2 + (core ^ jnp.arange(2, dtype=jnp.int32))[None]).reshape(8).astype(jnp.int32)
    activated, grad = gelu_call(
        place, mine.reshape(8, 2, t, f), got.reshape(8, 2, t, f), out_grad.reshape(2, 8, t, f)
    )

    grad = grad.reshape(8, 2 * t, f)
    other = permute(grad, y_second)
    rest = permute(jnp.stack([grad, other]), y_first)
    order = jnp.stack([y, y ^ far, y ^ near, y ^ 2]).astype(jnp.int32)
    grad_all = order_call(order, grad, other, rest).reshape(64 * t, f)

    part = lax.dot_general(grad_all, weight, (((1,), (1,)), ((), ())), preferred_element_type=F32)
    part = part.reshape(4, 2, 8 * t, d)
    got = permute(part[:, 1].astype(BF), swap_core)
    total = part[:, 0] + jnp.stack([got[0], got[2], got[1], got[3]]).astype(F32)
    got = permute(total[2:].astype(BF), x_second)
    total = total[:2] + got.astype(F32)
    got = permute(total[1].astype(BF), x_first)
    total = (total[0] + got.astype(F32)).astype(BF)
    blocks = lax.all_to_all(total.reshape(8, t, d), Z, 0, 0, tiled=True)
    input_grad = jnp.sum(blocks.astype(F32), 0).astype(BF)

    weight_grad = lax.dot_general(tokens, grad_all, (((0,), (0,)), ((), ())), preferred_element_type=F32).astype(BF)
    return activated.reshape(16 * t, f), input_grad, weight_grad


def solution(mesh):
    fine = Mesh(mesh.devices.reshape(SIZES), AXES)
    tokens = ("zl", "zh", "x", "core")
    specs = (P(tokens, "y"), P("y", tokens), P("y", tokens))
    return jax.shard_map(
        body, mesh=fine, in_specs=specs, out_specs=(specs[1], specs[0], specs[1]), check_vma=False
    )
```

time: 576 us -> 208 us (0.36)
  waiting for transfers between devices: 518 us -> 115 us
  blocking collectives: 0 us -> 30 us
  starting transfers between devices: 0.16 us -> 13.5 us
  between operations: 13.8 us -> 0.89 us
  Pallas kernels: 0 us -> 6.72 us
    reduce_scatter x2 -> x0, waiting for transfers between devices: 365 us -> none  [the longest x1 328 us: body(): lax.psum_scatter(lax.dot_general(grad_all, weight, (((1,), (1,)), ((), ()...]
    all_gather x2 -> x0, waiting for transfers between devices: 152 us -> none  [the longest x1 123 us: body(): gathered = lax.all_gather(inputs, ('col', 'depth'), axis=0, tiled=True)]
    ppermute x0 -> x14, waiting for transfers between devices: none -> 105 us  [permute(): return lax.ppermute(array, AXES, pairs)]
    all_to_all x0 -> x1, blocking collectives: none -> 30 us  [body(): lax.all_to_all(jnp.broadcast_to(inputs[None], (8, t, d)), Z, 0, 0, tiled=...]
    all_to_all x0 -> x1, waiting for transfers between devices: none -> 10.2 us  [body(): blocks = lax.all_to_all(total.reshape(8, t, d), Z, 0, 0, tiled=True)]
    ppermute x0 -> x14, starting transfers between devices: none -> 9.18 us  [permute(): return lax.ppermute(array, AXES, pairs)]
    pallas_call x0 -> x2, Pallas kernels: none -> 6.72 us  [the longest x1 6.07 us: gelu_call(): pl.pallas_call(gelu_kernel, grid_spec=pltpu.PrefetchScalarGridSpec(num_sc...]
  transfers between devices with their start and end apart: 4 -> 15, of which waited for: 4 -> 11; matrix products, arithmetic and copies ran while one was open for 3% -> 6% of each run, Pallas kernels for 0% -> 0%
where the time goes in v1:
time: 208 us; the launch traced here: 207 us
  waiting for transfers between devices  115 us (55%)
  blocking collectives  30 us (14%)
  matrix products  26.2 us (13%)
  starting transfers between devices  13.5 us (6%)
  local copies, waits for them, and re-layouts  7.66 us (4%)
  other arithmetic  6.96 us (3%)
  Pallas kernels  6.72 us (3%)
    ppermute x14, waiting for transfers between devices, permute(): return lax.ppermute(array, AXES, pairs)  105 us
    all_to_all x1, blocking collectives, body(): lax.all_to_all(jnp.broadcast_to(inputs[None], (8, t, d)), Z, 0, 0, tiled=...  30 us
    all_to_all x1, waiting for transfers between devices, body(): blocks = lax.all_to_all(total.reshape(8, t, d), Z, 0, 0, tiled=True)  10.2 us
    dot_general x1, matrix products, body(): lax.dot_general(tokens, grad_all, (((0,), (0,)), ((), ())), preferred_ele...  9.64 us
    dot_general x1, matrix products, body(): jnp.dot(tokens, weight, preferred_element_type=F32).reshape(8, 4, 2 * t, f)  9.63 us
    ppermute x14, starting transfers between devices, permute(): return lax.ppermute(array, AXES, pairs)  9.18 us
    dot_general x1, matrix products, body(): lax.dot_general(grad_all, weight, (((1,), (1,)), ((), ())), preferred_ele...  6.97 us
    pallas_call x1, Pallas kernels, gelu_call(): pl.pallas_call(gelu_kernel, grid_spec=pltpu.PrefetchScalarGridSpec(num_sc...  6.07 us
  transfers between devices with their start and end apart: 15, of which 11 were waited for; matrix products, arithmetic and copies ran while one was open for 6% of the time, Pallas kernels for 0%

profile of v1, /device:TPU:56, one launch (start us, length us, event | category | flops | bytes accessed | tf_op | source)
XLA Modules:
  0.0 207.2 jit_solution(17646936778813520256)
XLA Ops:
  0.6 1.0 broadcast_in_dim.2
  1.6 30.0 %all_to_all.10 = bf16[8,16,3072]{2,1,0:T(8,128)(2,1)S(1)} all-to-all(bf16[8,16,3072]{2,1,0:T(8,128)(2,1)S(1)} %broadcast_in_dim.2), channel_id=1, replica_groups=mesh['y'=4,'zl'=2,'zh'=4,'x'=4,'core'=2] {'zl','zh'}, dimensions={0} | all-to-all | bytes 1572864 | tf_op jit(solution)/shard_map/all_to_all | solution.py:109
  31.6 2.8 %collective-permute-start.2 = (bf16[8,16,3072]{2,1,0:T(8,128)(2,1)S(1)}, bf16[8,16,3072]{2,1,0:T(8,128)(2,1)S(1)}, u32[]{:S(2)}, u32[]{:S(2)}) collective-permute-start(bf16[8,16,3072]{2,1,0:T(8,128)(2,1)S(1)} %all_to_all.10), channel_id=1, source_target_pairs={{0,6},{1,3},{2,4},{3,1},{4,2},{5,7},{6,0},{7,5},{8,14},{9,11},{10,... | collective-permute-start | bytes 2359304 | tf_op jit(solution)/shard_map/ppermute | solution.py:29
  34.4 0.2 collective-permute-start.1
  34.6 17.1 %collective-permute-done.2 = bf16[8,16,3072]{2,1,0:T(8,128)(2,1)S(1)} collective-permute-done((bf16[8,16,3072]{2,1,0:T(8,128)(2,1)S(1)}, bf16[8,16,3072]{2,1,0:T(8,128)(2,1)S(1)}, u32[]{:S(2)}, u32[]{:S(2)}) %collective-permute-start.2) | collective-permute-done | bytes 786464 | tf_op jit(solution)/shard_map/ppermute | solution.py:29
  51.8 2.1 %collective-permute-start.5 = (bf16[8,16,3072]{2,1,0:T(8,128)(2,1)S(1)}, bf16[8,16,3072]{2,1,0:T(8,128)(2,1)S(1)}, u32[]{:S(2)}, u32[]{:S(2)}) collective-permute-start(bf16[8,16,3072]{2,1,0:T(8,128)(2,1)S(1)} %collective-permute-done.1), channel_id=1, source_target_pairs={{0,6},{1,3},{2,4},{3,1},{4,2},{5,7},{6,0},{7,5},{8,14},{9,11},{10,... | collective-permute-start | bytes 2359304 | tf_op jit(solution)/shard_map/ppermute | solution.py:29
  53.9 0.1 collective-permute-start.4
  54.1 10.8 %collective-permute-done.5 = bf16[8,16,3072]{2,1,0:T(8,128)(2,1)S(1)} collective-permute-done((bf16[8,16,3072]{2,1,0:T(8,128)(2,1)S(1)}, bf16[8,16,3072]{2,1,0:T(8,128)(2,1)S(1)}, u32[]{:S(2)}, u32[]{:S(2)}) %collective-permute-start.5) | collective-permute-done | bytes 786464 | tf_op jit(solution)/shard_map/ppermute | solution.py:29
  65.3 2.0 collective-permute-done.6
  67.3 9.6 %fusion.3 = f32[8,4,32,768]{3,2,1,0:T(8,128)S(1)} fusion(bf16[8,4,32,3072]{3,2,1,0:T(8,128)(2,1)S(1)} %bitcast.72, bf16[3072,768]{1,0:T(8,128)(2,1)} %param.4), kind=kOutput, calls=%fused_computation.6 | convolution fusion | flops 4831838208 | bytes 14155776 | tf_op jit(solution)/shard_map/dot_general | solution.py:116
  77.0 0.1 fusion.12
  77.1 1.5 copy-done.1
  78.7 0.8 collective-permute-start.7
  79.5 11.2 %collective-permute-done.7 = bf16[2,8,32,768]{3,2,1,0:T(8,128)(2,1)S(1)} collective-permute-done((bf16[2,8,32,768]{3,2,1,0:T(8,128)(2,1)S(1)}, bf16[2,8,32,768]{3,2,1,0:T(8,128)(2,1)S(1)}, u32[]{:S(2)}, u32[]{:S(2)}) %collective-permute-start.7) | collective-permute-done | bytes 786464 | tf_op jit(solution)/shard_map/ppermute | solution.py:29
  90.8 0.1 convert_element_type.33
  90.9 1.2 fusion.10
  92.2 0.3 collective-permute-start.8
  92.6 0.6 add.49.place_ref
  93.2 1.2 constant_dynamic-slice_fusion
  94.5 1.0 add.53.own_ref
  95.5 5.8 %collective-permute-done.8 = bf16[8,32,768]{2,1,0:T(8,128)(2,1)S(1)} collective-permute-done((bf16[8,32,768]{2,1,0:T(8,128)(2,1)S(1)}, bf16[8,32,768]{2,1,0:T(8,128)(2,1)S(1)}, u32[]{:S(2)}, u32[]{:S(2)}) %collective-permute-start.8) | collective-permute-done | bytes 393248 | tf_op jit(solution)/shard_map/ppermute | solution.py:29
  101.2 0.8 copy-done.2
  102.0 6.1 %gelu.1 = (bf16[2,8,16,768]{3,2,1,0:T(8,128)(2,1)}, bf16[8,2,16,768]{3,2,1,0:T(8,128)(2,1)}) custom-call(s32[8]{0:T(128)} %add.49.place_ref, f32[8,2,16,768]{3,2,1,0:T(8,128)} %add.53.own_ref, bf16[8,2,16,768]{3,2,1,0:T(8,128)(2,1)} %bitcast.71, bf16[2,8,16,768]{3,2,1,0:T(8,128)(2,1)} %bitcast.70), custom_call_target="tpu_custom_call" | custom-call | flops 5898240 | bytes 2359296 | tf_op jit(solution)/shard_map/gelu/pallas_call | solution.py:63
  108.1 0.2 collective-permute-start.9
  108.3 9.0 %collective-permute-done.9.b_ref = bf16[8,32,768]{2,1,0:T(8,128)(2,1)S(1)} collective-permute-done((bf16[8,32,768]{2,1,0:T(8,128)(2,1)}, bf16[8,32,768]{2,1,0:T(8,128)(2,1)S(1)}, u32[]{:S(2)}, u32[]{:S(2)}) %collective-permute-start.9) | collective-permute-done | bytes 393248 | tf_op jit(solution)/shard_map/ppermute | solution.py:29
  117.3 1.1 pad_maximum_fusion.1
  118.4 0.3 collective-permute-start.10
  118.7 11.9 %collective-permute-done.10.c_ref = bf16[2,8,32,768]{3,2,1,0:T(8,128)(2,1)S(1)} collective-permute-done((bf16[2,8,32,768]{3,2,1,0:T(8,128)(2,1)S(1)}, bf16[2,8,32,768]{3,2,1,0:T(8,128)(2,1)S(1)}, u32[]{:S(2)}, u32[]{:S(2)}) %collective-permute-start.10) | collective-permute-done | bytes 786464 | tf_op jit(solution)/shard_map/ppermute | solution.py:29
  130.6 1.0 copy-done
  131.6 0.6 order.1
  132.3 7.0 %fusion.1 = f32[4,2,128,3072]{3,2,1,0:T(8,128)S(1)} fusion(bf16[4,2,128,768]{3,2,1,0:T(8,128)(2,1)S(1)} %bitcast.62, bf16[3072,768]{1,0:T(8,128)(2,1)} %param.4), kind=kOutput, calls=%fused_computation.4 | convolution fusion | flops 4831838208 | bytes 18874368 | tf_op jit(solution)/shard_map/dot_general | solution.py:135
  139.2 0.5 fusion.5
  139.7 0.1 collective-permute-start.11
  139.8 5.6 %collective-permute-done.11 = bf16[4,128,3072]{2,1,0:T(8,128)(2,1)S(1)} collective-permute-done((bf16[4,128,3072]{2,1,0:T(8,128)(2,1)S(1)}, bf16[4,128,3072]{2,1,0:T(8,128)(2,1)S(1)}, u32[]{:S(2)}, u32[]{:S(2)}) %collective-permute-start.11) | collective-permute-done | bytes 3145760 | tf_op jit(solution)/shard_map/ppermute | solution.py:29
  145.5 0.2 fusion.14
  145.7 0.9 fusion
  146.5 0.2 slice.84
  146.8 2.2 %collective-permute-start.12 = (bf16[2,128,3072]{2,1,0:T(8,128)(2,1)S(1)}, bf16[2,128,3072]{2,1,0:T(8,128)(2,1)S(1)}, u32[]{:S(2)}, u32[]{:S(2)}) collective-permute-start(bf16[2,128,3072]{2,1,0:T(8,128)(2,1)S(1)} %slice.84), channel_id=1, source_target_pairs={{0,6},{1,3},{2,4},{3,1},{4,2},{5,7},{6,0},{7,5},{8,14},{9,11},{10,... | collective-permute-start | bytes 4718600 | tf_op jit(solution)/shard_map/ppermute | solution.py:29
  148.9 19.5 %collective-permute-done.12 = bf16[2,128,3072]{2,1,0:T(8,128)(2,1)S(1)} collective-permute-done((bf16[2,128,3072]{2,1,0:T(8,128)(2,1)S(1)}, bf16[2,128,3072]{2,1,0:T(8,128)(2,1)S(1)}, u32[]{:S(2)}, u32[]{:S(2)}) %collective-permute-start.12) | collective-permute-done | bytes 1572896 | tf_op jit(solution)/shard_map/ppermute | solution.py:29
  168.5 0.5 slice_add_fusion
  169.0 0.1 fusion.8
  169.1 0.1 collective-permute-start.13
  169.2 12.0 %collective-permute-done.13 = bf16[128,3072]{1,0:T(8,128)(2,1)S(1)} collective-permute-done((bf16[128,3072]{1,0:T(8,128)(2,1)S(1)}, bf16[128,3072]{1,0:T(8,128)(2,1)S(1)}, u32[]{:S(2)}, u32[]{:S(2)}) %collective-permute-start.13) | collective-permute-done | bytes 786464 | tf_op jit(solution)/shard_map/ppermute | solution.py:29
  181.2 1.1 fusion.7
  182.3 4.3 %all-to-all-start.1 = ((bf16[8,16,3072]{2,1,0:T(8,128)(2,1)}), bf16[8,16,3072]{2,1,0:T(8,128)(2,1)S(1)}, u32[]{:S(2)}, u32[]{:S(2)}) async-start(bf16[8,16,3072]{2,1,0:T(8,128)(2,1)} %bitcast.27), calls=%async_computation.1 | async-start | bytes 1572864 | tf_op jit(solution)/shard_map/all_to_all | solution.py:143
  186.6 9.6 %convolution_convert_fusion = bf16[3072,768]{1,0:T(8,128)(2,1)} fusion(bf16[1024,3072]{1,0:T(8,128)(2,1)} %bitcast.73, bf16[1024,768]{1,0:T(8,128)(2,1)S(1)} %bitcast.63), kind=kOutput, calls=%fused_computation.3 | convolution fusion | flops 4834197504 | bytes 12582912 | tf_op jit(solution)/shard_map/dot_general | solution.py:146
  196.2 10.2 %all-to-all-done.1 = bf16[8,16,3072]{2,1,0:T(8,128)(2,1)S(1)} async-done(((bf16[8,16,3072]{2,1,0:T(8,128)(2,1)}), bf16[8,16,3072]{2,1,0:T(8,128)(2,1)S(1)}, u32[]{:S(2)}, u32[]{:S(2)}) %all-to-all-start.1) | async-done | bytes 786464 | tf_op jit(solution)/shard_map/all_to_all | solution.py:143
  206.4 0.8 reduce_sum.12
  (26 shorter events, 0.9 us)
Async XLA Ops:
  31.6 20.1 %collective-permute-start.2 = (bf16[8,16,3072]{2,1,0:T(8,128)(2,1)S(1)}, bf16[8,16,3072]{2,1,0:T(8,128)(2,1)S(1)}, u32[]{:S(2)}, u32[]{:S(2)}) collective-permute-start(bf16[8,16,3072]{2,1,0:T(8,128)(2,1)S(1)} %all_to_all.10), channel_id=1, source_target_pairs={{0,6},{1,3},{2,4},{3,1},{4,2},{5,7},{6,0},{7,5},{8,14},{9,11},{10,... | collective-permute-start | bytes 2359304 | tf_op jit(solution)/shard_map/ppermute | solution.py:29
  34.4 17.4 %collective-permute-start.1 = (bf16[8,16,3072]{2,1,0:T(8,128)(2,1)S(1)}, bf16[8,16,3072]{2,1,0:T(8,128)(2,1)S(1)}, u32[]{:S(2)}, u32[]{:S(2)}) collective-permute-start(bf16[8,16,3072]{2,1,0:T(8,128)(2,1)S(1)} %all_to_all.10), channel_id=1, source_target_pairs={{0,2},{1,7},{2,0},{3,5},{4,6},{5,3},{6,4},{7,1},{8,10},{9,15},{10,... | collective-permute-start | bytes 2359304 | tf_op jit(solution)/shard_map/ppermute | solution.py:29
  34.6 19.4 %collective-permute-start = (bf16[8,16,3072]{2,1,0:T(8,128)(2,1)S(1)}, bf16[8,16,3072]{2,1,0:T(8,128)(2,1)S(1)}, u32[]{:S(2)}, u32[]{:S(2)}) collective-permute-start(bf16[8,16,3072]{2,1,0:T(8,128)(2,1)S(1)} %all_to_all.10), channel_id=1, source_target_pairs={{0,1},{1,0},{2,3},{3,2},{4,5},{5,4},{6,7},{7,6},{8,9},{9,8},{10,11... | collective-permute-start | bytes 2359304 | tf_op jit(solution)/shard_map/ppermute | solution.py:29
  51.7 13.2 %collective-permute-start.3 = (bf16[8,16,3072]{2,1,0:T(8,128)(2,1)S(1)}, bf16[8,16,3072]{2,1,0:T(8,128)(2,1)S(1)}, u32[]{:S(2)}, u32[]{:S(2)}) collective-permute-start(bf16[8,16,3072]{2,1,0:T(8,128)(2,1)S(1)} %collective-permute-done.2), channel_id=1, source_target_pairs={{0,1},{1,0},{2,3},{3,2},{4,5},{5,4},{6,7},{7,6},{8,9},{9,8},{10,11... | collective-permute-start | bytes 2359304 | tf_op jit(solution)/shard_map/ppermute | solution.py:29
  51.8 13.2 %collective-permute-start.5 = (bf16[8,16,3072]{2,1,0:T(8,128)(2,1)S(1)}, bf16[8,16,3072]{2,1,0:T(8,128)(2,1)S(1)}, u32[]{:S(2)}, u32[]{:S(2)}) collective-permute-start(bf16[8,16,3072]{2,1,0:T(8,128)(2,1)S(1)} %collective-permute-done.1), channel_id=1, source_target_pairs={{0,6},{1,3},{2,4},{3,1},{4,2},{5,7},{6,0},{7,5},{8,14},{9,11},{10,... | collective-permute-start | bytes 2359304 | tf_op jit(solution)/shard_map/ppermute | solution.py:29
  53.9 11.2 %collective-permute-start.4 = (bf16[8,16,3072]{2,1,0:T(8,128)(2,1)S(1)}, bf16[8,16,3072]{2,1,0:T(8,128)(2,1)S(1)}, u32[]{:S(2)}, u32[]{:S(2)}) collective-permute-start(bf16[8,16,3072]{2,1,0:T(8,128)(2,1)S(1)} %collective-permute-done.1), channel_id=1, source_target_pairs={{0,1},{1,0},{2,3},{3,2},{4,5},{5,4},{6,7},{7,6},{8,9},{9,8},{10,11... | collective-permute-start | bytes 2359304 | tf_op jit(solution)/shard_map/ppermute | solution.py:29
  65.0 2.3 %collective-permute-start.6 = (bf16[8,16,3072]{2,1,0:T(8,128)(2,1)S(1)}, bf16[8,16,3072]{2,1,0:T(8,128)(2,1)S(1)}, u32[]{:S(2)}, u32[]{:S(2)}) collective-permute-start(bf16[8,16,3072]{2,1,0:T(8,128)(2,1)S(1)} %collective-permute-done.5), channel_id=1, source_target_pairs={{0,1},{1,0},{2,3},{3,2},{4,5},{5,4},{6,7},{7,6},{8,9},{9,8},{10,11... | collective-permute-start | bytes 2359304 | tf_op jit(solution)/shard_map/ppermute | solution.py:29
  67.3 9.6 %copy-start.3 = (bf16[64,16,3072]{2,1,0:T(8,128)(2,1)}, bf16[64,16,3072]{2,1,0:T(8,128)(2,1)S(1)}, u32[]{:S(2)}) copy-start(bf16[64,16,3072]{2,1,0:T(8,128)(2,1)S(1)} %constant_dynamic-update-slice_fusion) | copy-start | bytes 18874372
  77.0 1.7 copy-start.1
  78.7 12.1 %collective-permute-start.7 = (bf16[2,8,32,768]{3,2,1,0:T(8,128)(2,1)S(1)}, bf16[2,8,32,768]{3,2,1,0:T(8,128)(2,1)S(1)}, u32[]{:S(2)}, u32[]{:S(2)}) collective-permute-start(bf16[2,8,32,768]{3,2,1,0:T(8,128)(2,1)S(1)} %pad_maximum_fusion), channel_id=1, source_target_pairs={{0,64},{1,193},{2,66},{3,195},{4,68},{5,197},{6,70},{7,199},{8,72}... | collective-permute-start | bytes 2359304 | tf_op jit(solution)/shard_map/ppermute | solution.py:29
  92.2 9.1 %collective-permute-start.8 = (bf16[8,32,768]{2,1,0:T(8,128)(2,1)S(1)}, bf16[8,32,768]{2,1,0:T(8,128)(2,1)S(1)}, u32[]{:S(2)}, u32[]{:S(2)}) collective-permute-start(bf16[8,32,768]{2,1,0:T(8,128)(2,1)S(1)} %fusion.10), channel_id=1, source_target_pairs={{0,192},{1,65},{2,194},{3,67},{4,196},{5,69},{6,198},{7,71},{8,200... | collective-permute-start | bytes 1179656 | tf_op jit(solution)/shard_map/ppermute | solution.py:29
  101.2 0.8 copy-start.2
  108.1 9.2 %collective-permute-start.9 = (bf16[8,32,768]{2,1,0:T(8,128)(2,1)}, bf16[8,32,768]{2,1,0:T(8,128)(2,1)S(1)}, u32[]{:S(2)}, u32[]{:S(2)}) collective-permute-start(bf16[8,32,768]{2,1,0:T(8,128)(2,1)} %bitcast.64), channel_id=1, source_target_pairs={{0,192},{1,65},{2,194},{3,67},{4,196},{5,69},{6,198},{7,71},{8,200... | collective-permute-start | bytes 1179656 | tf_op jit(solution)/shard_map/ppermute | solution.py:29
  118.4 12.3 %collective-permute-start.10 = (bf16[2,8,32,768]{3,2,1,0:T(8,128)(2,1)S(1)}, bf16[2,8,32,768]{3,2,1,0:T(8,128)(2,1)S(1)}, u32[]{:S(2)}, u32[]{:S(2)}) collective-permute-start(bf16[2,8,32,768]{3,2,1,0:T(8,128)(2,1)S(1)} %pad_maximum_fusion.1), channel_id=1, source_target_pairs={{0,64},{1,193},{2,66},{3,195},{4,68},{5,197},{6,70},{7,199},{8,72}... | collective-permute-start | bytes 2359304 | tf_op jit(solution)/shard_map/ppermute | solution.py:29
  130.6 1.0 copy-start
  139.7 5.7 %collective-permute-start.11 = (bf16[4,128,3072]{2,1,0:T(8,128)(2,1)S(1)}, bf16[4,128,3072]{2,1,0:T(8,128)(2,1)S(1)}, u32[]{:S(2)}, u32[]{:S(2)}) collective-permute-start(bf16[4,128,3072]{2,1,0:T(8,128)(2,1)S(1)} %fusion.5), channel_id=1, source_target_pairs={{0,1},{1,0},{2,3},{3,2},{4,5},{5,4},{6,7},{7,6},{8,9},{9,8},{10,11... | collective-permute-start | bytes 9437192 | tf_op jit(solution)/shard_map/ppermute | solution.py:29
  146.8 21.7 %collective-permute-start.12 = (bf16[2,128,3072]{2,1,0:T(8,128)(2,1)S(1)}, bf16[2,128,3072]{2,1,0:T(8,128)(2,1)S(1)}, u32[]{:S(2)}, u32[]{:S(2)}) collective-permute-start(bf16[2,128,3072]{2,1,0:T(8,128)(2,1)S(1)} %slice.84), channel_id=1, source_target_pairs={{0,6},{1,3},{2,4},{3,1},{4,2},{5,7},{6,0},{7,5},{8,14},{9,11},{10,... | collective-permute-start | bytes 4718600 | tf_op jit(solution)/shard_map/ppermute | solution.py:29
  169.1 12.1 %collective-permute-start.13 = (bf16[128,3072]{1,0:T(8,128)(2,1)S(1)}, bf16[128,3072]{1,0:T(8,128)(2,1)S(1)}, u32[]{:S(2)}, u32[]{:S(2)}) collective-permute-start(bf16[128,3072]{1,0:T(8,128)(2,1)S(1)} %fusion.8), channel_id=1, source_target_pairs={{0,2},{1,7},{2,0},{3,5},{4,6},{5,3},{6,4},{7,1},{8,10},{9,15},{10,... | collective-permute-start | bytes 2359304 | tf_op jit(solution)/shard_map/ppermute | solution.py:29
  182.3 24.1 %all-to-all-start.1 = ((bf16[8,16,3072]{2,1,0:T(8,128)(2,1)}), bf16[8,16,3072]{2,1,0:T(8,128)(2,1)S(1)}, u32[]{:S(2)}, u32[]{:S(2)}) async-start(bf16[8,16,3072]{2,1,0:T(8,128)(2,1)} %bitcast.27), calls=%async_computation.1 | async-start | bytes 1572864 | tf_op jit(solution)/shard_map/all_to_all | solution.py:143

commit v2 on v1

v2 whole, which is shorter than its diff:
```python
import functools
import math

import jax
import jax.numpy as jnp
import numpy as np
from jax import lax
from jax.experimental import pallas as pl
from jax.experimental.pallas import tpu as pltpu
from jax.sharding import Mesh
from jax.sharding import PartitionSpec as P

gelu_coef = 0.044715

AXES = ("y", "zl", "zh", "x", "core")
SIZES = (4, 2, 4, 4, 2)
Z = ("zl", "zh")
BF = jnp.bfloat16
F32 = jnp.float32


def permute(array, move):
    pairs = []
    for y, zl, zh, x, core in np.ndindex(*SIZES):
        y2, x2, core2 = move(y, x, core)
        source = np.ravel_multi_index((y, zl, zh, x, core), SIZES)
        target = np.ravel_multi_index((y2, zl, zh, x2, core2), SIZES)
        pairs.append((int(source), int(target)))
    return lax.ppermute(array, AXES, pairs)


first = lambda core: 3 if core else 1
second = lambda core: 1 if core else 3
swap_core = lambda y, x, core: (y, x, 1 - core)
x_first = lambda y, x, core: (y, x ^ first(core), core)
x_second = lambda y, x, core: (y, x ^ second(core), core)
y_first = lambda y, x, core: (y ^ first(core), x, core)
y_second = lambda y, x, core: (y ^ second(core), x, core)


def gelu_pair(pre, cotangent):
    scale = math.sqrt(2.0 / math.pi)
    inner = scale * (pre + gelu_coef * pre * pre * pre)
    tanh_val = jnp.tanh(inner)
    activated = (0.5 * pre * (1.0 + tanh_val)).astype(BF)
    slope = 0.5 * (1.0 + tanh_val) + 0.5 * pre * (1.0 - tanh_val * tanh_val) * scale * (
        1.0 + 3.0 * gelu_coef * pre * pre
    )
    return activated, (cotangent.astype(F32) * slope).astype(BF)


def gelu_kernel(place_ref, own_ref, other_ref, cot_ref, act_ref, grad_ref):
    for slot in range(own_ref.shape[0]):
        pre = own_ref[slot] + other_ref[slot].astype(F32)
        activated, grad = gelu_pair(pre, cot_ref[place_ref[slot]])
        act_ref[place_ref[slot]] = activated
        grad_ref[slot] = grad


def gelu_call(place, own, other, cotangent):
    whole = pl.BlockSpec(memory_space=pltpu.VMEM)
    return pl.pallas_call(
        gelu_kernel,
        in_specs=[pl.BlockSpec(memory_space=pltpu.SMEM), whole, whole, whole],
        out_specs=[whole, whole],
        out_shape=[jax.ShapeDtypeStruct(own.shape, BF)] * 2,
        compiler_params=pltpu.CompilerParams(vmem_limit_bytes=16 * 2**20),
        cost_estimate=pl.CostEstimate(flops=30 * own.size, bytes_accessed=12 * own.size, transcendentals=own.size),
        name="gelu",
    )(place, own, other, cotangent)


def order_kernel(place_ref, a_ref, b_ref, c_ref, out_ref):
    out_ref[:, pl.ds(place_ref[0], 1)] = a_ref[...][:, None]
    out_ref[:, pl.ds(place_ref[1], 1)] = b_ref[...][:, None]
    out_ref[:, pl.ds(place_ref[2], 1)] = c_ref[0][:, None]
    out_ref[:, pl.ds(place_ref[3], 1)] = c_ref[1][:, None]


def order_call(place, a, b, c):
    slots, rows, f = a.shape
    whole = pl.BlockSpec(memory_space=pltpu.VMEM)
    return pl.pallas_call(
        order_kernel,
        in_specs=[pl.BlockSpec(memory_space=pltpu.SMEM), whole, whole, whole],
        out_specs=whole,
        out_shape=jax.ShapeDtypeStruct((slots, 4, rows, f), BF),
        compiler_params=pltpu.CompilerParams(vmem_limit_bytes=16 * 2**20),
        cost_estimate=pl.CostEstimate(flops=0, bytes_accessed=16 * a.size, transcendentals=0),
        name="order",
    )(place, a, b, c)


CHUNKS = 2


def after(value, *others):
    return lax.optimization_barrier((value, *others))[0]


class Chunk:
    pass


def body(inputs, weight, out_grad):
    y, x, core = lax.axis_index("y"), lax.axis_index("x"), lax.axis_index("core")
    d, f = weight.shape
    t = inputs.shape[0] // CHUNKS
    near = jnp.where(core == 0, 1, 3)
    far = jnp.where(core == 0, 3, 1)
    pick = lambda a, i: lax.dynamic_index_in_dim(a, i, 1, keepdims=False)

    steps = jnp.stack([jnp.int32(0), near, far, jnp.int32(2)]).astype(jnp.int32)
    place = ((x ^ steps)[None] * 2 + (core ^ jnp.arange(2, dtype=jnp.int32))[:, None]).reshape(8).astype(jnp.int32)
    order = jnp.stack([y, y ^ far, y ^ near, y ^ 2]).astype(jnp.int32)
    cotangents = jnp.transpose(out_grad.reshape(2, 8, CHUNKS, t, f), (2, 1, 0, 3, 4)).reshape(CHUNKS, 8, 2 * t, f)

    def spread(c, block):
        c.own = lax.all_to_all(jnp.broadcast_to(block[None], (8, t, d)), Z, 0, 0, tiled=True)

    def along_x(c, *wait):
        source = after(c.own, *wait) if wait else c.own
        c.one = permute(source, x_first)
        c.two = permute(source, x_second)
        c.three = permute(c.one, x_second)

    def assemble(c):
        c.other = [permute(p, swap_core) for p in (c.own, c.two, c.one, c.three)]
        c.tokens = jnp.concatenate([c.own, c.one, c.two, c.three] + c.other, 0).reshape(64 * t, d)

    def project(c, *wait):
        tokens = after(c.tokens, *wait) if wait else c.tokens
        c.part = jnp.dot(tokens, weight, preferred_element_type=F32).reshape(8, 4, 2 * t, f)
        c.send = jnp.stack([pick(c.part, y ^ near), pick(c.part, y ^ 2)]).astype(BF)

    def sum_first(c):
        got = permute(c.send, y_first).astype(F32)
        c.mine = pick(c.part, y) + got[0]
        c.theirs = (pick(c.part, y ^ far) + got[1]).astype(BF)

    def sum_second(c):
        c.got = permute(c.theirs, y_second)

    def gelu(c, cotangent, *wait):
        got = after(c.got, *wait) if wait else c.got
        c.activated, c.grad = gelu_call(place, c.mine, got, cotangent)

    def spread_first(c):
        c.grad_far = permute(c.grad, y_second)

    def spread_second(c, wait=(), behind=()):
        rest = permute(after(jnp.stack([c.grad, c.grad_far]), *wait), y_first)
        c.grad_all = order_call(order, c.grad, c.grad_far, after(rest, *behind)).reshape(2, 32 * t, f)

    def back(c, *wait):
        dims = (((1,), (1,)), ((), ()))
        give = lax.dot_general(c.grad_all[1], weight, dims, preferred_element_type=F32).astype(BF)
        keep = lax.dot_general(c.grad_all[0], weight, dims, preferred_element_type=F32).reshape(4, 8 * t, d)
        got = permute(give.reshape(4, 8 * t, d), swap_core)
        c.away = (keep[2:] + jnp.stack([got[1], got[3]]).astype(F32)).astype(BF)
        c.here = keep[:2] + jnp.stack([got[0], got[2]]).astype(F32)

    def reduce_first(c, wait=(), behind=()):
        got = after(permute(after(c.away, *wait), x_second), *behind).astype(F32)
        c.away = (c.here[1] + got[1]).astype(BF)
        c.here = c.here[0] + got[0]

    def reduce_second(c, *wait):
        got = permute(after(c.away, *wait) if wait else c.away, x_first).astype(F32)
        c.total = (c.here + got).astype(BF).reshape(8, t, d)

    def reduce_last(c, *wait):
        total = after(c.total, *wait) if wait else c.total
        blocks = lax.all_to_all(total, Z, 0, 0, tiled=True)
        c.input_grad = jnp.sum(blocks.astype(F32), 0).astype(BF)

    def weights(c, *wait):
        grads = after(c.grad_all, *wait).reshape(64 * t, f)
        return lax.dot_general(c.tokens, grads, (((0,), (0,)), ((), ())), preferred_element_type=F32)

    a, b = Chunk(), Chunk()
    spread(a, inputs[:t])
    along_x(a)
    spread(b, after(inputs[t:], a.own))
    assemble(a)
    along_x(b, a.three)
    project(a)
    sum_first(a)
    sum_second(a)
    assemble(b)
    project(b, a.theirs)
    gelu(a, cotangents[0])
    spread_first(a)
    sum_first(b)
    spread_second(a)
    sum_second(b)
    gelu(b, cotangents[1], a.grad_far)
    back(a)
    spread_first(b)
    wa = weights(a, a.away)
    sent = a.away
    reduce_first(a)
    spread_second(b, wait=(sent,), behind=(wa,))
    back(b)
    sent = a.away
    reduce_second(a)
    wb = weights(b, b.away, a.total)
    weight_grad = (wa + wb).astype(BF)
    reduce_first(b, wait=(sent,), behind=(weight_grad,))
    reduce_last(a)
    reduce_second(b)
    reduce_last(b)

    input_grad = jnp.concatenate([a.input_grad, b.input_grad], 0)
    activated = jnp.stack([after(a.activated, b.total), b.activated]).reshape(CHUNKS, 8, 2, t, f)
    activated = jnp.transpose(activated, (2, 1, 0, 3, 4)).reshape(out_grad.shape)
    return activated, input_grad, weight_grad


def solution(mesh):
    fine = Mesh(mesh.devices.reshape(SIZES), AXES)
    tokens = ("zl", "zh", "x", "core")
    specs = (P(tokens, "y"), P("y", tokens), P("y", tokens))
    return jax.shard_map(
        body, mesh=fine, in_specs=specs, out_specs=(specs[1], specs[0], specs[1]), check_vma=False
    )
```

time: 208 us -> 176 us (0.85)
  blocking collectives: 30 us -> 0 us
  starting transfers between devices: 13.5 us -> 38.7 us
  waiting for transfers between devices: 115 us -> 90.5 us
  local copies, waits for them, and re-layouts: 7.66 us -> 12.6 us
  matrix products: 26.2 us -> 21.9 us
  Pallas kernels: 6.72 us -> 2.93 us
    ppermute x14 -> x28, waiting for transfers between devices: 105 us -> 54.9 us  [permute(): return lax.ppermute(array, AXES, pairs)]
    all_to_all x1 -> x0, blocking collectives: 30 us -> none  [body(): lax.all_to_all(jnp.broadcast_to(inputs[None], (8, t, d)), Z, 0, 0, tiled=...]
    all_to_all x1 -> x4, waiting for transfers between devices: 10.2 us -> 35.6 us  [the longest x2 18.9 us: spread(): lax.all_to_all(jnp.broadcast_to(block[None], (8, t, d)), Z, 0, 0, tiled=T...]
    all_to_all x1 -> x4, starting transfers between devices: 4.29 us -> 20.2 us  [the longest x2 12 us: spread(): lax.all_to_all(jnp.broadcast_to(block[None], (8, t, d)), Z, 0, 0, tiled=T...]
    ppermute x14 -> x28, starting transfers between devices: 9.18 us -> 18.6 us  [permute(): return lax.ppermute(array, AXES, pairs)]
    pallas_call x1 -> x2, Pallas kernels: 6.07 us -> 1.74 us  [gelu_call(): pl.pallas_call(gelu_kernel, in_specs=[pl.BlockSpec(memory_space=pltpu.SME...]
    dot_general x3 -> x8, matrix products: 26.2 us -> 21.9 us  [the longest x2 9.14 us: weights(): lax.dot_general(c.tokens, grads, (((0,), (0,)), ((), ())), preferred_elem...]
    unnamed x15 -> x18, local copies, waits for them, and re-layouts: 3.72 us -> 6.6 us
  transfers between devices with their start and end apart: 15 -> 32, of which waited for: 11 -> 18; matrix products, arithmetic and copies ran while one was open for 6% -> 20% of each run, Pallas kernels for 0% -> 1%
where the time goes in v2:
time: 176 us; the launch traced here: 173 us
  waiting for transfers between devices  90.5 us (51%)
  starting transfers between devices  38.7 us (22%)
  matrix products  21.9 us (12%)
  local copies, waits for them, and re-layouts  12.6 us (7%)
  other arithmetic  5.63 us (3%)
  Pallas kernels  2.93 us (2%)
    ppermute x28, waiting for transfers between devices, permute(): return lax.ppermute(array, AXES, pairs)  54.9 us
    all_to_all x2, waiting for transfers between devices, spread(): lax.all_to_all(jnp.broadcast_to(block[None], (8, t, d)), Z, 0, 0, tiled=T...  18.9 us
    ppermute x28, starting transfers between devices, permute(): return lax.ppermute(array, AXES, pairs)  18.6 us
    all_to_all x2, waiting for transfers between devices, reduce_last(): blocks = lax.all_to_all(total, Z, 0, 0, tiled=True)  16.7 us
    all_to_all x2, starting transfers between devices, spread(): lax.all_to_all(jnp.broadcast_to(block[None], (8, t, d)), Z, 0, 0, tiled=T...  12 us
    dot_general x2, matrix products, weights(): lax.dot_general(c.tokens, grads, (((0,), (0,)), ((), ())), preferred_elem...  9.14 us
    all_to_all x2, starting transfers between devices, reduce_last(): blocks = lax.all_to_all(total, Z, 0, 0, tiled=True)  8.18 us
    dot_general x2, matrix products, project(): jnp.dot(tokens, weight, preferred_element_type=F32).reshape(8, 4, 2 * t, f)  7.09 us
  transfers between devices with their start and end apart: 32, of which 18 were waited for; matrix products, arithmetic and copies ran while one was open for 20% of the time, Pallas kernels for 1%

profile of v2, /device:TPU:56, one launch (start us, length us, event | category | flops | bytes accessed | tf_op | source)
XLA Modules:
  0.0 173.4 jit_solution(13037111070473175316)
XLA Ops:
  0.6 0.8 fusion.34
  2.2 8.6 %all-to-all-start = ((bf16[8,8,3072]{2,1,0:T(8,128)(2,1)}), bf16[8,8,3072]{2,1,0:T(8,128)(2,1)S(1)}, u32[]{:S(2)}, u32[]{:S(2)}) async-start(bf16[8,8,3072]{2,1,0:T(8,128)(2,1)} %broadcast_in_dim.4), calls=%async_computation | async-start | bytes 786432 | tf_op jit(solution)/shard_map/all_to_all | solution.py:119
  10.8 1.0 copy.22
  12.0 12.1 %all-to-all-done = bf16[8,8,3072]{2,1,0:T(8,128)(2,1)S(1)} async-done(((bf16[8,8,3072]{2,1,0:T(8,128)(2,1)}), bf16[8,8,3072]{2,1,0:T(8,128)(2,1)S(1)}, u32[]{:S(2)}, u32[]{:S(2)}) %all-to-all-start) | async-done | bytes 393248 | tf_op jit(solution)/shard_map/all_to_all | solution.py:119
  24.0 2.8 %collective-permute-start.1 = (bf16[8,8,3072]{2,1,0:T(8,128)(2,1)S(1)}, bf16[8,8,3072]{2,1,0:T(8,128)(2,1)S(1)}, u32[]{:S(2)}, u32[]{:S(2)}) collective-permute-start(bf16[8,8,3072]{2,1,0:T(8,128)(2,1)S(1)} %all-to-all-done), channel_id=1, source_target_pairs={{0,6},{1,3},{2,4},{3,1},{4,2},{5,7},{6,0},{7,5},{8,14},{9,11},{10,... | collective-permute-start | bytes 1179656 | tf_op jit(solution)/shard_map/ppermute | solution.py:29
  27.9 3.4 %all-to-all-start.1 = ((bf16[8,8,3072]{2,1,0:T(8,128)(2,1)}), bf16[8,8,3072]{2,1,0:T(8,128)(2,1)S(1)}, u32[]{:S(2)}, u32[]{:S(2)}) async-start(bf16[8,8,3072]{2,1,0:T(8,128)(2,1)} %broadcast_in_dim.5), calls=%async_computation.1 | async-start | bytes 786432 | tf_op jit(solution)/shard_map/all_to_all | solution.py:119
  32.2 2.3 %collective-permute-done = bf16[8,8,3072]{2,1,0:T(8,128)(2,1)S(1)} collective-permute-done((bf16[8,8,3072]{2,1,0:T(8,128)(2,1)S(1)}, bf16[8,8,3072]{2,1,0:T(8,128)(2,1)S(1)}, u32[]{:S(2)}, u32[]{:S(2)}) %collective-permute-start) | collective-permute-done | bytes 393248 | tf_op jit(solution)/shard_map/ppermute | solution.py:29
  34.6 1.0 collective-permute-start.2
  35.5 0.8 constant_dynamic-update-slice_fusion.6
  37.1 6.8 %all-to-all-done.1 = bf16[8,8,3072]{2,1,0:T(8,128)(2,1)S(1)} async-done(((bf16[8,8,3072]{2,1,0:T(8,128)(2,1)}), bf16[8,8,3072]{2,1,0:T(8,128)(2,1)S(1)}, u32[]{:S(2)}, u32[]{:S(2)}) %all-to-all-start.1) | async-done | bytes 393248 | tf_op jit(solution)/shard_map/all_to_all | solution.py:119
  43.9 1.2 collective-permute-start.10
  47.0 1.8 %constant_dynamic-update-slice_fusion.2 = bf16[64,8,3072]{2,1,0:T(8,128)(2,1)} fusion(bf16[64,8,3072]{2,1,0:T(8,128)(2,1)} %constant_dynamic-update-slice_fusion.3, bf16[8,8,3072]{2,1,0:T(8,128)(2,1)} %collective-permute-done.4), kind=kLoop, calls=%fused_computation.56 | loop fusion | bytes 786432
  50.3 4.5 %fusion = f32[8,4,16,768]{3,2,1,0:T(8,128)S(1)} fusion(bf16[8,4,16,3072]{3,2,1,0:T(8,128)(2,1)} %bitcast.2, bf16[3072,768]{1,0:T(8,128)(2,1)S(1)} %copy-done), kind=kOutput, calls=%fused_computation.1 | convolution fusion | flops 2415919104 | bytes 9437184 | tf_op jit(solution)/shard_map/dot_general | solution.py:133
  54.9 0.8 collective-permute-start.7
  55.7 1.3 collective-permute-start.14
  57.0 1.2 collective-permute-start.11
  58.3 4.5 %collective-permute-done.7 = bf16[2,8,16,768]{3,2,1,0:T(8,128)(2,1)S(1)} collective-permute-done((bf16[2,8,16,768]{3,2,1,0:T(8,128)(2,1)S(1)}, bf16[2,8,16,768]{3,2,1,0:T(8,128)(2,1)S(1)}, u32[]{:S(2)}, u32[]{:S(2)}) %collective-permute-start.7) | collective-permute-done | bytes 393248 | tf_op jit(solution)/shard_map/ppermute | solution.py:29
  63.3 2.8 %collective-permute-done.11 = bf16[8,8,3072]{2,1,0:T(8,128)(2,1)S(1)} collective-permute-done((bf16[8,8,3072]{2,1,0:T(8,128)(2,1)S(1)}, bf16[8,8,3072]{2,1,0:T(8,128)(2,1)S(1)}, u32[]{:S(2)}, u32[]{:S(2)}) %collective-permute-start.11) | collective-permute-done | bytes 393248 | tf_op jit(solution)/shard_map/ppermute | solution.py:29
  66.2 3.7 %collective-permute-done.8.other_ref = bf16[8,16,768]{2,1,0:T(8,128)(2,1)S(1)} collective-permute-done((bf16[8,16,768]{2,1,0:T(8,128)(2,1)S(1)}, bf16[8,16,768]{2,1,0:T(8,128)(2,1)S(1)}, u32[]{:S(2)}, u32[]{:S(2)}) %collective-permute-start.8) | collective-permute-done | bytes 196640 | tf_op jit(solution)/shard_map/ppermute | solution.py:29
  69.9 0.9 gelu.2
  71.1 2.6 %fusion.35 = f32[512,768]{1,0:T(8,128)S(1)} fusion(bf16[512,3072]{1,0:T(8,128)(2,1)S(1)} %bitcast.160, bf16[3072,768]{1,0:T(8,128)(2,1)S(1)} %copy-done), kind=kOutput, calls=%fused_computation.83 | convolution fusion | flops 2415919104 | bytes 9437184 | tf_op jit(solution)/shard_map/dot_general | solution.py:133
  74.0 5.5 %collective-permute-done.18.b_ref = bf16[8,16,768]{2,1,0:T(8,128)(2,1)S(1)} collective-permute-done((bf16[8,16,768]{2,1,0:T(8,128)(2,1)S(1)}, bf16[8,16,768]{2,1,0:T(8,128)(2,1)S(1)}, u32[]{:S(2)}, u32[]{:S(2)}) %collective-permute-start.18) | collective-permute-done | bytes 196640 | tf_op jit(solution)/shard_map/ppermute | solution.py:29
  79.7 2.0 %collective-permute-done.16 = bf16[2,8,16,768]{3,2,1,0:T(8,128)(2,1)S(1)} collective-permute-done((bf16[2,8,16,768]{3,2,1,0:T(8,128)(2,1)S(1)}, bf16[2,8,16,768]{3,2,1,0:T(8,128)(2,1)S(1)}, u32[]{:S(2)}, u32[]{:S(2)}) %collective-permute-start.16) | collective-permute-done | bytes 393248 | tf_op jit(solution)/shard_map/ppermute | solution.py:29
  81.8 5.6 %collective-permute-done.20.c_ref = bf16[2,8,16,768]{3,2,1,0:T(8,128)(2,1)S(1)} collective-permute-done((bf16[2,8,16,768]{3,2,1,0:T(8,128)(2,1)S(1)}, bf16[2,8,16,768]{3,2,1,0:T(8,128)(2,1)S(1)}, u32[]{:S(2)}, u32[]{:S(2)}) %collective-permute-start.20) | collective-permute-done | bytes 393248 | tf_op jit(solution)/shard_map/ppermute | solution.py:29
  88.1 1.4 convolution_convert_fusion.1
  89.7 1.6 collective-permute-start.17
  91.3 1.4 fusion.36
  92.7 3.9 %collective-permute-done.17.other_ref = bf16[8,16,768]{2,1,0:T(8,128)(2,1)S(1)} collective-permute-done((bf16[8,16,768]{2,1,0:T(8,128)(2,1)S(1)}, bf16[8,16,768]{2,1,0:T(8,128)(2,1)S(1)}, u32[]{:S(2)}, u32[]{:S(2)}) %collective-permute-start.17) | collective-permute-done | bytes 196640 | tf_op jit(solution)/shard_map/ppermute | solution.py:29
  96.6 0.9 gelu.3
  97.5 1.6 collective-permute-start.19
  99.4 5.1 %collective-permute-done.19.b_ref = bf16[8,16,768]{2,1,0:T(8,128)(2,1)S(1)} collective-permute-done((bf16[8,16,768]{2,1,0:T(8,128)(2,1)S(1)}, bf16[8,16,768]{2,1,0:T(8,128)(2,1)S(1)}, u32[]{:S(2)}, u32[]{:S(2)}) %collective-permute-start.19) | collective-permute-done | bytes 196640 | tf_op jit(solution)/shard_map/ppermute | solution.py:29
  105.0 2.4 %collective-permute-start.24 = (bf16[2,64,3072]{2,1,0:T(8,128)(2,1)S(1)}, bf16[2,64,3072]{2,1,0:T(8,128)(2,1)S(1)}, u32[]{:S(2)}, u32[]{:S(2)}) collective-permute-start(bf16[2,64,3072]{2,1,0:T(8,128)(2,1)S(1)} %add_convert_fusion.2), channel_id=1, source_target_pairs={{0,6},{1,3},{2,4},{3,1},{4,2},{5,7},{6,0},{7,5},{8,14},{9,11},{10,... | collective-permute-start | bytes 2359304 | tf_op jit(solution)/shard_map/ppermute | solution.py:29
  107.6 4.6 %fusion.2 = f32[3072,768]{1,0:T(8,128)S(1)} fusion(bf16[512,768]{1,0:T(8,128)(2,1)S(1)} %bitcast.139, bf16[64,8,3072]{2,1,0:T(8,128)(2,1)} %constant_dynamic-update-slice_fusion), kind=kOutput, calls=%fused_computation.5 | convolution fusion | flops 2415919104 | bytes 13369344 | tf_op jit(solution)/shard_map/dot_general | solution.py:179
  113.4 1.4 convolution_convert_fusion
  115.0 1.4 fusion.37
  116.4 2.1 %collective-permute-done.24 = bf16[2,64,3072]{2,1,0:T(8,128)(2,1)S(1)} collective-permute-done((bf16[2,64,3072]{2,1,0:T(8,128)(2,1)S(1)}, bf16[2,64,3072]{2,1,0:T(8,128)(2,1)S(1)}, u32[]{:S(2)}, u32[]{:S(2)}) %collective-permute-start.24) | collective-permute-done | bytes 786464 | tf_op jit(solution)/shard_map/ppermute | solution.py:29
  119.7 6.9 %collective-permute-done.26 = bf16[64,3072]{1,0:T(8,128)(2,1)S(1)} collective-permute-done((bf16[64,3072]{1,0:T(8,128)(2,1)S(1)}, bf16[64,3072]{1,0:T(8,128)(2,1)S(1)}, u32[]{:S(2)}, u32[]{:S(2)}) %collective-permute-start.26) | collective-permute-done | bytes 393248 | tf_op jit(solution)/shard_map/ppermute | solution.py:29
  126.6 0.9 fusion.13
  127.8 2.2 %collective-permute-start.25 = (bf16[2,64,3072]{2,1,0:T(8,128)(2,1)S(1)}, bf16[2,64,3072]{2,1,0:T(8,128)(2,1)S(1)}, u32[]{:S(2)}, u32[]{:S(2)}) collective-permute-start(bf16[2,64,3072]{2,1,0:T(8,128)(2,1)S(1)} %add_convert_fusion.1), channel_id=1, source_target_pairs={{0,6},{1,3},{2,4},{3,1},{4,2},{5,7},{6,0},{7,5},{8,14},{9,11},{10,... | collective-permute-start | bytes 2359304 | tf_op jit(solution)/shard_map/ppermute | solution.py:29
  130.0 4.5 %add_convert_fusion = bf16[3072,768]{1,0:T(8,128)(2,1)} fusion(f32[3072,768]{1,0:T(8,128)S(1)} %fusion.2, bf16[512,768]{1,0:T(8,128)(2,1)S(1)} %bitcast.140, bf16[64,8,3072]{2,1,0:T(8,128)(2,1)S(1)} %constant_dynamic-update-slice_fusion.8), kind=kOutput, calls=%fused_computation | convolution fusion | flops 2420637696 | bytes 18087936 | tf_op jit(solution)/shard_map/dot_general | solution.py:179
  134.7 6.4 %collective-permute-done.25 = bf16[2,64,3072]{2,1,0:T(8,128)(2,1)S(1)} collective-permute-done((bf16[2,64,3072]{2,1,0:T(8,128)(2,1)S(1)}, bf16[2,64,3072]{2,1,0:T(8,128)(2,1)S(1)}, u32[]{:S(2)}, u32[]{:S(2)}) %collective-permute-start.25) | collective-permute-done | bytes 786464 | tf_op jit(solution)/shard_map/ppermute | solution.py:29
  141.5 4.3 %all-to-all-start.2 = ((bf16[8,8,3072]{2,1,0:T(8,128)(2,1)}), bf16[8,8,3072]{2,1,0:T(8,128)(2,1)S(1)}, u32[]{:S(2)}, u32[]{:S(2)}) async-start(bf16[8,8,3072]{2,1,0:T(8,128)(2,1)} %fusion.13), calls=%async_computation.2 | async-start | bytes 786432 | tf_op jit(solution)/shard_map/all_to_all | solution.py:174
  145.7 3.5 %collective-permute-done.27 = bf16[64,3072]{1,0:T(8,128)(2,1)S(1)} collective-permute-done((bf16[64,3072]{1,0:T(8,128)(2,1)S(1)}, bf16[64,3072]{1,0:T(8,128)(2,1)S(1)}, u32[]{:S(2)}, u32[]{:S(2)}) %collective-permute-start.27) | collective-permute-done | bytes 393248 | tf_op jit(solution)/shard_map/ppermute | solution.py:29
  149.2 2.0 %fusion.14 = bf16[8,8,3072]{2,1,0:T(8,128)(2,1)} fusion(bf16[64,3072]{1,0:T(8,128)(2,1)S(1)} %collective-permute-done.27, f32[2,64,3072]{2,1,0:T(8,128)S(1)} %convert_element_type.93, f32[2,64,3072]{2,1,0:T(8,128)} %copy-done.1), kind=kLoop, calls=%fused_computation.25 | loop fusion | flops 786432 | bytes 2359296 | tf_op jit(solution)/shard_map/reshape | solution.py:170
  151.2 5.4 %all-to-all-done.2 = bf16[8,8,3072]{2,1,0:T(8,128)(2,1)S(1)} async-done(((bf16[8,8,3072]{2,1,0:T(8,128)(2,1)}), bf16[8,8,3072]{2,1,0:T(8,128)(2,1)S(1)}, u32[]{:S(2)}, u32[]{:S(2)}) %all-to-all-start.2) | async-done | bytes 393248 | tf_op jit(solution)/shard_map/all_to_all | solution.py:174
  156.6 3.9 %all-to-all-start.3 = ((bf16[8,8,3072]{2,1,0:T(8,128)(2,1)}), bf16[8,8,3072]{2,1,0:T(8,128)(2,1)S(1)}, u32[]{:S(2)}, u32[]{:S(2)}) async-start(bf16[8,8,3072]{2,1,0:T(8,128)(2,1)} %fusion.14), calls=%async_computation.3 | async-start | bytes 786432 | tf_op jit(solution)/shard_map/all_to_all | solution.py:174
  160.6 0.8 copy.15
  161.4 11.3 %all-to-all-done.3 = bf16[8,8,3072]{2,1,0:T(8,128)(2,1)S(1)} async-done(((bf16[8,8,3072]{2,1,0:T(8,128)(2,1)}), bf16[8,8,3072]{2,1,0:T(8,128)(2,1)S(1)}, u32[]{:S(2)}, u32[]{:S(2)}) %all-to-all-start.3) | async-done | bytes 393248 | tf_op jit(solution)/shard_map/all_to_all | solution.py:174
  (89 shorter events, 14.5 us)
Async XLA Ops:
  2.2 21.8 %all-to-all-start = ((bf16[8,8,3072]{2,1,0:T(8,128)(2,1)}), bf16[8,8,3072]{2,1,0:T(8,128)(2,1)S(1)}, u32[]{:S(2)}, u32[]{:S(2)}) async-start(bf16[8,8,3072]{2,1,0:T(8,128)(2,1)} %broadcast_in_dim.4), calls=%async_computation | async-start | bytes 786432 | tf_op jit(solution)/shard_map/all_to_all | solution.py:119
  24.0 11.5 %collective-permute-start.1 = (bf16[8,8,3072]{2,1,0:T(8,128)(2,1)S(1)}, bf16[8,8,3072]{2,1,0:T(8,128)(2,1)S(1)}, u32[]{:S(2)}, u32[]{:S(2)}) collective-permute-start(bf16[8,8,3072]{2,1,0:T(8,128)(2,1)S(1)} %all-to-all-done), channel_id=1, source_target_pairs={{0,6},{1,3},{2,4},{3,1},{4,2},{5,7},{6,0},{7,5},{8,14},{9,11},{10,... | collective-permute-start | bytes 1179656 | tf_op jit(solution)/shard_map/ppermute | solution.py:29
  26.8 7.8 %collective-permute-start = (bf16[8,8,3072]{2,1,0:T(8,128)(2,1)S(1)}, bf16[8,8,3072]{2,1,0:T(8,128)(2,1)S(1)}, u32[]{:S(2)}, u32[]{:S(2)}) collective-permute-start(bf16[8,8,3072]{2,1,0:T(8,128)(2,1)S(1)} %all-to-all-done), channel_id=1, source_target_pairs={{0,2},{1,7},{2,0},{3,5},{4,6},{5,3},{6,4},{7,1},{8,10},{9,15},{10,... | collective-permute-start | bytes 1179656 | tf_op jit(solution)/shard_map/ppermute | solution.py:29
  27.9 15.9 %all-to-all-start.1 = ((bf16[8,8,3072]{2,1,0:T(8,128)(2,1)}), bf16[8,8,3072]{2,1,0:T(8,128)(2,1)S(1)}, u32[]{:S(2)}, u32[]{:S(2)}) async-start(bf16[8,8,3072]{2,1,0:T(8,128)(2,1)} %broadcast_in_dim.5), calls=%async_computation.1 | async-start | bytes 786432 | tf_op jit(solution)/shard_map/all_to_all | solution.py:119
  31.4 14.6 %collective-permute-start.3 = (bf16[8,8,3072]{2,1,0:T(8,128)(2,1)S(1)}, bf16[8,8,3072]{2,1,0:T(8,128)(2,1)S(1)}, u32[]{:S(2)}, u32[]{:S(2)}) collective-permute-start(bf16[8,8,3072]{2,1,0:T(8,128)(2,1)S(1)} %all-to-all-done), channel_id=1, source_target_pairs={{0,1},{1,0},{2,3},{3,2},{4,5},{5,4},{6,7},{7,6},{8,9},{9,8},{10,11... | collective-permute-start | bytes 1179656 | tf_op jit(solution)/shard_map/ppermute | solution.py:29
  34.6 14.2 %collective-permute-start.5 = (bf16[8,8,3072]{2,1,0:T(8,128)(2,1)S(1)}, bf16[8,8,3072]{2,1,0:T(8,128)(2,1)S(1)}, u32[]{:S(2)}, u32[]{:S(2)}) collective-permute-start(bf16[8,8,3072]{2,1,0:T(8,128)(2,1)S(1)} %collective-permute-done), channel_id=1, source_target_pairs={{0,1},{1,0},{2,3},{3,2},{4,5},{5,4},{6,7},{7,6},{8,9},{9,8},{10,11... | collective-permute-start | bytes 1179656 | tf_op jit(solution)/shard_map/ppermute | solution.py:29
  34.6 9.4 %collective-permute-start.2 = (bf16[8,8,3072]{2,1,0:T(8,128)(2,1)S(1)}, bf16[8,8,3072]{2,1,0:T(8,128)(2,1)S(1)}, u32[]{:S(2)}, u32[]{:S(2)}) collective-permute-start(bf16[8,8,3072]{2,1,0:T(8,128)(2,1)S(1)} %collective-permute-done), channel_id=1, source_target_pairs={{0,6},{1,3},{2,4},{3,1},{4,2},{5,7},{6,0},{7,5},{8,14},{9,11},{10,... | collective-permute-start | bytes 1179656 | tf_op jit(solution)/shard_map/ppermute | solution.py:29
  35.5 11.2 %collective-permute-start.4 = (bf16[8,8,3072]{2,1,0:T(8,128)(2,1)S(1)}, bf16[8,8,3072]{2,1,0:T(8,128)(2,1)}, u32[]{:S(2)}, u32[]{:S(2)}) collective-permute-start(bf16[8,8,3072]{2,1,0:T(8,128)(2,1)S(1)} %collective-permute-done.1), channel_id=1, source_target_pairs={{0,1},{1,0},{2,3},{3,2},{4,5},{5,4},{6,7},{7,6},{8,9},{9,8},{10,11... | collective-permute-start | bytes 1179656 | tf_op jit(solution)/shard_map/ppermute | solution.py:29
  43.9 6.4 %copy-start = (bf16[3072,768]{1,0:T(8,128)(2,1)S(1)}, bf16[3072,768]{1,0:T(8,128)(2,1)}, u32[]{:S(2)}) copy-start(bf16[3072,768]{1,0:T(8,128)(2,1)} %param.4) | copy-start | bytes 14155780
  43.9 22.2 %collective-permute-start.12 = (bf16[8,8,3072]{2,1,0:T(8,128)(2,1)S(1)}, bf16[8,8,3072]{2,1,0:T(8,128)(2,1)S(1)}, u32[]{:S(2)}, u32[]{:S(2)}) collective-permute-start(bf16[8,8,3072]{2,1,0:T(8,128)(2,1)S(1)} %all-to-all-done.1), channel_id=1, source_target_pairs={{0,1},{1,0},{2,3},{3,2},{4,5},{5,4},{6,7},{7,6},{8,9},{9,8},{10,11... | collective-permute-start | bytes 1179656 | tf_op jit(solution)/shard_map/ppermute | solution.py:29
  43.9 14.3 %collective-permute-start.10 = (bf16[8,8,3072]{2,1,0:T(8,128)(2,1)S(1)}, bf16[8,8,3072]{2,1,0:T(8,128)(2,1)S(1)}, u32[]{:S(2)}, u32[]{:S(2)}) collective-permute-start(bf16[8,8,3072]{2,1,0:T(8,128)(2,1)S(1)} %all-to-all-done.1), channel_id=1, source_target_pairs={{0,6},{1,3},{2,4},{3,1},{4,2},{5,7},{6,0},{7,5},{8,14},{9,11},{10,... | collective-permute-start | bytes 1179656 | tf_op jit(solution)/shard_map/ppermute | solution.py:29
  46.0 9.8 %collective-permute-start.9 = (bf16[8,8,3072]{2,1,0:T(8,128)(2,1)S(1)}, bf16[8,8,3072]{2,1,0:T(8,128)(2,1)S(1)}, u32[]{:S(2)}, u32[]{:S(2)}) collective-permute-start(bf16[8,8,3072]{2,1,0:T(8,128)(2,1)S(1)} %all-to-all-done.1), channel_id=1, source_target_pairs={{0,2},{1,7},{2,0},{3,5},{4,6},{5,3},{6,4},{7,1},{8,10},{9,15},{10,... | collective-permute-start | bytes 1179656 | tf_op jit(solution)/shard_map/ppermute | solution.py:29
  46.7 2.8 %collective-permute-start.6 = (bf16[8,8,3072]{2,1,0:T(8,128)(2,1)S(1)}, bf16[8,8,3072]{2,1,0:T(8,128)(2,1)S(1)}, u32[]{:S(2)}, u32[]{:S(2)}) collective-permute-start(bf16[8,8,3072]{2,1,0:T(8,128)(2,1)S(1)} %collective-permute-done.2), channel_id=1, source_target_pairs={{0,1},{1,0},{2,3},{3,2},{4,5},{5,4},{6,7},{7,6},{8,9},{9,8},{10,11... | collective-permute-start | bytes 1179656 | tf_op jit(solution)/shard_map/ppermute | solution.py:29
  54.9 7.9 %collective-permute-start.7 = (bf16[2,8,16,768]{3,2,1,0:T(8,128)(2,1)S(1)}, bf16[2,8,16,768]{3,2,1,0:T(8,128)(2,1)S(1)}, u32[]{:S(2)}, u32[]{:S(2)}) collective-permute-start(bf16[2,8,16,768]{3,2,1,0:T(8,128)(2,1)S(1)} %pad_maximum_fusion), channel_id=1, source_target_pairs={{0,64},{1,193},{2,66},{3,195},{4,68},{5,197},{6,70},{7,199},{8,72}... | collective-permute-start | bytes 1179656 | tf_op jit(solution)/shard_map/ppermute | solution.py:29
  55.7 10.4 %collective-permute-start.14 = (bf16[8,8,3072]{2,1,0:T(8,128)(2,1)S(1)}, bf16[8,8,3072]{2,1,0:T(8,128)(2,1)S(1)}, u32[]{:S(2)}, u32[]{:S(2)}) collective-permute-start(bf16[8,8,3072]{2,1,0:T(8,128)(2,1)S(1)} %collective-permute-done.9), channel_id=1, source_target_pairs={{0,1},{1,0},{2,3},{3,2},{4,5},{5,4},{6,7},{7,6},{8,9},{9,8},{10,11... | collective-permute-start | bytes 1179656 | tf_op jit(solution)/shard_map/ppermute | solution.py:29
  57.0 9.0 %collective-permute-start.11 = (bf16[8,8,3072]{2,1,0:T(8,128)(2,1)S(1)}, bf16[8,8,3072]{2,1,0:T(8,128)(2,1)S(1)}, u32[]{:S(2)}, u32[]{:S(2)}) collective-permute-start(bf16[8,8,3072]{2,1,0:T(8,128)(2,1)S(1)} %collective-permute-done.9), channel_id=1, source_target_pairs={{0,6},{1,3},{2,4},{3,1},{4,2},{5,7},{6,0},{7,5},{8,14},{9,11},{10,... | collective-permute-start | bytes 1179656 | tf_op jit(solution)/shard_map/ppermute | solution.py:29
  58.2 7.9 %collective-permute-start.13 = (bf16[8,8,3072]{2,1,0:T(8,128)(2,1)S(1)}, bf16[8,8,3072]{2,1,0:T(8,128)(2,1)S(1)}, u32[]{:S(2)}, u32[]{:S(2)}) collective-permute-start(bf16[8,8,3072]{2,1,0:T(8,128)(2,1)S(1)} %collective-permute-done.10), channel_id=1, source_target_pairs={{0,1},{1,0},{2,3},{3,2},{4,5},{5,4},{6,7},{7,6},{8,9},{9,8},{10,11... | collective-permute-start | bytes 1179656 | tf_op jit(solution)/shard_map/ppermute | solution.py:29
  62.9 7.0 %collective-permute-start.8 = (bf16[8,16,768]{2,1,0:T(8,128)(2,1)S(1)}, bf16[8,16,768]{2,1,0:T(8,128)(2,1)S(1)}, u32[]{:S(2)}, u32[]{:S(2)}) collective-permute-start(bf16[8,16,768]{2,1,0:T(8,128)(2,1)S(1)} %get-tuple-element.38), channel_id=1, source_target_pairs={{0,192},{1,65},{2,194},{3,67},{4,196},{5,69},{6,198},{7,71},{8,200... | collective-permute-start | bytes 589832 | tf_op jit(solution)/shard_map/ppermute | solution.py:29
  66.0 5.1 %collective-permute-start.15 = (bf16[8,8,3072]{2,1,0:T(8,128)(2,1)S(1)}, bf16[8,8,3072]{2,1,0:T(8,128)(2,1)S(1)}, u32[]{:S(2)}, u32[]{:S(2)}) collective-permute-start(bf16[8,8,3072]{2,1,0:T(8,128)(2,1)S(1)} %collective-permute-done.11), channel_id=1, source_target_pairs={{0,1},{1,0},{2,3},{3,2},{4,5},{5,4},{6,7},{7,6},{8,9},{9,8},{10,11... | collective-permute-start | bytes 1179656 | tf_op jit(solution)/shard_map/ppermute | solution.py:29
  70.8 8.7 %collective-permute-start.18 = (bf16[8,16,768]{2,1,0:T(8,128)(2,1)S(1)}, bf16[8,16,768]{2,1,0:T(8,128)(2,1)S(1)}, u32[]{:S(2)}, u32[]{:S(2)}) collective-permute-start(bf16[8,16,768]{2,1,0:T(8,128)(2,1)S(1)} %get-tuple-element.22.a_ref), channel_id=1, source_target_pairs={{0,192},{1,65},{2,194},{3,67},{4,196},{5,69},{6,198},{7,71},{8,200... | collective-permute-start | bytes 589832 | tf_op jit(solution)/shard_map/ppermute | solution.py:29
  73.9 7.9 %collective-permute-start.16 = (bf16[2,8,16,768]{3,2,1,0:T(8,128)(2,1)S(1)}, bf16[2,8,16,768]{3,2,1,0:T(8,128)(2,1)S(1)}, u32[]{:S(2)}, u32[]{:S(2)}) collective-permute-start(bf16[2,8,16,768]{3,2,1,0:T(8,128)(2,1)S(1)} %pad_maximum_fusion.1), channel_id=1, source_target_pairs={{0,64},{1,193},{2,66},{3,195},{4,68},{5,197},{6,70},{7,199},{8,72}... | collective-permute-start | bytes 1179656 | tf_op jit(solution)/shard_map/ppermute | solution.py:29
  79.5 7.9 %collective-permute-start.20 = (bf16[2,8,16,768]{3,2,1,0:T(8,128)(2,1)S(1)}, bf16[2,8,16,768]{3,2,1,0:T(8,128)(2,1)S(1)}, u32[]{:S(2)}, u32[]{:S(2)}) collective-permute-start(bf16[2,8,16,768]{3,2,1,0:T(8,128)(2,1)S(1)} %pad_maximum_fusion.3), channel_id=1, source_target_pairs={{0,64},{1,193},{2,66},{3,195},{4,68},{5,197},{6,70},{7,199},{8,72}... | collective-permute-start | bytes 1179656 | tf_op jit(solution)/shard_map/ppermute | solution.py:29
  89.5 15.1 %collective-permute-start.21 = (bf16[4,64,3072]{2,1,0:T(8,128)(2,1)S(1)}, bf16[4,64,3072]{2,1,0:T(8,128)(2,1)S(1)}, u32[]{:S(2)}, u32[]{:S(2)}) collective-permute-start(bf16[4,64,3072]{2,1,0:T(8,128)(2,1)S(1)} %bitcast.161), channel_id=1, source_target_pairs={{0,1},{1,0},{2,3},{3,2},{4,5},{5,4},{6,7},{7,6},{8,9},{9,8},{10,11... | collective-permute-start | bytes 4718600 | tf_op jit(solution)/shard_map/ppermute | solution.py:29
  89.7 7.0 %collective-permute-start.17 = (bf16[8,16,768]{2,1,0:T(8,128)(2,1)S(1)}, bf16[8,16,768]{2,1,0:T(8,128)(2,1)S(1)}, u32[]{:S(2)}, u32[]{:S(2)}) collective-permute-start(bf16[8,16,768]{2,1,0:T(8,128)(2,1)S(1)} %get-tuple-element.39), channel_id=1, source_target_pairs={{0,192},{1,65},{2,194},{3,67},{4,196},{5,69},{6,198},{7,71},{8,200... | collective-permute-start | bytes 589832 | tf_op jit(solution)/shard_map/ppermute | solution.py:29
  97.5 7.0 %collective-permute-start.19 = (bf16[8,16,768]{2,1,0:T(8,128)(2,1)S(1)}, bf16[8,16,768]{2,1,0:T(8,128)(2,1)S(1)}, u32[]{:S(2)}, u32[]{:S(2)}) collective-permute-start(bf16[8,16,768]{2,1,0:T(8,128)(2,1)S(1)} %get-tuple-element.24.a_ref), channel_id=1, source_target_pairs={{0,192},{1,65},{2,194},{3,67},{4,196},{5,69},{6,198},{7,71},{8,200... | collective-permute-start | bytes 589832 | tf_op jit(solution)/shard_map/ppermute | solution.py:29
  104.9 7.9 %collective-permute-start.22 = (bf16[2,8,16,768]{3,2,1,0:T(8,128)(2,1)S(1)}, bf16[2,8,16,768]{3,2,1,0:T(8,128)(2,1)S(1)}, u32[]{:S(2)}, u32[]{:S(2)}) collective-permute-start(bf16[2,8,16,768]{3,2,1,0:T(8,128)(2,1)S(1)} %pad_maximum_fusion.2), channel_id=1, source_target_pairs={{0,64},{1,193},{2,66},{3,195},{4,68},{5,197},{6,70},{7,199},{8,72}... | collective-permute-start | bytes 1179656 | tf_op jit(solution)/shard_map/ppermute | solution.py:29
  105.0 13.5 %collective-permute-start.24 = (bf16[2,64,3072]{2,1,0:T(8,128)(2,1)S(1)}, bf16[2,64,3072]{2,1,0:T(8,128)(2,1)S(1)}, u32[]{:S(2)}, u32[]{:S(2)}) collective-permute-start(bf16[2,64,3072]{2,1,0:T(8,128)(2,1)S(1)} %add_convert_fusion.2), channel_id=1, source_target_pairs={{0,6},{1,3},{2,4},{3,1},{4,2},{5,7},{6,0},{7,5},{8,14},{9,11},{10,... | collective-permute-start | bytes 2359304 | tf_op jit(solution)/shard_map/ppermute | solution.py:29
  114.9 12.6 %collective-permute-start.23 = (bf16[4,64,3072]{2,1,0:T(8,128)(2,1)S(1)}, bf16[4,64,3072]{2,1,0:T(8,128)(2,1)S(1)}, u32[]{:S(2)}, u32[]{:S(2)}) collective-permute-start(bf16[4,64,3072]{2,1,0:T(8,128)(2,1)S(1)} %bitcast.162), channel_id=1, source_target_pairs={{0,1},{1,0},{2,3},{3,2},{4,5},{5,4},{6,7},{7,6},{8,9},{9,8},{10,11... | collective-permute-start | bytes 4718600 | tf_op jit(solution)/shard_map/ppermute | solution.py:29
  118.8 7.9 %collective-permute-start.26 = (bf16[64,3072]{1,0:T(8,128)(2,1)S(1)}, bf16[64,3072]{1,0:T(8,128)(2,1)S(1)}, u32[]{:S(2)}, u32[]{:S(2)}) collective-permute-start(bf16[64,3072]{1,0:T(8,128)(2,1)S(1)} %fusion.12), channel_id=1, source_target_pairs={{0,2},{1,7},{2,0},{3,5},{4,6},{5,3},{6,4},{7,1},{8,10},{9,15},{10,... | collective-permute-start | bytes 1179656 | tf_op jit(solution)/shard_map/ppermute | solution.py:29
  127.8 13.3 %collective-permute-start.25 = (bf16[2,64,3072]{2,1,0:T(8,128)(2,1)S(1)}, bf16[2,64,3072]{2,1,0:T(8,128)(2,1)S(1)}, u32[]{:S(2)}, u32[]{:S(2)}) collective-permute-start(bf16[2,64,3072]{2,1,0:T(8,128)(2,1)S(1)} %add_convert_fusion.1), channel_id=1, source_target_pairs={{0,6},{1,3},{2,4},{3,1},{4,2},{5,7},{6,0},{7,5},{8,14},{9,11},{10,... | collective-permute-start | bytes 2359304 | tf_op jit(solution)/shard_map/ppermute | solution.py:29
  134.6 6.6 %copy-start.1 = (f32[2,64,3072]{2,1,0:T(8,128)}, f32[2,64,3072]{2,1,0:T(8,128)S(1)}, u32[]{:S(2)}) copy-start(f32[2,64,3072]{2,1,0:T(8,128)S(1)} %convert_add_fusion.1) | copy-start | bytes 4718596
  141.4 7.9 %collective-permute-start.27 = (bf16[64,3072]{1,0:T(8,128)(2,1)S(1)}, bf16[64,3072]{1,0:T(8,128)(2,1)S(1)}, u32[]{:S(2)}, u32[]{:S(2)}) collective-permute-start(bf16[64,3072]{1,0:T(8,128)(2,1)S(1)} %fusion.15), channel_id=1, source_target_pairs={{0,2},{1,7},{2,0},{3,5},{4,6},{5,3},{6,4},{7,1},{8,10},{9,15},{10,... | collective-permute-start | bytes 1179656 | tf_op jit(solution)/shard_map/ppermute | solution.py:29
  141.5 15.2 %all-to-all-start.2 = ((bf16[8,8,3072]{2,1,0:T(8,128)(2,1)}), bf16[8,8,3072]{2,1,0:T(8,128)(2,1)S(1)}, u32[]{:S(2)}, u32[]{:S(2)}) async-start(bf16[8,8,3072]{2,1,0:T(8,128)(2,1)} %fusion.13), calls=%async_computation.2 | async-start | bytes 786432 | tf_op jit(solution)/shard_map/all_to_all | solution.py:174
  156.6 16.1 %all-to-all-start.3 = ((bf16[8,8,3072]{2,1,0:T(8,128)(2,1)}), bf16[8,8,3072]{2,1,0:T(8,128)(2,1)S(1)}, u32[]{:S(2)}, u32[]{:S(2)}) async-start(bf16[8,8,3072]{2,1,0:T(8,128)(2,1)} %fusion.14), calls=%async_computation.3 | async-start | bytes 786432 | tf_op jit(solution)/shard_map/all_to_all | solution.py:174

commit v3 on v2

--- a/solution.py
+++ b/solution.py
@@ -95,7 +95,7 @@
 
 
 def after(value, *others):
-    return lax.optimization_barrier((value, *others))[0]
+    return lax.optimization_barrier((value, *others))[0] if others else value
 
 
 class Chunk:
@@ -115,8 +115,9 @@
     order = jnp.stack([y, y ^ far, y ^ near, y ^ 2]).astype(jnp.int32)
     cotangents = jnp.transpose(out_grad.reshape(2, 8, CHUNKS, t, f), (2, 1, 0, 3, 4)).reshape(CHUNKS, 8, 2 * t, f)
 
-    def spread(c, block):
-        c.own = lax.all_to_all(jnp.broadcast_to(block[None], (8, t, d)), Z, 0, 0, tiled=True)
+    def spread(c, block, *wait):
+        copies = after(jnp.broadcast_to(block[None], (8, t, d)), *wait)
+        c.own = lax.all_to_all(copies, Z, 0, 0, tiled=True)
 
     def along_x(c, *wait):
         source = after(c.own, *wait) if wait else c.own
@@ -161,18 +162,19 @@
         c.here = keep[:2] + jnp.stack([got[0], got[2]]).astype(F32)
 
     def reduce_first(c, wait=(), behind=()):
-        got = after(permute(after(c.away, *wait), x_second), *behind).astype(F32)
-        c.away = (c.here[1] + got[1]).astype(BF)
-        c.here = c.here[0] + got[0]
-
-    def reduce_second(c, *wait):
-        got = permute(after(c.away, *wait) if wait else c.away, x_first).astype(F32)
-        c.total = (c.here + got).astype(BF).reshape(8, t, d)
+        got = after(permute(after(c.away, *wait), x_second), *behind)
+        c.away = (c.here[1] + got[1].astype(F32)).astype(BF)
+        c.here = (c.here[0], got[0])
+
+    def reduce_second(c, wait=(), behind=()):
+        got = after(permute(after(c.away, *wait), x_first), *behind)
+        here, first_got = c.here
+        c.total = (here + first_got.astype(F32) + got.astype(F32)).astype(BF).reshape(8, t, d)
 
     def reduce_last(c, *wait):
         total = after(c.total, *wait) if wait else c.total
-        blocks = lax.all_to_all(total, Z, 0, 0, tiled=True)
-        c.input_grad = jnp.sum(blocks.astype(F32), 0).astype(BF)
+        c.blocks = lax.all_to_all(total, Z, 0, 0, tiled=True)
+        c.input_grad = jnp.sum(c.blocks.astype(F32), 0).astype(BF)
 
     def weights(c, *wait):
         grads = after(c.grad_all, *wait).reshape(64 * t, f)
@@ -181,7 +183,7 @@
     a, b = Chunk(), Chunk()
     spread(a, inputs[:t])
     along_x(a)
-    spread(b, after(inputs[t:], a.own))
+    spread(b, inputs[t:], a.own)
     assemble(a)
     along_x(b, a.three)
     project(a)
@@ -192,24 +194,21 @@
     gelu(a, cotangents[0])
     spread_first(a)
     sum_first(b)
-    spread_second(a)
+    spread_second(a, wait=(b.send,))
     sum_second(b)
-    gelu(b, cotangents[1], a.grad_far)
     back(a)
+    gelu(b, cotangents[1], a.away)
     spread_first(b)
-    wa = weights(a, a.away)
-    sent = a.away
-    reduce_first(a)
-    spread_second(b, wait=(sent,), behind=(wa,))
+    reduce_first(a, behind=(b.grad,))
+    reduce_second(a)
+    spread_second(b, behind=(a.away,))
     back(b)
-    sent = a.away
-    reduce_second(a)
-    wb = weights(b, b.away, a.total)
-    weight_grad = (wa + wb).astype(BF)
-    reduce_first(b, wait=(sent,), behind=(weight_grad,))
-    reduce_last(a)
-    reduce_second(b)
+    sent = b.away
+    reduce_first(b, behind=(a.total,))
+    reduce_last(a, sent)
+    reduce_second(b, behind=(a.blocks,))
     reduce_last(b)
+    weight_grad = (weights(a, b.total) + weights(b, b.total)).astype(BF)
 
     input_grad = jnp.concatenate([a.input_grad, b.input_grad], 0)
     activated = jnp.stack([after(a.activated, b.total), b.activated]).reshape(CHUNKS, 8, 2, t, f)

time: 176 us -> 166 us (0.943); the launches traced: 173 us -> 166 us
  waiting for transfers between devices: 90.5 us -> 71.6 us
  other arithmetic: 5.63 us -> 10.8 us
  starting transfers between devices: 38.7 us -> 41.3 us
  matrix products: 21.9 us -> 24.4 us
    all_to_all x4, waiting for transfers between devices: 35.6 us -> 24.8 us  [the longest x2 18.9 us: spread(): c.own = lax.all_to_all(copies, Z, 0, 0, tiled=True)]
    ppermute x28, waiting for transfers between devices: 54.9 us -> 46.8 us  [permute(): return lax.ppermute(array, AXES, pairs)]
    dot_general x2, matrix products: 9.14 us -> 11.7 us  [weights(): lax.dot_general(c.tokens, grads, (((0,), (0,)), ((), ())), preferred_elem...]
    add x2, other arithmetic: 0.35 us -> 2.62 us  [back(): c.here = keep[:2] + jnp.stack([got[0], got[2]]).astype(F32)]
  transfers between devices with their start and end apart: 32 -> 32, of which waited for: 18 -> 15; matrix products, arithmetic and copies ran while one was open for 20% -> 26% of each run, Pallas kernels for 1% -> 1%
where the time goes in v3:
time: 166 us
  waiting for transfers between devices  71.6 us (43%)
  starting transfers between devices  41.3 us (25%)
  matrix products  24.4 us (15%)
  local copies, waits for them, and re-layouts  13.5 us (8%)
  other arithmetic  10.8 us (7%)
  Pallas kernels  2.94 us (2%)
    ppermute x28, waiting for transfers between devices, permute(): return lax.ppermute(array, AXES, pairs)  46.8 us
    ppermute x28, starting transfers between devices, permute(): return lax.ppermute(array, AXES, pairs)  19.8 us
    all_to_all x2, waiting for transfers between devices, spread(): c.own = lax.all_to_all(copies, Z, 0, 0, tiled=True)  18.9 us
    all_to_all x2, starting transfers between devices, spread(): c.own = lax.all_to_all(copies, Z, 0, 0, tiled=True)  12 us
    dot_general x2, matrix products, weights(): lax.dot_general(c.tokens, grads, (((0,), (0,)), ((), ())), preferred_elem...  11.7 us
    all_to_all x2, starting transfers between devices, reduce_last(): c.blocks = lax.all_to_all(total, Z, 0, 0, tiled=True)  9.48 us
    dot_general x2, matrix products, project(): jnp.dot(tokens, weight, preferred_element_type=F32).reshape(8, 4, 2 * t, f)  7.1 us
    unnamed x18, local copies, waits for them, and re-layouts  6.65 us
  transfers between devices with their start and end apart: 32, of which 15 were waited for; matrix products, arithmetic and copies ran while one was open for 26% of the time, Pallas kernels for 1%

profile of v3, /device:TPU:56, one launch (start us, length us, event | category | flops | bytes accessed | tf_op | source)
XLA Modules:
  0.0 165.6 jit_solution(17526164186221251237)
XLA Ops:
  0.6 0.8 fusion.34
  2.2 8.6 %all-to-all-start = ((bf16[8,8,3072]{2,1,0:T(8,128)(2,1)}), bf16[8,8,3072]{2,1,0:T(8,128)(2,1)S(1)}, u32[]{:S(2)}, u32[]{:S(2)}) async-start(bf16[8,8,3072]{2,1,0:T(8,128)(2,1)} %broadcast_in_dim.4), calls=%async_computation | async-start | bytes 786432 | tf_op jit(solution)/shard_map/all_to_all | solution.py:120
  10.8 1.0 copy.22
  12.0 12.1 %all-to-all-done = bf16[8,8,3072]{2,1,0:T(8,128)(2,1)S(1)} async-done(((bf16[8,8,3072]{2,1,0:T(8,128)(2,1)}), bf16[8,8,3072]{2,1,0:T(8,128)(2,1)S(1)}, u32[]{:S(2)}, u32[]{:S(2)}) %all-to-all-start) | async-done | bytes 393248 | tf_op jit(solution)/shard_map/all_to_all | solution.py:120
  24.0 2.8 %collective-permute-start.1 = (bf16[8,8,3072]{2,1,0:T(8,128)(2,1)S(1)}, bf16[8,8,3072]{2,1,0:T(8,128)(2,1)S(1)}, u32[]{:S(2)}, u32[]{:S(2)}) collective-permute-start(bf16[8,8,3072]{2,1,0:T(8,128)(2,1)S(1)} %all-to-all-done), channel_id=1, source_target_pairs={{0,6},{1,3},{2,4},{3,1},{4,2},{5,7},{6,0},{7,5},{8,14},{9,11},{10,... | collective-permute-start | bytes 1179656 | tf_op jit(solution)/shard_map/ppermute | solution.py:29
  27.9 3.4 %all-to-all-start.1 = ((bf16[8,8,3072]{2,1,0:T(8,128)(2,1)}), bf16[8,8,3072]{2,1,0:T(8,128)(2,1)S(1)}, u32[]{:S(2)}, u32[]{:S(2)}) async-start(bf16[8,8,3072]{2,1,0:T(8,128)(2,1)} %broadcast_in_dim.5), calls=%async_computation.1 | async-start | bytes 786432 | tf_op jit(solution)/shard_map/all_to_all | solution.py:120
  32.2 2.3 %collective-permute-done = bf16[8,8,3072]{2,1,0:T(8,128)(2,1)S(1)} collective-permute-done((bf16[8,8,3072]{2,1,0:T(8,128)(2,1)S(1)}, bf16[8,8,3072]{2,1,0:T(8,128)(2,1)S(1)}, u32[]{:S(2)}, u32[]{:S(2)}) %collective-permute-start) | collective-permute-done | bytes 393248 | tf_op jit(solution)/shard_map/ppermute | solution.py:29
  34.6 1.0 collective-permute-start.2
  37.1 6.8 %all-to-all-done.1 = bf16[8,8,3072]{2,1,0:T(8,128)(2,1)S(1)} async-done(((bf16[8,8,3072]{2,1,0:T(8,128)(2,1)}), bf16[8,8,3072]{2,1,0:T(8,128)(2,1)S(1)}, u32[]{:S(2)}, u32[]{:S(2)}) %all-to-all-start.1) | async-done | bytes 393248 | tf_op jit(solution)/shard_map/all_to_all | solution.py:120
  43.9 1.2 collective-permute-start.10
  47.0 1.8 %constant_dynamic-update-slice_fusion.2 = bf16[64,8,3072]{2,1,0:T(8,128)(2,1)} fusion(bf16[64,8,3072]{2,1,0:T(8,128)(2,1)} %constant_dynamic-update-slice_fusion.3, bf16[8,8,3072]{2,1,0:T(8,128)(2,1)} %collective-permute-done.4), kind=kLoop, calls=%fused_computation.55 | loop fusion | bytes 786432
  50.3 4.5 %fusion = f32[8,4,16,768]{3,2,1,0:T(8,128)S(1)} fusion(bf16[8,4,16,3072]{3,2,1,0:T(8,128)(2,1)} %bitcast.2, bf16[3072,768]{1,0:T(8,128)(2,1)S(1)} %copy-done), kind=kOutput, calls=%fused_computation.1 | convolution fusion | flops 2415919104 | bytes 9437184 | tf_op jit(solution)/shard_map/dot_general | solution.py:134
  54.9 0.8 collective-permute-start.7
  55.8 1.3 collective-permute-start.14
  57.0 1.2 collective-permute-start.11
  58.3 4.5 %collective-permute-done.7 = bf16[2,8,16,768]{3,2,1,0:T(8,128)(2,1)S(1)} collective-permute-done((bf16[2,8,16,768]{3,2,1,0:T(8,128)(2,1)S(1)}, bf16[2,8,16,768]{3,2,1,0:T(8,128)(2,1)S(1)}, u32[]{:S(2)}, u32[]{:S(2)}) %collective-permute-start.7) | collective-permute-done | bytes 393248 | tf_op jit(solution)/shard_map/ppermute | solution.py:29
  63.3 2.7 %collective-permute-done.11 = bf16[8,8,3072]{2,1,0:T(8,128)(2,1)S(1)} collective-permute-done((bf16[8,8,3072]{2,1,0:T(8,128)(2,1)S(1)}, bf16[8,8,3072]{2,1,0:T(8,128)(2,1)S(1)}, u32[]{:S(2)}, u32[]{:S(2)}) %collective-permute-start.11) | collective-permute-done | bytes 393248 | tf_op jit(solution)/shard_map/ppermute | solution.py:29
  66.2 3.7 %collective-permute-done.8.other_ref = bf16[8,16,768]{2,1,0:T(8,128)(2,1)S(1)} collective-permute-done((bf16[8,16,768]{2,1,0:T(8,128)(2,1)S(1)}, bf16[8,16,768]{2,1,0:T(8,128)(2,1)S(1)}, u32[]{:S(2)}, u32[]{:S(2)}) %collective-permute-start.8) | collective-permute-done | bytes 196640 | tf_op jit(solution)/shard_map/ppermute | solution.py:29
  69.9 0.9 gelu.2
  71.2 2.6 %fusion.35 = f32[512,768]{1,0:T(8,128)S(1)} fusion(bf16[512,3072]{1,0:T(8,128)(2,1)S(1)} %bitcast.160, bf16[3072,768]{1,0:T(8,128)(2,1)S(1)} %copy-done), kind=kOutput, calls=%fused_computation.83 | convolution fusion | flops 2415919104 | bytes 9437184 | tf_op jit(solution)/shard_map/dot_general | solution.py:134
  73.9 3.9 %collective-permute-done.18.b_ref = bf16[8,16,768]{2,1,0:T(8,128)(2,1)S(1)} collective-permute-done((bf16[8,16,768]{2,1,0:T(8,128)(2,1)S(1)}, bf16[8,16,768]{2,1,0:T(8,128)(2,1)S(1)}, u32[]{:S(2)}, u32[]{:S(2)}) %collective-permute-start.18) | collective-permute-done | bytes 196640 | tf_op jit(solution)/shard_map/ppermute | solution.py:29
  78.0 2.0 %collective-permute-start.16 = (bf16[2,8,16,768]{3,2,1,0:T(8,128)(2,1)S(1)}, bf16[2,8,16,768]{3,2,1,0:T(8,128)(2,1)S(1)}, u32[]{:S(2)}, u32[]{:S(2)}) collective-permute-start(bf16[2,8,16,768]{3,2,1,0:T(8,128)(2,1)S(1)} %pad_maximum_fusion.1), channel_id=1, source_target_pairs={{0,64},{1,193},{2,66},{3,195},{4,68},{5,197},{6,70},{7,199},{8,72}... | collective-permute-start | bytes 1179656 | tf_op jit(solution)/shard_map/ppermute | solution.py:29
  80.0 5.7 %collective-permute-done.19.c_ref = bf16[2,8,16,768]{3,2,1,0:T(8,128)(2,1)S(1)} collective-permute-done((bf16[2,8,16,768]{3,2,1,0:T(8,128)(2,1)S(1)}, bf16[2,8,16,768]{3,2,1,0:T(8,128)(2,1)S(1)}, u32[]{:S(2)}, u32[]{:S(2)}) %collective-permute-start.19) | collective-permute-done | bytes 393248 | tf_op jit(solution)/shard_map/ppermute | solution.py:29
  86.4 1.4 convolution_convert_fusion.1
  87.9 2.0 %collective-permute-done.16 = bf16[2,8,16,768]{3,2,1,0:T(8,128)(2,1)S(1)} collective-permute-done((bf16[2,8,16,768]{3,2,1,0:T(8,128)(2,1)S(1)}, bf16[2,8,16,768]{3,2,1,0:T(8,128)(2,1)S(1)}, u32[]{:S(2)}, u32[]{:S(2)}) %collective-permute-start.16) | collective-permute-done | bytes 393248 | tf_op jit(solution)/shard_map/ppermute | solution.py:29
  90.4 1.4 fusion.36
  92.4 2.2 %collective-permute-start.23 = (bf16[2,64,3072]{2,1,0:T(8,128)(2,1)S(1)}, bf16[2,64,3072]{2,1,0:T(8,128)(2,1)S(1)}, u32[]{:S(2)}, u32[]{:S(2)}) collective-permute-start(bf16[2,64,3072]{2,1,0:T(8,128)(2,1)S(1)} %add_convert_fusion.2), channel_id=1, source_target_pairs={{0,6},{1,3},{2,4},{3,1},{4,2},{5,7},{6,0},{7,5},{8,14},{9,11},{10,... | collective-permute-start | bytes 2359304 | tf_op jit(solution)/shard_map/ppermute | solution.py:29
  94.6 2.5 %collective-permute-done.17.other_ref = bf16[8,16,768]{2,1,0:T(8,128)(2,1)S(1)} collective-permute-done((bf16[8,16,768]{2,1,0:T(8,128)(2,1)S(1)}, bf16[8,16,768]{2,1,0:T(8,128)(2,1)S(1)}, u32[]{:S(2)}, u32[]{:S(2)}) %collective-permute-start.17) | collective-permute-done | bytes 196640 | tf_op jit(solution)/shard_map/ppermute | solution.py:29
  97.1 0.9 gelu.3
  98.8 8.0 %collective-permute-done.21.b_ref = bf16[8,16,768]{2,1,0:T(8,128)(2,1)S(1)} collective-permute-done((bf16[8,16,768]{2,1,0:T(8,128)(2,1)S(1)}, bf16[8,16,768]{2,1,0:T(8,128)(2,1)S(1)}, u32[]{:S(2)}, u32[]{:S(2)}) %collective-permute-start.21) | collective-permute-done | bytes 196640 | tf_op jit(solution)/shard_map/ppermute | solution.py:29
  106.9 7.7 %collective-permute-done.22.c_ref = bf16[2,8,16,768]{3,2,1,0:T(8,128)(2,1)S(1)} collective-permute-done((bf16[2,8,16,768]{3,2,1,0:T(8,128)(2,1)S(1)}, bf16[2,8,16,768]{3,2,1,0:T(8,128)(2,1)S(1)}, u32[]{:S(2)}, u32[]{:S(2)}) %collective-permute-start.22) | collective-permute-done | bytes 393248 | tf_op jit(solution)/shard_map/ppermute | solution.py:29
  115.3 1.4 convolution_convert_fusion
  117.0 2.1 %collective-permute-start.26 = (bf16[64,3072]{1,0:T(8,128)(2,1)S(1)}, bf16[64,3072]{1,0:T(8,128)(2,1)S(1)}, u32[]{:S(2)}, u32[]{:S(2)}) collective-permute-start(bf16[64,3072]{1,0:T(8,128)(2,1)S(1)} %fusion.11), channel_id=1, source_target_pairs={{0,2},{1,7},{2,0},{3,5},{4,6},{5,3},{6,4},{7,1},{8,10},{9,15},{10,... | collective-permute-start | bytes 1179656 | tf_op jit(solution)/shard_map/ppermute | solution.py:29
  119.1 1.4 fusion.37
  120.8 1.0 fusion.30
  121.8 1.1 add_convert_fusion.1
  122.8 2.1 %collective-permute-start.25 = (bf16[2,64,3072]{2,1,0:T(8,128)(2,1)}, bf16[2,64,3072]{2,1,0:T(8,128)(2,1)}, u32[]{:S(2)}, u32[]{:S(2)}) collective-permute-start(bf16[2,64,3072]{2,1,0:T(8,128)(2,1)} %add_convert_fusion.1), channel_id=1, source_target_pairs={{0,6},{1,3},{2,4},{3,1},{4,2},{5,7},{6,0},{7,5},{8,14},{9,11},{10,... | collective-permute-start | bytes 2359304 | tf_op jit(solution)/shard_map/ppermute | solution.py:29
  124.9 0.9 fusion.13
  125.8 4.7 %all-to-all-start.2 = ((bf16[8,8,3072]{2,1,0:T(8,128)(2,1)}), bf16[8,8,3072]{2,1,0:T(8,128)(2,1)}, u32[]{:S(2)}, u32[]{:S(2)}) async-start(bf16[8,8,3072]{2,1,0:T(8,128)(2,1)} %fusion.13), calls=%async_computation.2 | async-start | bytes 786432 | tf_op jit(solution)/shard_map/all_to_all | solution.py:176
  130.5 2.4 %convert_add_fusion = f32[2,64,3072]{2,1,0:T(8,128)} fusion(f32[2,64,3072]{2,1,0:T(8,128)S(1)} %bitcast.150, bf16[1,64,3072]{2,1,0:T(8,128)(2,1)} %get-tuple-element.47, bf16[1,64,3072]{2,1,0:T(8,128)(2,1)} %get-tuple-element.48), kind=kLoop, calls=%fused_computation.7 | loop fusion | flops 1179648 | bytes 3932160 | tf_op jit(solution)/shard_map/add | solution.py:162
  132.9 3.4 %collective-permute-done.25 = bf16[2,64,3072]{2,1,0:T(8,128)(2,1)} collective-permute-done((bf16[2,64,3072]{2,1,0:T(8,128)(2,1)}, bf16[2,64,3072]{2,1,0:T(8,128)(2,1)}, u32[]{:S(2)}, u32[]{:S(2)}) %collective-permute-start.25) | collective-permute-done | bytes 786464 | tf_op jit(solution)/shard_map/ppermute | solution.py:29
  136.4 1.3 fusion.14
  138.2 5.9 %all-to-all-done.2 = bf16[8,8,3072]{2,1,0:T(8,128)(2,1)} async-done(((bf16[8,8,3072]{2,1,0:T(8,128)(2,1)}), bf16[8,8,3072]{2,1,0:T(8,128)(2,1)}, u32[]{:S(2)}, u32[]{:S(2)}) %all-to-all-start.2) | async-done | bytes 393248 | tf_op jit(solution)/shard_map/all_to_all | solution.py:176
  144.1 1.1 reduce_sum.24
  145.5 2.1 %fusion.12 = bf16[8,8,3072]{2,1,0:T(8,128)(2,1)} fusion(bf16[64,3072]{1,0:T(8,128)(2,1)S(1)} %collective-permute-done.27, f32[2,64,3072]{2,1,0:T(8,128)} %convert_add_fusion, bf16[2,64,3072]{2,1,0:T(8,128)(2,1)} %collective-permute-done.25), kind=kLoop, calls=%fused_computation.23 | loop fusion | flops 983040 | bytes 1966080 | tf_op jit(solution)/shard_map/reshape | solution.py:172
  147.6 4.8 %all-to-all-start.3 = ((bf16[8,8,3072]{2,1,0:T(8,128)(2,1)}), bf16[8,8,3072]{2,1,0:T(8,128)(2,1)S(1)}, u32[]{:S(2)}, u32[]{:S(2)}) async-start(bf16[8,8,3072]{2,1,0:T(8,128)(2,1)} %fusion.12), calls=%async_computation.3 | async-start | bytes 786432 | tf_op jit(solution)/shard_map/all_to_all | solution.py:176
  153.2 4.6 %fusion.26 = f32[3072,768]{1,0:T(8,128)S(1)} fusion(bf16[512,768]{1,0:T(8,128)(2,1)S(1)} %bitcast.140, bf16[64,8,3072]{2,1,0:T(8,128)(2,1)} %copy-done.1), kind=kOutput, calls=%fused_computation.74 | convolution fusion | flops 2415919104 | bytes 13369344 | tf_op jit(solution)/shard_map/dot_general | solution.py:181
  157.8 7.1 %add_convert_fusion = bf16[3072,768]{1,0:T(8,128)(2,1)} fusion(f32[3072,768]{1,0:T(8,128)S(1)} %fusion.26, bf16[512,768]{1,0:T(8,128)(2,1)S(1)} %bitcast.139, bf16[64,8,3072]{2,1,0:T(8,128)(2,1)} %constant_dynamic-update-slice_fusion), kind=kOutput, calls=%fused_computation | convolution fusion | flops 2420637696 | bytes 18087936 | tf_op jit(solution)/shard_map/dot_general | solution.py:181
  (87 shorter events, 15.6 us)
Async XLA Ops:
  2.2 21.8 %all-to-all-start = ((bf16[8,8,3072]{2,1,0:T(8,128)(2,1)}), bf16[8,8,3072]{2,1,0:T(8,128)(2,1)S(1)}, u32[]{:S(2)}, u32[]{:S(2)}) async-start(bf16[8,8,3072]{2,1,0:T(8,128)(2,1)} %broadcast_in_dim.4), calls=%async_computation | async-start | bytes 786432 | tf_op jit(solution)/shard_map/all_to_all | solution.py:120
  24.0 11.5 %collective-permute-start.1 = (bf16[8,8,3072]{2,1,0:T(8,128)(2,1)S(1)}, bf16[8,8,3072]{2,1,0:T(8,128)(2,1)S(1)}, u32[]{:S(2)}, u32[]{:S(2)}) collective-permute-start(bf16[8,8,3072]{2,1,0:T(8,128)(2,1)S(1)} %all-to-all-done), channel_id=1, source_target_pairs={{0,6},{1,3},{2,4},{3,1},{4,2},{5,7},{6,0},{7,5},{8,14},{9,11},{10,... | collective-permute-start | bytes 1179656 | tf_op jit(solution)/shard_map/ppermute | solution.py:29
  26.8 7.8 %collective-permute-start = (bf16[8,8,3072]{2,1,0:T(8,128)(2,1)S(1)}, bf16[8,8,3072]{2,1,0:T(8,128)(2,1)S(1)}, u32[]{:S(2)}, u32[]{:S(2)}) collective-permute-start(bf16[8,8,3072]{2,1,0:T(8,128)(2,1)S(1)} %all-to-all-done), channel_id=1, source_target_pairs={{0,2},{1,7},{2,0},{3,5},{4,6},{5,3},{6,4},{7,1},{8,10},{9,15},{10,... | collective-permute-start | bytes 1179656 | tf_op jit(solution)/shard_map/ppermute | solution.py:29
  27.9 15.9 %all-to-all-start.1 = ((bf16[8,8,3072]{2,1,0:T(8,128)(2,1)}), bf16[8,8,3072]{2,1,0:T(8,128)(2,1)S(1)}, u32[]{:S(2)}, u32[]{:S(2)}) async-start(bf16[8,8,3072]{2,1,0:T(8,128)(2,1)} %broadcast_in_dim.5), calls=%async_computation.1 | async-start | bytes 786432 | tf_op jit(solution)/shard_map/all_to_all | solution.py:120
  31.4 14.6 %collective-permute-start.3 = (bf16[8,8,3072]{2,1,0:T(8,128)(2,1)S(1)}, bf16[8,8,3072]{2,1,0:T(8,128)(2,1)S(1)}, u32[]{:S(2)}, u32[]{:S(2)}) collective-permute-start(bf16[8,8,3072]{2,1,0:T(8,128)(2,1)S(1)} %all-to-all-done), channel_id=1, source_target_pairs={{0,1},{1,0},{2,3},{3,2},{4,5},{5,4},{6,7},{7,6},{8,9},{9,8},{10,11... | collective-permute-start | bytes 1179656 | tf_op jit(solution)/shard_map/ppermute | solution.py:29
  34.6 14.2 %collective-permute-start.5 = (bf16[8,8,3072]{2,1,0:T(8,128)(2,1)S(1)}, bf16[8,8,3072]{2,1,0:T(8,128)(2,1)S(1)}, u32[]{:S(2)}, u32[]{:S(2)}) collective-permute-start(bf16[8,8,3072]{2,1,0:T(8,128)(2,1)S(1)} %collective-permute-done), channel_id=1, source_target_pairs={{0,1},{1,0},{2,3},{3,2},{4,5},{5,4},{6,7},{7,6},{8,9},{9,8},{10,11... | collective-permute-start | bytes 1179656 | tf_op jit(solution)/shard_map/ppermute | solution.py:29
  34.6 9.4 %collective-permute-start.2 = (bf16[8,8,3072]{2,1,0:T(8,128)(2,1)S(1)}, bf16[8,8,3072]{2,1,0:T(8,128)(2,1)S(1)}, u32[]{:S(2)}, u32[]{:S(2)}) collective-permute-start(bf16[8,8,3072]{2,1,0:T(8,128)(2,1)S(1)} %collective-permute-done), channel_id=1, source_target_pairs={{0,6},{1,3},{2,4},{3,1},{4,2},{5,7},{6,0},{7,5},{8,14},{9,11},{10,... | collective-permute-start | bytes 1179656 | tf_op jit(solution)/shard_map/ppermute | solution.py:29
  35.5 11.2 %collective-permute-start.4 = (bf16[8,8,3072]{2,1,0:T(8,128)(2,1)S(1)}, bf16[8,8,3072]{2,1,0:T(8,128)(2,1)}, u32[]{:S(2)}, u32[]{:S(2)}) collective-permute-start(bf16[8,8,3072]{2,1,0:T(8,128)(2,1)S(1)} %collective-permute-done.1), channel_id=1, source_target_pairs={{0,1},{1,0},{2,3},{3,2},{4,5},{5,4},{6,7},{7,6},{8,9},{9,8},{10,11... | collective-permute-start | bytes 1179656 | tf_op jit(solution)/shard_map/ppermute | solution.py:29
  43.9 6.4 %copy-start = (bf16[3072,768]{1,0:T(8,128)(2,1)S(1)}, bf16[3072,768]{1,0:T(8,128)(2,1)}, u32[]{:S(2)}) copy-start(bf16[3072,768]{1,0:T(8,128)(2,1)} %param.4) | copy-start | bytes 14155780
  43.9 22.2 %collective-permute-start.12 = (bf16[8,8,3072]{2,1,0:T(8,128)(2,1)S(1)}, bf16[8,8,3072]{2,1,0:T(8,128)(2,1)S(1)}, u32[]{:S(2)}, u32[]{:S(2)}) collective-permute-start(bf16[8,8,3072]{2,1,0:T(8,128)(2,1)S(1)} %all-to-all-done.1), channel_id=1, source_target_pairs={{0,1},{1,0},{2,3},{3,2},{4,5},{5,4},{6,7},{7,6},{8,9},{9,8},{10,11... | collective-permute-start | bytes 1179656 | tf_op jit(solution)/shard_map/ppermute | solution.py:29
  43.9 14.3 %collective-permute-start.10 = (bf16[8,8,3072]{2,1,0:T(8,128)(2,1)S(1)}, bf16[8,8,3072]{2,1,0:T(8,128)(2,1)S(1)}, u32[]{:S(2)}, u32[]{:S(2)}) collective-permute-start(bf16[8,8,3072]{2,1,0:T(8,128)(2,1)S(1)} %all-to-all-done.1), channel_id=1, source_target_pairs={{0,6},{1,3},{2,4},{3,1},{4,2},{5,7},{6,0},{7,5},{8,14},{9,11},{10,... | collective-permute-start | bytes 1179656 | tf_op jit(solution)/shard_map/ppermute | solution.py:29
  46.0 9.8 %collective-permute-start.9 = (bf16[8,8,3072]{2,1,0:T(8,128)(2,1)S(1)}, bf16[8,8,3072]{2,1,0:T(8,128)(2,1)S(1)}, u32[]{:S(2)}, u32[]{:S(2)}) collective-permute-start(bf16[8,8,3072]{2,1,0:T(8,128)(2,1)S(1)} %all-to-all-done.1), channel_id=1, source_target_pairs={{0,2},{1,7},{2,0},{3,5},{4,6},{5,3},{6,4},{7,1},{8,10},{9,15},{10,... | collective-permute-start | bytes 1179656 | tf_op jit(solution)/shard_map/ppermute | solution.py:29
  46.7 2.8 %collective-permute-start.6 = (bf16[8,8,3072]{2,1,0:T(8,128)(2,1)S(1)}, bf16[8,8,3072]{2,1,0:T(8,128)(2,1)S(1)}, u32[]{:S(2)}, u32[]{:S(2)}) collective-permute-start(bf16[8,8,3072]{2,1,0:T(8,128)(2,1)S(1)} %collective-permute-done.2), channel_id=1, source_target_pairs={{0,1},{1,0},{2,3},{3,2},{4,5},{5,4},{6,7},{7,6},{8,9},{9,8},{10,11... | collective-permute-start | bytes 1179656 | tf_op jit(solution)/shard_map/ppermute | solution.py:29
  54.9 7.9 %collective-permute-start.7 = (bf16[2,8,16,768]{3,2,1,0:T(8,128)(2,1)S(1)}, bf16[2,8,16,768]{3,2,1,0:T(8,128)(2,1)S(1)}, u32[]{:S(2)}, u32[]{:S(2)}) collective-permute-start(bf16[2,8,16,768]{3,2,1,0:T(8,128)(2,1)S(1)} %pad_maximum_fusion), channel_id=1, source_target_pairs={{0,64},{1,193},{2,66},{3,195},{4,68},{5,197},{6,70},{7,199},{8,72}... | collective-permute-start | bytes 1179656 | tf_op jit(solution)/shard_map/ppermute | solution.py:29
  55.8 10.4 %collective-permute-start.14 = (bf16[8,8,3072]{2,1,0:T(8,128)(2,1)S(1)}, bf16[8,8,3072]{2,1,0:T(8,128)(2,1)S(1)}, u32[]{:S(2)}, u32[]{:S(2)}) collective-permute-start(bf16[8,8,3072]{2,1,0:T(8,128)(2,1)S(1)} %collective-permute-done.9), channel_id=1, source_target_pairs={{0,1},{1,0},{2,3},{3,2},{4,5},{5,4},{6,7},{7,6},{8,9},{9,8},{10,11... | collective-permute-start | bytes 1179656 | tf_op jit(solution)/shard_map/ppermute | solution.py:29
  57.0 9.0 %collective-permute-start.11 = (bf16[8,8,3072]{2,1,0:T(8,128)(2,1)S(1)}, bf16[8,8,3072]{2,1,0:T(8,128)(2,1)S(1)}, u32[]{:S(2)}, u32[]{:S(2)}) collective-permute-start(bf16[8,8,3072]{2,1,0:T(8,128)(2,1)S(1)} %collective-permute-done.9), channel_id=1, source_target_pairs={{0,6},{1,3},{2,4},{3,1},{4,2},{5,7},{6,0},{7,5},{8,14},{9,11},{10,... | collective-permute-start | bytes 1179656 | tf_op jit(solution)/shard_map/ppermute | solution.py:29
  58.2 7.9 %collective-permute-start.13 = (bf16[8,8,3072]{2,1,0:T(8,128)(2,1)S(1)}, bf16[8,8,3072]{2,1,0:T(8,128)(2,1)S(1)}, u32[]{:S(2)}, u32[]{:S(2)}) collective-permute-start(bf16[8,8,3072]{2,1,0:T(8,128)(2,1)S(1)} %collective-permute-done.10), channel_id=1, source_target_pairs={{0,1},{1,0},{2,3},{3,2},{4,5},{5,4},{6,7},{7,6},{8,9},{9,8},{10,11... | collective-permute-start | bytes 1179656 | tf_op jit(solution)/shard_map/ppermute | solution.py:29
  63.0 7.0 %collective-permute-start.8 = (bf16[8,16,768]{2,1,0:T(8,128)(2,1)S(1)}, bf16[8,16,768]{2,1,0:T(8,128)(2,1)S(1)}, u32[]{:S(2)}, u32[]{:S(2)}) collective-permute-start(bf16[8,16,768]{2,1,0:T(8,128)(2,1)S(1)} %get-tuple-element.42), channel_id=1, source_target_pairs={{0,192},{1,65},{2,194},{3,67},{4,196},{5,69},{6,198},{7,71},{8,200... | collective-permute-start | bytes 589832 | tf_op jit(solution)/shard_map/ppermute | solution.py:29
  66.0 5.1 %collective-permute-start.15 = (bf16[8,8,3072]{2,1,0:T(8,128)(2,1)S(1)}, bf16[8,8,3072]{2,1,0:T(8,128)(2,1)S(1)}, u32[]{:S(2)}, u32[]{:S(2)}) collective-permute-start(bf16[8,8,3072]{2,1,0:T(8,128)(2,1)S(1)} %collective-permute-done.11), channel_id=1, source_target_pairs={{0,1},{1,0},{2,3},{3,2},{4,5},{5,4},{6,7},{7,6},{8,9},{9,8},{10,11... | collective-permute-start | bytes 1179656 | tf_op jit(solution)/shard_map/ppermute | solution.py:29
  70.8 7.0 %collective-permute-start.18 = (bf16[8,16,768]{2,1,0:T(8,128)(2,1)S(1)}, bf16[8,16,768]{2,1,0:T(8,128)(2,1)S(1)}, u32[]{:S(2)}, u32[]{:S(2)}) collective-permute-start(bf16[8,16,768]{2,1,0:T(8,128)(2,1)S(1)} %get-tuple-element.24.a_ref), channel_id=1, source_target_pairs={{0,192},{1,65},{2,194},{3,67},{4,196},{5,69},{6,198},{7,71},{8,200... | collective-permute-start | bytes 589832 | tf_op jit(solution)/shard_map/ppermute | solution.py:29
  71.2 2.6 %copy-start.1 = (bf16[64,8,3072]{2,1,0:T(8,128)(2,1)}, bf16[64,8,3072]{2,1,0:T(8,128)(2,1)S(1)}, u32[]{:S(2)}) copy-start(bf16[64,8,3072]{2,1,0:T(8,128)(2,1)S(1)} %constant_dynamic-update-slice_fusion.8) | copy-start | bytes 9437188
  77.8 7.9 %collective-permute-start.19 = (bf16[2,8,16,768]{3,2,1,0:T(8,128)(2,1)S(1)}, bf16[2,8,16,768]{3,2,1,0:T(8,128)(2,1)S(1)}, u32[]{:S(2)}, u32[]{:S(2)}) collective-permute-start(bf16[2,8,16,768]{3,2,1,0:T(8,128)(2,1)S(1)} %pad_maximum_fusion.2), channel_id=1, source_target_pairs={{0,64},{1,193},{2,66},{3,195},{4,68},{5,197},{6,70},{7,199},{8,72}... | collective-permute-start | bytes 1179656 | tf_op jit(solution)/shard_map/ppermute | solution.py:29
  78.0 11.9 %collective-permute-start.16 = (bf16[2,8,16,768]{3,2,1,0:T(8,128)(2,1)S(1)}, bf16[2,8,16,768]{3,2,1,0:T(8,128)(2,1)S(1)}, u32[]{:S(2)}, u32[]{:S(2)}) collective-permute-start(bf16[2,8,16,768]{3,2,1,0:T(8,128)(2,1)S(1)} %pad_maximum_fusion.1), channel_id=1, source_target_pairs={{0,64},{1,193},{2,66},{3,195},{4,68},{5,197},{6,70},{7,199},{8,72}... | collective-permute-start | bytes 1179656 | tf_op jit(solution)/shard_map/ppermute | solution.py:29
  87.8 4.2 %collective-permute-start.20 = (bf16[4,64,3072]{2,1,0:T(8,128)(2,1)S(1)}, bf16[4,64,3072]{2,1,0:T(8,128)(2,1)S(1)}, u32[]{:S(2)}, u32[]{:S(2)}) collective-permute-start(bf16[4,64,3072]{2,1,0:T(8,128)(2,1)S(1)} %bitcast.161), channel_id=1, source_target_pairs={{0,1},{1,0},{2,3},{3,2},{4,5},{5,4},{6,7},{7,6},{8,9},{9,8},{10,11... | collective-permute-start | bytes 4718600 | tf_op jit(solution)/shard_map/ppermute | solution.py:29
  90.1 7.0 %collective-permute-start.17 = (bf16[8,16,768]{2,1,0:T(8,128)(2,1)S(1)}, bf16[8,16,768]{2,1,0:T(8,128)(2,1)S(1)}, u32[]{:S(2)}, u32[]{:S(2)}) collective-permute-start(bf16[8,16,768]{2,1,0:T(8,128)(2,1)S(1)} %get-tuple-element.43), channel_id=1, source_target_pairs={{0,192},{1,65},{2,194},{3,67},{4,196},{5,69},{6,198},{7,71},{8,200... | collective-permute-start | bytes 589832 | tf_op jit(solution)/shard_map/ppermute | solution.py:29
  92.4 14.5 %collective-permute-start.23 = (bf16[2,64,3072]{2,1,0:T(8,128)(2,1)S(1)}, bf16[2,64,3072]{2,1,0:T(8,128)(2,1)S(1)}, u32[]{:S(2)}, u32[]{:S(2)}) collective-permute-start(bf16[2,64,3072]{2,1,0:T(8,128)(2,1)S(1)} %add_convert_fusion.2), channel_id=1, source_target_pairs={{0,6},{1,3},{2,4},{3,1},{4,2},{5,7},{6,0},{7,5},{8,14},{9,11},{10,... | collective-permute-start | bytes 2359304 | tf_op jit(solution)/shard_map/ppermute | solution.py:29
  97.9 8.8 %collective-permute-start.21 = (bf16[8,16,768]{2,1,0:T(8,128)(2,1)S(1)}, bf16[8,16,768]{2,1,0:T(8,128)(2,1)S(1)}, u32[]{:S(2)}, u32[]{:S(2)}) collective-permute-start(bf16[8,16,768]{2,1,0:T(8,128)(2,1)S(1)} %get-tuple-element.27.a_ref), channel_id=1, source_target_pairs={{0,192},{1,65},{2,194},{3,67},{4,196},{5,69},{6,198},{7,71},{8,200... | collective-permute-start | bytes 589832 | tf_op jit(solution)/shard_map/ppermute | solution.py:29
  106.8 7.9 %collective-permute-start.22 = (bf16[2,8,16,768]{3,2,1,0:T(8,128)(2,1)S(1)}, bf16[2,8,16,768]{3,2,1,0:T(8,128)(2,1)S(1)}, u32[]{:S(2)}, u32[]{:S(2)}) collective-permute-start(bf16[2,8,16,768]{3,2,1,0:T(8,128)(2,1)S(1)} %pad_maximum_fusion.3), channel_id=1, source_target_pairs={{0,64},{1,193},{2,66},{3,195},{4,68},{5,197},{6,70},{7,199},{8,72}... | collective-permute-start | bytes 1179656 | tf_op jit(solution)/shard_map/ppermute | solution.py:29
  116.7 4.1 %collective-permute-start.24 = (bf16[4,64,3072]{2,1,0:T(8,128)(2,1)S(1)}, bf16[4,64,3072]{2,1,0:T(8,128)(2,1)S(1)}, u32[]{:S(2)}, u32[]{:S(2)}) collective-permute-start(bf16[4,64,3072]{2,1,0:T(8,128)(2,1)S(1)} %bitcast.162), channel_id=1, source_target_pairs={{0,1},{1,0},{2,3},{3,2},{4,5},{5,4},{6,7},{7,6},{8,9},{9,8},{10,11... | collective-permute-start | bytes 4718600 | tf_op jit(solution)/shard_map/ppermute | solution.py:29
  117.0 7.9 %collective-permute-start.26 = (bf16[64,3072]{1,0:T(8,128)(2,1)S(1)}, bf16[64,3072]{1,0:T(8,128)(2,1)S(1)}, u32[]{:S(2)}, u32[]{:S(2)}) collective-permute-start(bf16[64,3072]{1,0:T(8,128)(2,1)S(1)} %fusion.11), channel_id=1, source_target_pairs={{0,2},{1,7},{2,0},{3,5},{4,6},{5,3},{6,4},{7,1},{8,10},{9,15},{10,... | collective-permute-start | bytes 1179656 | tf_op jit(solution)/shard_map/ppermute | solution.py:29
  122.8 13.5 %collective-permute-start.25 = (bf16[2,64,3072]{2,1,0:T(8,128)(2,1)}, bf16[2,64,3072]{2,1,0:T(8,128)(2,1)}, u32[]{:S(2)}, u32[]{:S(2)}) collective-permute-start(bf16[2,64,3072]{2,1,0:T(8,128)(2,1)} %add_convert_fusion.1), channel_id=1, source_target_pairs={{0,6},{1,3},{2,4},{3,1},{4,2},{5,7},{6,0},{7,5},{8,14},{9,11},{10,... | collective-permute-start | bytes 2359304 | tf_op jit(solution)/shard_map/ppermute | solution.py:29
  125.8 18.3 %all-to-all-start.2 = ((bf16[8,8,3072]{2,1,0:T(8,128)(2,1)}), bf16[8,8,3072]{2,1,0:T(8,128)(2,1)}, u32[]{:S(2)}, u32[]{:S(2)}) async-start(bf16[8,8,3072]{2,1,0:T(8,128)(2,1)} %fusion.13), calls=%async_computation.2 | async-start | bytes 786432 | tf_op jit(solution)/shard_map/all_to_all | solution.py:176
  137.7 7.9 %collective-permute-start.27 = (bf16[64,3072]{1,0:T(8,128)(2,1)S(1)}, bf16[64,3072]{1,0:T(8,128)(2,1)S(1)}, u32[]{:S(2)}, u32[]{:S(2)}) collective-permute-start(bf16[64,3072]{1,0:T(8,128)(2,1)S(1)} %fusion.14), channel_id=1, source_target_pairs={{0,2},{1,7},{2,0},{3,5},{4,6},{5,3},{6,4},{7,1},{8,10},{9,15},{10,... | collective-permute-start | bytes 1179656 | tf_op jit(solution)/shard_map/ppermute | solution.py:29
  147.6 17.2 %all-to-all-start.3 = ((bf16[8,8,3072]{2,1,0:T(8,128)(2,1)}), bf16[8,8,3072]{2,1,0:T(8,128)(2,1)S(1)}, u32[]{:S(2)}, u32[]{:S(2)}) async-start(bf16[8,8,3072]{2,1,0:T(8,128)(2,1)} %fusion.12), calls=%async_computation.3 | async-start | bytes 786432 | tf_op jit(solution)/shard_map/all_to_all | solution.py:176

commit v4 on v3

--- a/solution.py
+++ b/solution.py
@@ -94,6 +94,24 @@
 CHUNKS = 2
 
 
+def copy_kernel(block_ref, *copies_refs):
+    for i, copies_ref in enumerate(copies_refs):
+        copies_ref[...] = jnp.broadcast_to(block_ref[i][None], copies_ref.shape)
+
+
+def copy_call(blocks):
+    chunks, t, d = blocks.shape
+    whole = pl.BlockSpec(memory_space=pltpu.VMEM)
+    return pl.pallas_call(
+        copy_kernel,
+        in_specs=[whole],
+        out_specs=[whole] * chunks,
+        out_shape=[jax.ShapeDtypeStruct((8, t, d), BF)] * chunks,
+        compiler_params=pltpu.CompilerParams(vmem_limit_bytes=16 * 2**20),
+        name="copies",
+    )(blocks)
+
+
 def after(value, *others):
     return lax.optimization_barrier((value, *others))[0] if others else value
 
@@ -110,13 +128,13 @@
     far = jnp.where(core == 0, 3, 1)
     pick = lambda a, i: lax.dynamic_index_in_dim(a, i, 1, keepdims=False)
 
-    steps = jnp.stack([jnp.int32(0), near, far, jnp.int32(2)]).astype(jnp.int32)
-    place = ((x ^ steps)[None] * 2 + (core ^ jnp.arange(2, dtype=jnp.int32))[:, None]).reshape(8).astype(jnp.int32)
+    steps = jnp.stack([jnp.int32(0), near, far, jnp.int32(2), jnp.int32(0), far, near, jnp.int32(2)]).astype(jnp.int32)
+    place = ((x ^ steps) * 2 + (core ^ (jnp.arange(8, dtype=jnp.int32) // 4))).astype(jnp.int32)
     order = jnp.stack([y, y ^ far, y ^ near, y ^ 2]).astype(jnp.int32)
     cotangents = jnp.transpose(out_grad.reshape(2, 8, CHUNKS, t, f), (2, 1, 0, 3, 4)).reshape(CHUNKS, 8, 2 * t, f)
 
-    def spread(c, block, *wait):
-        copies = after(jnp.broadcast_to(block[None], (8, t, d)), *wait)
+    def spread(c, copies, *wait):
+        copies = after(copies, *wait)
         c.own = lax.all_to_all(copies, Z, 0, 0, tiled=True)
 
     def along_x(c, *wait):
@@ -126,7 +144,7 @@
         c.three = permute(c.one, x_second)
 
     def assemble(c):
-        c.other = [permute(p, swap_core) for p in (c.own, c.two, c.one, c.three)]
+        c.other = [permute(p, swap_core) for p in (c.own, c.one, c.two, c.three)]
         c.tokens = jnp.concatenate([c.own, c.one, c.two, c.three] + c.other, 0).reshape(64 * t, d)
 
     def project(c, *wait):
@@ -156,10 +174,10 @@
     def back(c, *wait):
         dims = (((1,), (1,)), ((), ()))
         give = lax.dot_general(c.grad_all[1], weight, dims, preferred_element_type=F32).astype(BF)
-        keep = lax.dot_general(c.grad_all[0], weight, dims, preferred_element_type=F32).reshape(4, 8 * t, d)
+        keep = lax.dot_general(after(c.grad_all[0], *wait), weight, dims, preferred_element_type=F32).reshape(4, 8 * t, d)
         got = permute(give.reshape(4, 8 * t, d), swap_core)
-        c.away = (keep[2:] + jnp.stack([got[1], got[3]]).astype(F32)).astype(BF)
-        c.here = keep[:2] + jnp.stack([got[0], got[2]]).astype(F32)
+        c.away = (keep[2:] + got[2:].astype(F32)).astype(BF)
+        c.here = keep[:2] + got[:2].astype(F32)
 
     def reduce_first(c, wait=(), behind=()):
         got = after(permute(after(c.away, *wait), x_second), *behind)
@@ -181,9 +199,10 @@
         return lax.dot_general(c.tokens, grads, (((0,), (0,)), ((), ())), preferred_element_type=F32)
 
     a, b = Chunk(), Chunk()
-    spread(a, inputs[:t])
+    copies = copy_call(inputs.reshape(CHUNKS, t, d))
+    spread(a, copies[0])
     along_x(a)
-    spread(b, inputs[t:], a.own)
+    spread(b, copies[1], a.own)
     assemble(a)
     along_x(b, a.three)
     project(a)
@@ -196,7 +215,7 @@
     sum_first(b)
     spread_second(a, wait=(b.send,))
     sum_second(b)
-    back(a)
+    back(a, b.theirs)
     gelu(b, cotangents[1], a.away)
     spread_first(b)
     reduce_first(a, behind=(b.grad,))

time: 166 us -> 170 us (1.024)
  waiting for transfers between devices: 71.6 us -> 80.2 us
  local copies, waits for them, and re-layouts: 13.5 us -> 11.2 us
  starting transfers between devices: 41.3 us -> 39.1 us
    ppermute x28, waiting for transfers between devices: 46.8 us -> 56 us  [permute(): return lax.ppermute(array, AXES, pairs)]
    add x3 -> x2, other arithmetic: 2.69 us -> 0.42 us  [the longest x1 0.41 us: back(): c.here = keep[:2] + got[:2].astype(F32)]
    ppermute x28, starting transfers between devices: 19.8 us -> 17.6 us  [permute(): return lax.ppermute(array, AXES, pairs)]
    slice x5 -> x2, local copies, waits for them, and re-layouts: 2.4 us -> 0.68 us  [the longest x1 0.34 us: back(): c.here = keep[:2] + got[:2].astype(F32)]
    unnamed x18 -> x22, local copies, waits for them, and re-layouts: 6.65 us -> 7.58 us
  transfers between devices with their start and end apart: 32 -> 32, of which waited for: 15 -> 16; matrix products, arithmetic and copies ran while one was open for 26% -> 23% of each run, Pallas kernels for 1% -> 1%
where the time goes in v4:
time: 170 us; the launch traced here: 169 us
  waiting for transfers between devices  80.2 us (47%)
  starting transfers between devices  39.1 us (23%)
  matrix products  24.4 us (14%)
  local copies, waits for them, and re-layouts  11.2 us (7%)
  other arithmetic  9.5 us (6%)
  Pallas kernels  3.84 us (2%)
    ppermute x28, waiting for transfers between devices, permute(): return lax.ppermute(array, AXES, pairs)  56 us
    all_to_all x2, waiting for transfers between devices, spread(): c.own = lax.all_to_all(copies, Z, 0, 0, tiled=True)  17.9 us
    ppermute x28, starting transfers between devices, permute(): return lax.ppermute(array, AXES, pairs)  17.6 us
    all_to_all x2, starting transfers between devices, spread(): c.own = lax.all_to_all(copies, Z, 0, 0, tiled=True)  12 us
    dot_general x2, matrix products, weights(): lax.dot_general(c.tokens, grads, (((0,), (0,)), ((), ())), preferred_elem...  11.7 us
    all_to_all x2, starting transfers between devices, reduce_last(): c.blocks = lax.all_to_all(total, Z, 0, 0, tiled=True)  9.54 us
    unnamed x22, local copies, waits for them, and re-layouts  7.58 us
    dot_general x2, matrix products, project(): jnp.dot(tokens, weight, preferred_element_type=F32).reshape(8, 4, 2 * t, f)  7.1 us
  transfers between devices with their start and end apart: 32, of which 16 were waited for; matrix products, arithmetic and copies ran while one was open for 23% of the time, Pallas kernels for 1%

profile of v4, /device:TPU:56, one launch (start us, length us, event | category | flops | bytes accessed | tf_op | source)
XLA Modules:
  0.0 169.2 jit_solution(5974371036497239475)
XLA Ops:
  0.6 0.9 copy-done
  1.5 0.9 copies.1
  2.4 8.6 %all-to-all-start = ((bf16[8,8,3072]{2,1,0:T(8,128)(2,1)}), bf16[8,8,3072]{2,1,0:T(8,128)(2,1)S(1)}, u32[]{:S(2)}, u32[]{:S(2)}) async-start(bf16[8,8,3072]{2,1,0:T(8,128)(2,1)} %get-tuple-element.23), calls=%async_computation | async-start | bytes 786432 | tf_op jit(solution)/shard_map/all_to_all | solution.py:138
  11.0 1.0 copy.22
  12.1 12.1 %all-to-all-done = bf16[8,8,3072]{2,1,0:T(8,128)(2,1)S(1)} async-done(((bf16[8,8,3072]{2,1,0:T(8,128)(2,1)}), bf16[8,8,3072]{2,1,0:T(8,128)(2,1)S(1)}, u32[]{:S(2)}, u32[]{:S(2)}) %all-to-all-start) | async-done | bytes 393248 | tf_op jit(solution)/shard_map/all_to_all | solution.py:138
  24.2 2.8 %collective-permute-start.1 = (bf16[8,8,3072]{2,1,0:T(8,128)(2,1)S(1)}, bf16[8,8,3072]{2,1,0:T(8,128)(2,1)S(1)}, u32[]{:S(2)}, u32[]{:S(2)}) collective-permute-start(bf16[8,8,3072]{2,1,0:T(8,128)(2,1)S(1)} %all-to-all-done), channel_id=1, source_target_pairs={{0,6},{1,3},{2,4},{3,1},{4,2},{5,7},{6,0},{7,5},{8,14},{9,11},{10,... | collective-permute-start | bytes 1179656 | tf_op jit(solution)/shard_map/ppermute | solution.py:29
  27.2 3.4 %all-to-all-start.1 = ((bf16[8,8,3072]{2,1,0:T(8,128)(2,1)}), bf16[8,8,3072]{2,1,0:T(8,128)(2,1)S(1)}, u32[]{:S(2)}, u32[]{:S(2)}) async-start(bf16[8,8,3072]{2,1,0:T(8,128)(2,1)} %get-tuple-element.26), calls=%async_computation.1 | async-start | bytes 786432 | tf_op jit(solution)/shard_map/all_to_all | solution.py:138
  31.5 3.3 %collective-permute-done = bf16[8,8,3072]{2,1,0:T(8,128)(2,1)S(1)} collective-permute-done((bf16[8,8,3072]{2,1,0:T(8,128)(2,1)S(1)}, bf16[8,8,3072]{2,1,0:T(8,128)(2,1)S(1)}, u32[]{:S(2)}, u32[]{:S(2)}) %collective-permute-start) | collective-permute-done | bytes 393248 | tf_op jit(solution)/shard_map/ppermute | solution.py:29
  34.8 1.0 collective-permute-start.2
  37.3 5.9 %all-to-all-done.1 = bf16[8,8,3072]{2,1,0:T(8,128)(2,1)S(1)} async-done(((bf16[8,8,3072]{2,1,0:T(8,128)(2,1)}), bf16[8,8,3072]{2,1,0:T(8,128)(2,1)S(1)}, u32[]{:S(2)}, u32[]{:S(2)}) %all-to-all-start.1) | async-done | bytes 393248 | tf_op jit(solution)/shard_map/all_to_all | solution.py:138
  43.7 1.0 collective-permute-start.10
  44.7 0.8 constant_dynamic-update-slice_fusion.4
  47.1 1.8 %constant_dynamic-update-slice_fusion.1 = bf16[64,8,3072]{2,1,0:T(8,128)(2,1)} fusion(bf16[64,8,3072]{2,1,0:T(8,128)(2,1)} %constant_dynamic-update-slice_fusion.2, bf16[8,8,3072]{2,1,0:T(8,128)(2,1)} %collective-permute-done.5), kind=kLoop, calls=%fused_computation.54 | loop fusion | bytes 786432
  49.7 4.5 %fusion = f32[8,4,16,768]{3,2,1,0:T(8,128)S(1)} fusion(bf16[8,4,16,3072]{3,2,1,0:T(8,128)(2,1)} %bitcast.3, bf16[3072,768]{1,0:T(8,128)(2,1)S(1)} %copy-done.1), kind=kOutput, calls=%fused_computation.1 | convolution fusion | flops 2415919104 | bytes 9437184 | tf_op jit(solution)/shard_map/dot_general | solution.py:152
  54.3 0.8 collective-permute-start.7
  55.1 1.8 %collective-permute-start.13 = (bf16[8,8,3072]{2,1,0:T(8,128)(2,1)S(1)}, bf16[8,8,3072]{2,1,0:T(8,128)(2,1)S(1)}, u32[]{:S(2)}, u32[]{:S(2)}) collective-permute-start(bf16[8,8,3072]{2,1,0:T(8,128)(2,1)S(1)} %collective-permute-done.9), channel_id=1, source_target_pairs={{0,1},{1,0},{2,3},{3,2},{4,5},{5,4},{6,7},{7,6},{8,9},{9,8},{10,11... | collective-permute-start | bytes 1179656 | tf_op jit(solution)/shard_map/ppermute | solution.py:29
  56.9 1.0 collective-permute-start.11
  58.0 4.1 %collective-permute-done.7 = bf16[2,8,16,768]{3,2,1,0:T(8,128)(2,1)S(1)} collective-permute-done((bf16[2,8,16,768]{3,2,1,0:T(8,128)(2,1)S(1)}, bf16[2,8,16,768]{3,2,1,0:T(8,128)(2,1)S(1)}, u32[]{:S(2)}, u32[]{:S(2)}) %collective-permute-start.7) | collective-permute-done | bytes 393248 | tf_op jit(solution)/shard_map/ppermute | solution.py:29
  62.6 3.2 %collective-permute-done.11 = bf16[8,8,3072]{2,1,0:T(8,128)(2,1)S(1)} collective-permute-done((bf16[8,8,3072]{2,1,0:T(8,128)(2,1)S(1)}, bf16[8,8,3072]{2,1,0:T(8,128)(2,1)S(1)}, u32[]{:S(2)}, u32[]{:S(2)}) %collective-permute-start.11) | collective-permute-done | bytes 393248 | tf_op jit(solution)/shard_map/ppermute | solution.py:29
  66.0 3.2 %collective-permute-done.8.other_ref = bf16[8,16,768]{2,1,0:T(8,128)(2,1)S(1)} collective-permute-done((bf16[8,16,768]{2,1,0:T(8,128)(2,1)S(1)}, bf16[8,16,768]{2,1,0:T(8,128)(2,1)S(1)}, u32[]{:S(2)}, u32[]{:S(2)}) %collective-permute-start.8) | collective-permute-done | bytes 196640 | tf_op jit(solution)/shard_map/ppermute | solution.py:29
  69.3 0.9 gelu.2
  70.5 2.6 %fusion.33 = f32[512,768]{1,0:T(8,128)S(1)} fusion(bf16[512,3072]{1,0:T(8,128)(2,1)S(1)} %bitcast.162, bf16[3072,768]{1,0:T(8,128)(2,1)S(1)} %copy-done.1), kind=kOutput, calls=%fused_computation.82 | convolution fusion | flops 2415919104 | bytes 9437184 | tf_op jit(solution)/shard_map/dot_general | solution.py:152
  73.3 3.9 %collective-permute-done.18.b_ref = bf16[8,16,768]{2,1,0:T(8,128)(2,1)S(1)} collective-permute-done((bf16[8,16,768]{2,1,0:T(8,128)(2,1)S(1)}, bf16[8,16,768]{2,1,0:T(8,128)(2,1)S(1)}, u32[]{:S(2)}, u32[]{:S(2)}) %collective-permute-start.18) | collective-permute-done | bytes 196640 | tf_op jit(solution)/shard_map/ppermute | solution.py:29
  77.3 2.0 %collective-permute-start.16 = (bf16[2,8,16,768]{3,2,1,0:T(8,128)(2,1)S(1)}, bf16[2,8,16,768]{3,2,1,0:T(8,128)(2,1)S(1)}, u32[]{:S(2)}, u32[]{:S(2)}) collective-permute-start(bf16[2,8,16,768]{3,2,1,0:T(8,128)(2,1)S(1)} %pad_maximum_fusion.1), channel_id=1, source_target_pairs={{0,64},{1,193},{2,66},{3,195},{4,68},{5,197},{6,70},{7,199},{8,72}... | collective-permute-start | bytes 1179656 | tf_op jit(solution)/shard_map/ppermute | solution.py:29
  79.4 5.7 %collective-permute-done.19.c_ref = bf16[2,8,16,768]{3,2,1,0:T(8,128)(2,1)S(1)} collective-permute-done((bf16[2,8,16,768]{3,2,1,0:T(8,128)(2,1)S(1)}, bf16[2,8,16,768]{3,2,1,0:T(8,128)(2,1)S(1)}, u32[]{:S(2)}, u32[]{:S(2)}) %collective-permute-start.19) | collective-permute-done | bytes 393248 | tf_op jit(solution)/shard_map/ppermute | solution.py:29
  85.7 1.4 convolution_convert_fusion.1
  87.2 2.0 %collective-permute-done.16 = bf16[2,8,16,768]{3,2,1,0:T(8,128)(2,1)S(1)} collective-permute-done((bf16[2,8,16,768]{3,2,1,0:T(8,128)(2,1)S(1)}, bf16[2,8,16,768]{3,2,1,0:T(8,128)(2,1)S(1)}, u32[]{:S(2)}, u32[]{:S(2)}) %collective-permute-start.16) | collective-permute-done | bytes 393248 | tf_op jit(solution)/shard_map/ppermute | solution.py:29
  89.4 1.4 fusion.34
  91.6 2.4 %collective-permute-start.23 = (bf16[2,64,3072]{2,1,0:T(8,128)(2,1)S(1)}, bf16[2,64,3072]{2,1,0:T(8,128)(2,1)S(1)}, u32[]{:S(2)}, u32[]{:S(2)}) collective-permute-start(bf16[2,64,3072]{2,1,0:T(8,128)(2,1)S(1)} %get-tuple-element.54), channel_id=1, source_target_pairs={{0,6},{1,3},{2,4},{3,1},{4,2},{5,7},{6,0},{7,5},{8,14},{9,11},{10,... | collective-permute-start | bytes 2359304 | tf_op jit(solution)/shard_map/ppermute | solution.py:29
  94.2 6.7 %collective-permute-done.17.other_ref = bf16[8,16,768]{2,1,0:T(8,128)(2,1)S(1)} collective-permute-done((bf16[8,16,768]{2,1,0:T(8,128)(2,1)S(1)}, bf16[8,16,768]{2,1,0:T(8,128)(2,1)S(1)}, u32[]{:S(2)}, u32[]{:S(2)}) %collective-permute-start.17) | collective-permute-done | bytes 196640 | tf_op jit(solution)/shard_map/ppermute | solution.py:29
  100.9 0.9 gelu.3
  102.1 7.9 %collective-permute-done.21.b_ref = bf16[8,16,768]{2,1,0:T(8,128)(2,1)S(1)} collective-permute-done((bf16[8,16,768]{2,1,0:T(8,128)(2,1)S(1)}, bf16[8,16,768]{2,1,0:T(8,128)(2,1)S(1)}, u32[]{:S(2)}, u32[]{:S(2)}) %collective-permute-start.21) | collective-permute-done | bytes 196640 | tf_op jit(solution)/shard_map/ppermute | solution.py:29
  110.2 7.7 %collective-permute-done.22.c_ref = bf16[2,8,16,768]{3,2,1,0:T(8,128)(2,1)S(1)} collective-permute-done((bf16[2,8,16,768]{3,2,1,0:T(8,128)(2,1)S(1)}, bf16[2,8,16,768]{3,2,1,0:T(8,128)(2,1)S(1)}, u32[]{:S(2)}, u32[]{:S(2)}) %collective-permute-start.22) | collective-permute-done | bytes 393248 | tf_op jit(solution)/shard_map/ppermute | solution.py:29
  118.5 1.4 convolution_convert_fusion
  120.2 2.4 %collective-permute-start.26 = (bf16[64,3072]{1,0:T(8,128)(2,1)S(1)}, bf16[64,3072]{1,0:T(8,128)(2,1)S(1)}, u32[]{:S(2)}, u32[]{:S(2)}) collective-permute-start(bf16[64,3072]{1,0:T(8,128)(2,1)S(1)} %fusion.11), channel_id=1, source_target_pairs={{0,2},{1,7},{2,0},{3,5},{4,6},{5,3},{6,4},{7,1},{8,10},{9,15},{10,... | collective-permute-start | bytes 1179656 | tf_op jit(solution)/shard_map/ppermute | solution.py:29
  122.6 1.4 fusion.35
  124.4 1.3 add_convert_fusion.1
  125.7 2.7 %collective-permute-done.26 = bf16[64,3072]{1,0:T(8,128)(2,1)S(1)} collective-permute-done((bf16[64,3072]{1,0:T(8,128)(2,1)S(1)}, bf16[64,3072]{1,0:T(8,128)(2,1)S(1)}, u32[]{:S(2)}, u32[]{:S(2)}) %collective-permute-start.26) | collective-permute-done | bytes 393248 | tf_op jit(solution)/shard_map/ppermute | solution.py:29
  128.4 0.9 fusion.13
  129.3 4.8 %all-to-all-start.2 = ((bf16[8,8,3072]{2,1,0:T(8,128)(2,1)}), bf16[8,8,3072]{2,1,0:T(8,128)(2,1)}, u32[]{:S(2)}, u32[]{:S(2)}) async-start(bf16[8,8,3072]{2,1,0:T(8,128)(2,1)} %fusion.13), calls=%async_computation.2 | async-start | bytes 786432 | tf_op jit(solution)/shard_map/all_to_all | solution.py:194
  134.1 5.1 %collective-permute-done.25 = bf16[2,64,3072]{2,1,0:T(8,128)(2,1)} collective-permute-done((bf16[2,64,3072]{2,1,0:T(8,128)(2,1)}, bf16[2,64,3072]{2,1,0:T(8,128)(2,1)}, u32[]{:S(2)}, u32[]{:S(2)}) %collective-permute-start.25) | collective-permute-done | bytes 786464 | tf_op jit(solution)/shard_map/ppermute | solution.py:29
  139.3 1.8 %fusion.14 = bf16[64,3072]{1,0:T(8,128)(2,1)} fusion(f32[2,64,3072]{2,1,0:T(8,128)S(1)} %get-tuple-element.52, bf16[2,64,3072]{2,1,0:T(8,128)(2,1)} %collective-permute-done.25), kind=kLoop, calls=%fused_computation.25 | loop fusion | flops 589824 | bytes 1572864 | tf_op jit(solution)/shard_map/convert_element_type | solution.py:184
  141.4 6.2 %all-to-all-done.2 = bf16[8,8,3072]{2,1,0:T(8,128)(2,1)} async-done(((bf16[8,8,3072]{2,1,0:T(8,128)(2,1)}), bf16[8,8,3072]{2,1,0:T(8,128)(2,1)}, u32[]{:S(2)}, u32[]{:S(2)}) %all-to-all-start.2) | async-done | bytes 393248 | tf_op jit(solution)/shard_map/all_to_all | solution.py:194
  147.6 1.7 reduce_sum.24
  149.3 2.0 %fusion.12 = bf16[8,8,3072]{2,1,0:T(8,128)(2,1)} fusion(bf16[64,3072]{1,0:T(8,128)(2,1)} %collective-permute-done.27, f32[2,64,3072]{2,1,0:T(8,128)S(1)} %get-tuple-element.52, bf16[2,64,3072]{2,1,0:T(8,128)(2,1)} %collective-permute-done.25), kind=kLoop, calls=%fused_computation.23 | loop fusion | flops 983040 | bytes 1966080 | tf_op jit(solution)/shard_map/reshape | solution.py:190
  151.3 4.7 %all-to-all-start.3 = ((bf16[8,8,3072]{2,1,0:T(8,128)(2,1)}), bf16[8,8,3072]{2,1,0:T(8,128)(2,1)S(1)}, u32[]{:S(2)}, u32[]{:S(2)}) async-start(bf16[8,8,3072]{2,1,0:T(8,128)(2,1)} %fusion.12), calls=%async_computation.3 | async-start | bytes 786432 | tf_op jit(solution)/shard_map/all_to_all | solution.py:194
  156.8 4.6 %fusion.27 = f32[3072,768]{1,0:T(8,128)S(1)} fusion(bf16[512,768]{1,0:T(8,128)(2,1)S(1)} %bitcast.141, bf16[64,8,3072]{2,1,0:T(8,128)(2,1)} %copy-done.3), kind=kOutput, calls=%fused_computation.76 | convolution fusion | flops 2415919104 | bytes 13369344 | tf_op jit(solution)/shard_map/dot_general | solution.py:199
  161.4 7.1 %add_convert_fusion = bf16[3072,768]{1,0:T(8,128)(2,1)} fusion(f32[3072,768]{1,0:T(8,128)S(1)} %fusion.27, bf16[512,768]{1,0:T(8,128)(2,1)S(1)} %bitcast.140, bf16[64,8,3072]{2,1,0:T(8,128)(2,1)} %constant_dynamic-update-slice_fusion), kind=kOutput, calls=%fused_computation | convolution fusion | flops 2420637696 | bytes 18087936 | tf_op jit(solution)/shard_map/dot_general | solution.py:199
  (83 shorter events, 12.7 us)
Async XLA Ops:
  0.6 0.9 copy-start
  2.4 21.8 %all-to-all-start = ((bf16[8,8,3072]{2,1,0:T(8,128)(2,1)}), bf16[8,8,3072]{2,1,0:T(8,128)(2,1)S(1)}, u32[]{:S(2)}, u32[]{:S(2)}) async-start(bf16[8,8,3072]{2,1,0:T(8,128)(2,1)} %get-tuple-element.23), calls=%async_computation | async-start | bytes 786432 | tf_op jit(solution)/shard_map/all_to_all | solution.py:138
  24.2 11.5 %collective-permute-start.1 = (bf16[8,8,3072]{2,1,0:T(8,128)(2,1)S(1)}, bf16[8,8,3072]{2,1,0:T(8,128)(2,1)S(1)}, u32[]{:S(2)}, u32[]{:S(2)}) collective-permute-start(bf16[8,8,3072]{2,1,0:T(8,128)(2,1)S(1)} %all-to-all-done), channel_id=1, source_target_pairs={{0,6},{1,3},{2,4},{3,1},{4,2},{5,7},{6,0},{7,5},{8,14},{9,11},{10,... | collective-permute-start | bytes 1179656 | tf_op jit(solution)/shard_map/ppermute | solution.py:29
  27.0 7.8 %collective-permute-start = (bf16[8,8,3072]{2,1,0:T(8,128)(2,1)S(1)}, bf16[8,8,3072]{2,1,0:T(8,128)(2,1)S(1)}, u32[]{:S(2)}, u32[]{:S(2)}) collective-permute-start(bf16[8,8,3072]{2,1,0:T(8,128)(2,1)S(1)} %all-to-all-done), channel_id=1, source_target_pairs={{0,2},{1,7},{2,0},{3,5},{4,6},{5,3},{6,4},{7,1},{8,10},{9,15},{10,... | collective-permute-start | bytes 1179656 | tf_op jit(solution)/shard_map/ppermute | solution.py:29
  27.2 15.9 %all-to-all-start.1 = ((bf16[8,8,3072]{2,1,0:T(8,128)(2,1)}), bf16[8,8,3072]{2,1,0:T(8,128)(2,1)S(1)}, u32[]{:S(2)}, u32[]{:S(2)}) async-start(bf16[8,8,3072]{2,1,0:T(8,128)(2,1)} %get-tuple-element.26), calls=%async_computation.1 | async-start | bytes 786432 | tf_op jit(solution)/shard_map/all_to_all | solution.py:138
  30.6 14.9 %collective-permute-start.3 = (bf16[8,8,3072]{2,1,0:T(8,128)(2,1)S(1)}, bf16[8,8,3072]{2,1,0:T(8,128)(2,1)S(1)}, u32[]{:S(2)}, u32[]{:S(2)}) collective-permute-start(bf16[8,8,3072]{2,1,0:T(8,128)(2,1)S(1)} %all-to-all-done), channel_id=1, source_target_pairs={{0,1},{1,0},{2,3},{3,2},{4,5},{5,4},{6,7},{7,6},{8,9},{9,8},{10,11... | collective-permute-start | bytes 1179656 | tf_op jit(solution)/shard_map/ppermute | solution.py:29
  34.8 11.5 %collective-permute-start.4 = (bf16[8,8,3072]{2,1,0:T(8,128)(2,1)S(1)}, bf16[8,8,3072]{2,1,0:T(8,128)(2,1)S(1)}, u32[]{:S(2)}, u32[]{:S(2)}) collective-permute-start(bf16[8,8,3072]{2,1,0:T(8,128)(2,1)S(1)} %collective-permute-done), channel_id=1, source_target_pairs={{0,1},{1,0},{2,3},{3,2},{4,5},{5,4},{6,7},{7,6},{8,9},{9,8},{10,11... | collective-permute-start | bytes 1179656 | tf_op jit(solution)/shard_map/ppermute | solution.py:29
  34.8 9.0 %collective-permute-start.2 = (bf16[8,8,3072]{2,1,0:T(8,128)(2,1)S(1)}, bf16[8,8,3072]{2,1,0:T(8,128)(2,1)S(1)}, u32[]{:S(2)}, u32[]{:S(2)}) collective-permute-start(bf16[8,8,3072]{2,1,0:T(8,128)(2,1)S(1)} %collective-permute-done), channel_id=1, source_target_pairs={{0,6},{1,3},{2,4},{3,1},{4,2},{5,7},{6,0},{7,5},{8,14},{9,11},{10,... | collective-permute-start | bytes 1179656 | tf_op jit(solution)/shard_map/ppermute | solution.py:29
  35.7 11.4 %collective-permute-start.5 = (bf16[8,8,3072]{2,1,0:T(8,128)(2,1)S(1)}, bf16[8,8,3072]{2,1,0:T(8,128)(2,1)}, u32[]{:S(2)}, u32[]{:S(2)}) collective-permute-start(bf16[8,8,3072]{2,1,0:T(8,128)(2,1)S(1)} %collective-permute-done.1), channel_id=1, source_target_pairs={{0,1},{1,0},{2,3},{3,2},{4,5},{5,4},{6,7},{7,6},{8,9},{9,8},{10,11... | collective-permute-start | bytes 1179656 | tf_op jit(solution)/shard_map/ppermute | solution.py:29
  43.2 6.5 %copy-start.1 = (bf16[3072,768]{1,0:T(8,128)(2,1)S(1)}, bf16[3072,768]{1,0:T(8,128)(2,1)}, u32[]{:S(2)}) copy-start(bf16[3072,768]{1,0:T(8,128)(2,1)} %param.4) | copy-start | bytes 14155780
  43.2 22.7 %collective-permute-start.12 = (bf16[8,8,3072]{2,1,0:T(8,128)(2,1)S(1)}, bf16[8,8,3072]{2,1,0:T(8,128)(2,1)S(1)}, u32[]{:S(2)}, u32[]{:S(2)}) collective-permute-start(bf16[8,8,3072]{2,1,0:T(8,128)(2,1)S(1)} %all-to-all-done.1), channel_id=1, source_target_pairs={{0,1},{1,0},{2,3},{3,2},{4,5},{5,4},{6,7},{7,6},{8,9},{9,8},{10,11... | collective-permute-start | bytes 1179656 | tf_op jit(solution)/shard_map/ppermute | solution.py:29
  43.7 14.2 %collective-permute-start.10 = (bf16[8,8,3072]{2,1,0:T(8,128)(2,1)S(1)}, bf16[8,8,3072]{2,1,0:T(8,128)(2,1)S(1)}, u32[]{:S(2)}, u32[]{:S(2)}) collective-permute-start(bf16[8,8,3072]{2,1,0:T(8,128)(2,1)S(1)} %all-to-all-done.1), channel_id=1, source_target_pairs={{0,6},{1,3},{2,4},{3,1},{4,2},{5,7},{6,0},{7,5},{8,14},{9,11},{10,... | collective-permute-start | bytes 1179656 | tf_op jit(solution)/shard_map/ppermute | solution.py:29
  45.5 9.6 %collective-permute-start.9 = (bf16[8,8,3072]{2,1,0:T(8,128)(2,1)S(1)}, bf16[8,8,3072]{2,1,0:T(8,128)(2,1)S(1)}, u32[]{:S(2)}, u32[]{:S(2)}) collective-permute-start(bf16[8,8,3072]{2,1,0:T(8,128)(2,1)S(1)} %all-to-all-done.1), channel_id=1, source_target_pairs={{0,2},{1,7},{2,0},{3,5},{4,6},{5,3},{6,4},{7,1},{8,10},{9,15},{10,... | collective-permute-start | bytes 1179656 | tf_op jit(solution)/shard_map/ppermute | solution.py:29
  46.3 2.6 %collective-permute-start.6 = (bf16[8,8,3072]{2,1,0:T(8,128)(2,1)S(1)}, bf16[8,8,3072]{2,1,0:T(8,128)(2,1)S(1)}, u32[]{:S(2)}, u32[]{:S(2)}) collective-permute-start(bf16[8,8,3072]{2,1,0:T(8,128)(2,1)S(1)} %collective-permute-done.2), channel_id=1, source_target_pairs={{0,1},{1,0},{2,3},{3,2},{4,5},{5,4},{6,7},{7,6},{8,9},{9,8},{10,11... | collective-permute-start | bytes 1179656 | tf_op jit(solution)/shard_map/ppermute | solution.py:29
  54.3 7.9 %collective-permute-start.7 = (bf16[2,8,16,768]{3,2,1,0:T(8,128)(2,1)S(1)}, bf16[2,8,16,768]{3,2,1,0:T(8,128)(2,1)S(1)}, u32[]{:S(2)}, u32[]{:S(2)}) collective-permute-start(bf16[2,8,16,768]{3,2,1,0:T(8,128)(2,1)S(1)} %pad_maximum_fusion), channel_id=1, source_target_pairs={{0,64},{1,193},{2,66},{3,195},{4,68},{5,197},{6,70},{7,199},{8,72}... | collective-permute-start | bytes 1179656 | tf_op jit(solution)/shard_map/ppermute | solution.py:29
  55.1 10.9 %collective-permute-start.13 = (bf16[8,8,3072]{2,1,0:T(8,128)(2,1)S(1)}, bf16[8,8,3072]{2,1,0:T(8,128)(2,1)S(1)}, u32[]{:S(2)}, u32[]{:S(2)}) collective-permute-start(bf16[8,8,3072]{2,1,0:T(8,128)(2,1)S(1)} %collective-permute-done.9), channel_id=1, source_target_pairs={{0,1},{1,0},{2,3},{3,2},{4,5},{5,4},{6,7},{7,6},{8,9},{9,8},{10,11... | collective-permute-start | bytes 1179656 | tf_op jit(solution)/shard_map/ppermute | solution.py:29
  56.9 9.0 %collective-permute-start.11 = (bf16[8,8,3072]{2,1,0:T(8,128)(2,1)S(1)}, bf16[8,8,3072]{2,1,0:T(8,128)(2,1)S(1)}, u32[]{:S(2)}, u32[]{:S(2)}) collective-permute-start(bf16[8,8,3072]{2,1,0:T(8,128)(2,1)S(1)} %collective-permute-done.9), channel_id=1, source_target_pairs={{0,6},{1,3},{2,4},{3,1},{4,2},{5,7},{6,0},{7,5},{8,14},{9,11},{10,... | collective-permute-start | bytes 1179656 | tf_op jit(solution)/shard_map/ppermute | solution.py:29
  57.9 8.1 %collective-permute-start.14 = (bf16[8,8,3072]{2,1,0:T(8,128)(2,1)S(1)}, bf16[8,8,3072]{2,1,0:T(8,128)(2,1)S(1)}, u32[]{:S(2)}, u32[]{:S(2)}) collective-permute-start(bf16[8,8,3072]{2,1,0:T(8,128)(2,1)S(1)} %collective-permute-done.10), channel_id=1, source_target_pairs={{0,1},{1,0},{2,3},{3,2},{4,5},{5,4},{6,7},{7,6},{8,9},{9,8},{10,11... | collective-permute-start | bytes 1179656 | tf_op jit(solution)/shard_map/ppermute | solution.py:29
  62.3 7.0 %collective-permute-start.8 = (bf16[8,16,768]{2,1,0:T(8,128)(2,1)S(1)}, bf16[8,16,768]{2,1,0:T(8,128)(2,1)S(1)}, u32[]{:S(2)}, u32[]{:S(2)}) collective-permute-start(bf16[8,16,768]{2,1,0:T(8,128)(2,1)S(1)} %get-tuple-element.48), channel_id=1, source_target_pairs={{0,192},{1,65},{2,194},{3,67},{4,196},{5,69},{6,198},{7,71},{8,200... | collective-permute-start | bytes 589832 | tf_op jit(solution)/shard_map/ppermute | solution.py:29
  65.9 4.6 %collective-permute-start.15 = (bf16[8,8,3072]{2,1,0:T(8,128)(2,1)S(1)}, bf16[8,8,3072]{2,1,0:T(8,128)(2,1)S(1)}, u32[]{:S(2)}, u32[]{:S(2)}) collective-permute-start(bf16[8,8,3072]{2,1,0:T(8,128)(2,1)S(1)} %collective-permute-done.11), channel_id=1, source_target_pairs={{0,1},{1,0},{2,3},{3,2},{4,5},{5,4},{6,7},{7,6},{8,9},{9,8},{10,11... | collective-permute-start | bytes 1179656 | tf_op jit(solution)/shard_map/ppermute | solution.py:29
  70.2 7.0 %collective-permute-start.18 = (bf16[8,16,768]{2,1,0:T(8,128)(2,1)S(1)}, bf16[8,16,768]{2,1,0:T(8,128)(2,1)S(1)}, u32[]{:S(2)}, u32[]{:S(2)}) collective-permute-start(bf16[8,16,768]{2,1,0:T(8,128)(2,1)S(1)} %get-tuple-element.29.a_ref), channel_id=1, source_target_pairs={{0,192},{1,65},{2,194},{3,67},{4,196},{5,69},{6,198},{7,71},{8,200... | collective-permute-start | bytes 589832 | tf_op jit(solution)/shard_map/ppermute | solution.py:29
  70.5 2.6 %copy-start.3 = (bf16[64,8,3072]{2,1,0:T(8,128)(2,1)}, bf16[64,8,3072]{2,1,0:T(8,128)(2,1)S(1)}, u32[]{:S(2)}) copy-start(bf16[64,8,3072]{2,1,0:T(8,128)(2,1)S(1)} %constant_dynamic-update-slice_fusion.8) | copy-start | bytes 9437188
  77.2 7.9 %collective-permute-start.19 = (bf16[2,8,16,768]{3,2,1,0:T(8,128)(2,1)S(1)}, bf16[2,8,16,768]{3,2,1,0:T(8,128)(2,1)S(1)}, u32[]{:S(2)}, u32[]{:S(2)}) collective-permute-start(bf16[2,8,16,768]{3,2,1,0:T(8,128)(2,1)S(1)} %pad_maximum_fusion.2), channel_id=1, source_target_pairs={{0,64},{1,193},{2,66},{3,195},{4,68},{5,197},{6,70},{7,199},{8,72}... | collective-permute-start | bytes 1179656 | tf_op jit(solution)/shard_map/ppermute | solution.py:29
  77.3 11.9 %collective-permute-start.16 = (bf16[2,8,16,768]{3,2,1,0:T(8,128)(2,1)S(1)}, bf16[2,8,16,768]{3,2,1,0:T(8,128)(2,1)S(1)}, u32[]{:S(2)}, u32[]{:S(2)}) collective-permute-start(bf16[2,8,16,768]{3,2,1,0:T(8,128)(2,1)S(1)} %pad_maximum_fusion.1), channel_id=1, source_target_pairs={{0,64},{1,193},{2,66},{3,195},{4,68},{5,197},{6,70},{7,199},{8,72}... | collective-permute-start | bytes 1179656 | tf_op jit(solution)/shard_map/ppermute | solution.py:29
  87.1 4.1 %collective-permute-start.20 = (bf16[4,64,3072]{2,1,0:T(8,128)(2,1)S(1)}, bf16[4,64,3072]{2,1,0:T(8,128)(2,1)S(1)}, u32[]{:S(2)}, u32[]{:S(2)}) collective-permute-start(bf16[4,64,3072]{2,1,0:T(8,128)(2,1)S(1)} %bitcast.163), channel_id=1, source_target_pairs={{0,1},{1,0},{2,3},{3,2},{4,5},{5,4},{6,7},{7,6},{8,9},{9,8},{10,11... | collective-permute-start | bytes 4718600 | tf_op jit(solution)/shard_map/ppermute | solution.py:29
  91.6 18.4 %collective-permute-start.23 = (bf16[2,64,3072]{2,1,0:T(8,128)(2,1)S(1)}, bf16[2,64,3072]{2,1,0:T(8,128)(2,1)S(1)}, u32[]{:S(2)}, u32[]{:S(2)}) collective-permute-start(bf16[2,64,3072]{2,1,0:T(8,128)(2,1)S(1)} %get-tuple-element.54), channel_id=1, source_target_pairs={{0,6},{1,3},{2,4},{3,1},{4,2},{5,7},{6,0},{7,5},{8,14},{9,11},{10,... | collective-permute-start | bytes 2359304 | tf_op jit(solution)/shard_map/ppermute | solution.py:29
  94.0 6.9 %collective-permute-start.17 = (bf16[8,16,768]{2,1,0:T(8,128)(2,1)S(1)}, bf16[8,16,768]{2,1,0:T(8,128)(2,1)S(1)}, u32[]{:S(2)}, u32[]{:S(2)}) collective-permute-start(bf16[8,16,768]{2,1,0:T(8,128)(2,1)S(1)} %get-tuple-element.49), channel_id=1, source_target_pairs={{0,192},{1,65},{2,194},{3,67},{4,196},{5,69},{6,198},{7,71},{8,200... | collective-permute-start | bytes 589832 | tf_op jit(solution)/shard_map/ppermute | solution.py:29
  101.8 8.2 %collective-permute-start.21 = (bf16[8,16,768]{2,1,0:T(8,128)(2,1)S(1)}, bf16[8,16,768]{2,1,0:T(8,128)(2,1)S(1)}, u32[]{:S(2)}, u32[]{:S(2)}) collective-permute-start(bf16[8,16,768]{2,1,0:T(8,128)(2,1)S(1)} %get-tuple-element.33.a_ref), channel_id=1, source_target_pairs={{0,192},{1,65},{2,194},{3,67},{4,196},{5,69},{6,198},{7,71},{8,200... | collective-permute-start | bytes 589832 | tf_op jit(solution)/shard_map/ppermute | solution.py:29
  110.0 7.9 %collective-permute-start.22 = (bf16[2,8,16,768]{3,2,1,0:T(8,128)(2,1)S(1)}, bf16[2,8,16,768]{3,2,1,0:T(8,128)(2,1)S(1)}, u32[]{:S(2)}, u32[]{:S(2)}) collective-permute-start(bf16[2,8,16,768]{3,2,1,0:T(8,128)(2,1)S(1)} %pad_maximum_fusion.3), channel_id=1, source_target_pairs={{0,64},{1,193},{2,66},{3,195},{4,68},{5,197},{6,70},{7,199},{8,72}... | collective-permute-start | bytes 1179656 | tf_op jit(solution)/shard_map/ppermute | solution.py:29
  119.9 4.5 %collective-permute-start.24 = (bf16[4,64,3072]{2,1,0:T(8,128)(2,1)S(1)}, bf16[4,64,3072]{2,1,0:T(8,128)(2,1)S(1)}, u32[]{:S(2)}, u32[]{:S(2)}) collective-permute-start(bf16[4,64,3072]{2,1,0:T(8,128)(2,1)S(1)} %bitcast.164), channel_id=1, source_target_pairs={{0,1},{1,0},{2,3},{3,2},{4,5},{5,4},{6,7},{7,6},{8,9},{9,8},{10,11... | collective-permute-start | bytes 4718600 | tf_op jit(solution)/shard_map/ppermute | solution.py:29
  120.2 8.2 %collective-permute-start.26 = (bf16[64,3072]{1,0:T(8,128)(2,1)S(1)}, bf16[64,3072]{1,0:T(8,128)(2,1)S(1)}, u32[]{:S(2)}, u32[]{:S(2)}) collective-permute-start(bf16[64,3072]{1,0:T(8,128)(2,1)S(1)} %fusion.11), channel_id=1, source_target_pairs={{0,2},{1,7},{2,0},{3,5},{4,6},{5,3},{6,4},{7,1},{8,10},{9,15},{10,... | collective-permute-start | bytes 1179656 | tf_op jit(solution)/shard_map/ppermute | solution.py:29
  125.7 13.5 %collective-permute-start.25 = (bf16[2,64,3072]{2,1,0:T(8,128)(2,1)}, bf16[2,64,3072]{2,1,0:T(8,128)(2,1)}, u32[]{:S(2)}, u32[]{:S(2)}) collective-permute-start(bf16[2,64,3072]{2,1,0:T(8,128)(2,1)} %get-tuple-element.51), channel_id=1, source_target_pairs={{0,6},{1,3},{2,4},{3,1},{4,2},{5,7},{6,0},{7,5},{8,14},{9,11},{10,... | collective-permute-start | bytes 2359304 | tf_op jit(solution)/shard_map/ppermute | solution.py:29
  129.3 18.3 %all-to-all-start.2 = ((bf16[8,8,3072]{2,1,0:T(8,128)(2,1)}), bf16[8,8,3072]{2,1,0:T(8,128)(2,1)}, u32[]{:S(2)}, u32[]{:S(2)}) async-start(bf16[8,8,3072]{2,1,0:T(8,128)(2,1)} %fusion.13), calls=%async_computation.2 | async-start | bytes 786432 | tf_op jit(solution)/shard_map/all_to_all | solution.py:194
  141.1 8.2 %collective-permute-start.27 = (bf16[64,3072]{1,0:T(8,128)(2,1)}, bf16[64,3072]{1,0:T(8,128)(2,1)}, u32[]{:S(2)}, u32[]{:S(2)}) collective-permute-start(bf16[64,3072]{1,0:T(8,128)(2,1)} %fusion.14), channel_id=1, source_target_pairs={{0,2},{1,7},{2,0},{3,5},{4,6},{5,3},{6,4},{7,1},{8,10},{9,15},{10,... | collective-permute-start | bytes 1179656 | tf_op jit(solution)/shard_map/ppermute | solution.py:29
  151.3 17.2 %all-to-all-start.3 = ((bf16[8,8,3072]{2,1,0:T(8,128)(2,1)}), bf16[8,8,3072]{2,1,0:T(8,128)(2,1)S(1)}, u32[]{:S(2)}, u32[]{:S(2)}) async-start(bf16[8,8,3072]{2,1,0:T(8,128)(2,1)} %fusion.12), calls=%async_computation.3 | async-start | bytes 786432 | tf_op jit(solution)/shard_map/all_to_all | solution.py:194
  161.4 7.2 %copy-start.2 = (bf16[8,3072]{1,0:T(8,128)(2,1)S(1)}, bf16[8,3072]{1,0:T(8,128)(2,1)}, u32[]{:S(2)}) copy-start(bf16[8,3072]{1,0:T(8,128)(2,1)} %reduce_sum.24) | copy-start | bytes 147460

commit v5 on v4

--- a/solution.py
+++ b/solution.py
@@ -128,8 +128,8 @@
     far = jnp.where(core == 0, 3, 1)
     pick = lambda a, i: lax.dynamic_index_in_dim(a, i, 1, keepdims=False)
 
-    steps = jnp.stack([jnp.int32(0), near, far, jnp.int32(2), jnp.int32(0), far, near, jnp.int32(2)]).astype(jnp.int32)
-    place = ((x ^ steps) * 2 + (core ^ (jnp.arange(8, dtype=jnp.int32) // 4))).astype(jnp.int32)
+    steps = jnp.stack([jnp.int32(0), near, far, jnp.int32(2)]).astype(jnp.int32)
+    place = ((x ^ steps)[None] * 2 + (core ^ jnp.arange(2, dtype=jnp.int32))[:, None]).reshape(8).astype(jnp.int32)
     order = jnp.stack([y, y ^ far, y ^ near, y ^ 2]).astype(jnp.int32)
     cotangents = jnp.transpose(out_grad.reshape(2, 8, CHUNKS, t, f), (2, 1, 0, 3, 4)).reshape(CHUNKS, 8, 2 * t, f)
 
@@ -144,7 +144,7 @@
         c.three = permute(c.one, x_second)
 
     def assemble(c):
-        c.other = [permute(p, swap_core) for p in (c.own, c.one, c.two, c.three)]
+        c.other = [permute(p, swap_core) for p in (c.own, c.two, c.one, c.three)]
         c.tokens = jnp.concatenate([c.own, c.one, c.two, c.three] + c.other, 0).reshape(64 * t, d)
 
     def project(c, *wait):
@@ -174,10 +174,10 @@
     def back(c, *wait):
         dims = (((1,), (1,)), ((), ()))
         give = lax.dot_general(c.grad_all[1], weight, dims, preferred_element_type=F32).astype(BF)
-        keep = lax.dot_general(after(c.grad_all[0], *wait), weight, dims, preferred_element_type=F32).reshape(4, 8 * t, d)
+        keep = lax.dot_general(c.grad_all[0], weight, dims, preferred_element_type=F32).reshape(4, 8 * t, d)
         got = permute(give.reshape(4, 8 * t, d), swap_core)
-        c.away = (keep[2:] + got[2:].astype(F32)).astype(BF)
-        c.here = keep[:2] + got[:2].astype(F32)
+        c.away = (keep[2:] + jnp.stack([got[1], got[3]]).astype(F32)).astype(BF)
+        c.here = keep[:2] + jnp.stack([got[0], got[2]]).astype(F32)
 
     def reduce_first(c, wait=(), behind=()):
         got = after(permute(after(c.away, *wait), x_second), *behind)
@@ -215,7 +215,7 @@
     sum_first(b)
     spread_second(a, wait=(b.send,))
     sum_second(b)
-    back(a, b.theirs)
+    back(a)
     gelu(b, cotangents[1], a.away)
     spread_first(b)
     reduce_first(a, behind=(b.grad,))

time: 170 us -> 167 us (0.982)
  waiting for transfers between devices: 80.2 us -> 71.3 us
  starting transfers between devices: 39.1 us -> 42.3 us
    ppermute x28, waiting for transfers between devices: 56 us -> 46.7 us  [permute(): return lax.ppermute(array, AXES, pairs)]
    ppermute x28, starting transfers between devices: 17.6 us -> 20 us  [permute(): return lax.ppermute(array, AXES, pairs)]
    add x2 -> x3, other arithmetic: 0.42 us -> 2.69 us  [the longest x2 2.62 us: back(): c.here = keep[:2] + jnp.stack([got[0], got[2]]).astype(F32)]
    unnamed x22 -> x20, local copies, waits for them, and re-layouts: 7.58 us -> 7.54 us
  transfers between devices with their start and end apart: 32 -> 32, of which waited for: 16 -> 15; matrix products, arithmetic and copies ran while one was open for 23% -> 25% of each run, Pallas kernels for 1% -> 1%
where the time goes in v5:
time: 167 us; the launch traced here: 166 us
  waiting for transfers between devices  71.3 us (43%)
  starting transfers between devices  42.3 us (25%)
  matrix products  24.4 us (15%)
  local copies, waits for them, and re-layouts  12 us (7%)
  other arithmetic  10.8 us (6%)
  Pallas kernels  3.84 us (2%)
    ppermute x28, waiting for transfers between devices, permute(): return lax.ppermute(array, AXES, pairs)  46.7 us
    ppermute x28, starting transfers between devices, permute(): return lax.ppermute(array, AXES, pairs)  20 us
    all_to_all x2, waiting for transfers between devices, spread(): c.own = lax.all_to_all(copies, Z, 0, 0, tiled=True)  18.1 us
    all_to_all x2, starting transfers between devices, spread(): c.own = lax.all_to_all(copies, Z, 0, 0, tiled=True)  12 us
    dot_general x2, matrix products, weights(): lax.dot_general(c.tokens, grads, (((0,), (0,)), ((), ())), preferred_elem...  11.7 us
    all_to_all x2, starting transfers between devices, reduce_last(): c.blocks = lax.all_to_all(total, Z, 0, 0, tiled=True)  10.3 us
    unnamed x20, local copies, waits for them, and re-layouts  7.54 us
    dot_general x2, matrix products, project(): jnp.dot(tokens, weight, preferred_element_type=F32).reshape(8, 4, 2 * t, f)  7.11 us
  transfers between devices with their start and end apart: 32, of which 15 were waited for; matrix products, arithmetic and copies ran while one was open for 25% of the time, Pallas kernels for 1%

profile of v5, /device:TPU:56, one launch (start us, length us, event | category | flops | bytes accessed | tf_op | source)
XLA Modules:
  0.0 165.8 jit_solution(5294874655581033134)
XLA Ops:
  0.6 0.9 copy-done
  1.5 0.9 copies.1
  2.4 8.6 %all-to-all-start = ((bf16[8,8,3072]{2,1,0:T(8,128)(2,1)}), bf16[8,8,3072]{2,1,0:T(8,128)(2,1)S(1)}, u32[]{:S(2)}, u32[]{:S(2)}) async-start(bf16[8,8,3072]{2,1,0:T(8,128)(2,1)} %get-tuple-element.22), calls=%async_computation | async-start | bytes 786432 | tf_op jit(solution)/shard_map/all_to_all | solution.py:138
  11.0 1.0 copy.22
  12.1 12.1 %all-to-all-done = bf16[8,8,3072]{2,1,0:T(8,128)(2,1)S(1)} async-done(((bf16[8,8,3072]{2,1,0:T(8,128)(2,1)}), bf16[8,8,3072]{2,1,0:T(8,128)(2,1)S(1)}, u32[]{:S(2)}, u32[]{:S(2)}) %all-to-all-start) | async-done | bytes 393248 | tf_op jit(solution)/shard_map/all_to_all | solution.py:138
  24.2 2.8 %collective-permute-start.1 = (bf16[8,8,3072]{2,1,0:T(8,128)(2,1)S(1)}, bf16[8,8,3072]{2,1,0:T(8,128)(2,1)S(1)}, u32[]{:S(2)}, u32[]{:S(2)}) collective-permute-start(bf16[8,8,3072]{2,1,0:T(8,128)(2,1)S(1)} %all-to-all-done), channel_id=1, source_target_pairs={{0,6},{1,3},{2,4},{3,1},{4,2},{5,7},{6,0},{7,5},{8,14},{9,11},{10,... | collective-permute-start | bytes 1179656 | tf_op jit(solution)/shard_map/ppermute | solution.py:29
  27.4 3.4 %all-to-all-start.1 = ((bf16[8,8,3072]{2,1,0:T(8,128)(2,1)}), bf16[8,8,3072]{2,1,0:T(8,128)(2,1)S(1)}, u32[]{:S(2)}, u32[]{:S(2)}) async-start(bf16[8,8,3072]{2,1,0:T(8,128)(2,1)} %get-tuple-element.25), calls=%async_computation.1 | async-start | bytes 786432 | tf_op jit(solution)/shard_map/all_to_all | solution.py:138
  31.6 3.1 %collective-permute-done = bf16[8,8,3072]{2,1,0:T(8,128)(2,1)S(1)} collective-permute-done((bf16[8,8,3072]{2,1,0:T(8,128)(2,1)S(1)}, bf16[8,8,3072]{2,1,0:T(8,128)(2,1)S(1)}, u32[]{:S(2)}, u32[]{:S(2)}) %collective-permute-start) | collective-permute-done | bytes 393248 | tf_op jit(solution)/shard_map/ppermute | solution.py:29
  34.8 1.0 collective-permute-start.2
  37.3 6.0 %all-to-all-done.1 = bf16[8,8,3072]{2,1,0:T(8,128)(2,1)S(1)} async-done(((bf16[8,8,3072]{2,1,0:T(8,128)(2,1)}), bf16[8,8,3072]{2,1,0:T(8,128)(2,1)S(1)}, u32[]{:S(2)}, u32[]{:S(2)}) %all-to-all-start.1) | async-done | bytes 393248 | tf_op jit(solution)/shard_map/all_to_all | solution.py:138
  43.7 1.0 collective-permute-start.10
  46.4 1.8 %constant_dynamic-update-slice_fusion.2 = bf16[64,8,3072]{2,1,0:T(8,128)(2,1)} fusion(bf16[64,8,3072]{2,1,0:T(8,128)(2,1)} %constant_dynamic-update-slice_fusion.3, bf16[8,8,3072]{2,1,0:T(8,128)(2,1)} %collective-permute-done.4), kind=kLoop, calls=%fused_computation.55 | loop fusion | bytes 786432
  49.7 4.5 %fusion = f32[8,4,16,768]{3,2,1,0:T(8,128)S(1)} fusion(bf16[8,4,16,3072]{3,2,1,0:T(8,128)(2,1)} %bitcast.3, bf16[3072,768]{1,0:T(8,128)(2,1)S(1)} %copy-done.1), kind=kOutput, calls=%fused_computation.1 | convolution fusion | flops 2415919104 | bytes 9437184 | tf_op jit(solution)/shard_map/dot_general | solution.py:152
  54.3 0.8 collective-permute-start.7
  55.2 1.8 %collective-permute-start.14 = (bf16[8,8,3072]{2,1,0:T(8,128)(2,1)S(1)}, bf16[8,8,3072]{2,1,0:T(8,128)(2,1)S(1)}, u32[]{:S(2)}, u32[]{:S(2)}) collective-permute-start(bf16[8,8,3072]{2,1,0:T(8,128)(2,1)S(1)} %collective-permute-done.9), channel_id=1, source_target_pairs={{0,1},{1,0},{2,3},{3,2},{4,5},{5,4},{6,7},{7,6},{8,9},{9,8},{10,11... | collective-permute-start | bytes 1179656 | tf_op jit(solution)/shard_map/ppermute | solution.py:29
  57.9 4.3 %collective-permute-done.7 = bf16[2,8,16,768]{3,2,1,0:T(8,128)(2,1)S(1)} collective-permute-done((bf16[2,8,16,768]{3,2,1,0:T(8,128)(2,1)S(1)}, bf16[2,8,16,768]{3,2,1,0:T(8,128)(2,1)S(1)}, u32[]{:S(2)}, u32[]{:S(2)}) %collective-permute-start.7) | collective-permute-done | bytes 393248 | tf_op jit(solution)/shard_map/ppermute | solution.py:29
  62.7 3.3 %collective-permute-done.11 = bf16[8,8,3072]{2,1,0:T(8,128)(2,1)S(1)} collective-permute-done((bf16[8,8,3072]{2,1,0:T(8,128)(2,1)S(1)}, bf16[8,8,3072]{2,1,0:T(8,128)(2,1)S(1)}, u32[]{:S(2)}, u32[]{:S(2)}) %collective-permute-start.11) | collective-permute-done | bytes 393248 | tf_op jit(solution)/shard_map/ppermute | solution.py:29
  66.2 3.2 %collective-permute-done.8.other_ref = bf16[8,16,768]{2,1,0:T(8,128)(2,1)S(1)} collective-permute-done((bf16[8,16,768]{2,1,0:T(8,128)(2,1)S(1)}, bf16[8,16,768]{2,1,0:T(8,128)(2,1)S(1)}, u32[]{:S(2)}, u32[]{:S(2)}) %collective-permute-start.8) | collective-permute-done | bytes 196640 | tf_op jit(solution)/shard_map/ppermute | solution.py:29
  69.4 0.9 gelu.2
  70.6 2.6 %fusion.34 = f32[512,768]{1,0:T(8,128)S(1)} fusion(bf16[512,3072]{1,0:T(8,128)(2,1)S(1)} %bitcast.162, bf16[3072,768]{1,0:T(8,128)(2,1)S(1)} %copy-done.1), kind=kOutput, calls=%fused_computation.82 | convolution fusion | flops 2415919104 | bytes 9437184 | tf_op jit(solution)/shard_map/dot_general | solution.py:152
  73.3 3.9 %collective-permute-done.18.b_ref = bf16[8,16,768]{2,1,0:T(8,128)(2,1)S(1)} collective-permute-done((bf16[8,16,768]{2,1,0:T(8,128)(2,1)S(1)}, bf16[8,16,768]{2,1,0:T(8,128)(2,1)S(1)}, u32[]{:S(2)}, u32[]{:S(2)}) %collective-permute-start.18) | collective-permute-done | bytes 196640 | tf_op jit(solution)/shard_map/ppermute | solution.py:29
  77.4 2.0 %collective-permute-start.16 = (bf16[2,8,16,768]{3,2,1,0:T(8,128)(2,1)S(1)}, bf16[2,8,16,768]{3,2,1,0:T(8,128)(2,1)S(1)}, u32[]{:S(2)}, u32[]{:S(2)}) collective-permute-start(bf16[2,8,16,768]{3,2,1,0:T(8,128)(2,1)S(1)} %pad_maximum_fusion.1), channel_id=1, source_target_pairs={{0,64},{1,193},{2,66},{3,195},{4,68},{5,197},{6,70},{7,199},{8,72}... | collective-permute-start | bytes 1179656 | tf_op jit(solution)/shard_map/ppermute | solution.py:29
  79.5 5.7 %collective-permute-done.19.c_ref = bf16[2,8,16,768]{3,2,1,0:T(8,128)(2,1)S(1)} collective-permute-done((bf16[2,8,16,768]{3,2,1,0:T(8,128)(2,1)S(1)}, bf16[2,8,16,768]{3,2,1,0:T(8,128)(2,1)S(1)}, u32[]{:S(2)}, u32[]{:S(2)}) %collective-permute-start.19) | collective-permute-done | bytes 393248 | tf_op jit(solution)/shard_map/ppermute | solution.py:29
  85.8 1.4 convolution_convert_fusion.1
  87.3 2.0 %collective-permute-done.16 = bf16[2,8,16,768]{3,2,1,0:T(8,128)(2,1)S(1)} collective-permute-done((bf16[2,8,16,768]{3,2,1,0:T(8,128)(2,1)S(1)}, bf16[2,8,16,768]{3,2,1,0:T(8,128)(2,1)S(1)}, u32[]{:S(2)}, u32[]{:S(2)}) %collective-permute-start.16) | collective-permute-done | bytes 393248 | tf_op jit(solution)/shard_map/ppermute | solution.py:29
  89.8 1.4 fusion.35
  91.8 2.2 %collective-permute-start.23 = (bf16[2,64,3072]{2,1,0:T(8,128)(2,1)S(1)}, bf16[2,64,3072]{2,1,0:T(8,128)(2,1)S(1)}, u32[]{:S(2)}, u32[]{:S(2)}) collective-permute-start(bf16[2,64,3072]{2,1,0:T(8,128)(2,1)S(1)} %add_convert_fusion.2), channel_id=1, source_target_pairs={{0,6},{1,3},{2,4},{3,1},{4,2},{5,7},{6,0},{7,5},{8,14},{9,11},{10,... | collective-permute-start | bytes 2359304 | tf_op jit(solution)/shard_map/ppermute | solution.py:29
  94.0 2.4 %collective-permute-done.17.other_ref = bf16[8,16,768]{2,1,0:T(8,128)(2,1)S(1)} collective-permute-done((bf16[8,16,768]{2,1,0:T(8,128)(2,1)S(1)}, bf16[8,16,768]{2,1,0:T(8,128)(2,1)S(1)}, u32[]{:S(2)}, u32[]{:S(2)}) %collective-permute-start.17) | collective-permute-done | bytes 196640 | tf_op jit(solution)/shard_map/ppermute | solution.py:29
  96.5 0.9 gelu.3
  98.2 7.9 %collective-permute-done.21.b_ref = bf16[8,16,768]{2,1,0:T(8,128)(2,1)S(1)} collective-permute-done((bf16[8,16,768]{2,1,0:T(8,128)(2,1)S(1)}, bf16[8,16,768]{2,1,0:T(8,128)(2,1)S(1)}, u32[]{:S(2)}, u32[]{:S(2)}) %collective-permute-start.21) | collective-permute-done | bytes 196640 | tf_op jit(solution)/shard_map/ppermute | solution.py:29
  106.3 7.7 %collective-permute-done.22.c_ref = bf16[2,8,16,768]{3,2,1,0:T(8,128)(2,1)S(1)} collective-permute-done((bf16[2,8,16,768]{3,2,1,0:T(8,128)(2,1)S(1)}, bf16[2,8,16,768]{3,2,1,0:T(8,128)(2,1)S(1)}, u32[]{:S(2)}, u32[]{:S(2)}) %collective-permute-start.22) | collective-permute-done | bytes 393248 | tf_op jit(solution)/shard_map/ppermute | solution.py:29
  114.7 1.4 convolution_convert_fusion
  116.4 2.2 %collective-permute-start.26 = (bf16[64,3072]{1,0:T(8,128)(2,1)S(1)}, bf16[64,3072]{1,0:T(8,128)(2,1)S(1)}, u32[]{:S(2)}, u32[]{:S(2)}) collective-permute-start(bf16[64,3072]{1,0:T(8,128)(2,1)S(1)} %fusion.11), channel_id=1, source_target_pairs={{0,2},{1,7},{2,0},{3,5},{4,6},{5,3},{6,4},{7,1},{8,10},{9,15},{10,... | collective-permute-start | bytes 1179656 | tf_op jit(solution)/shard_map/ppermute | solution.py:29
  118.6 1.4 fusion.36
  120.3 1.0 fusion.30
  121.3 1.1 add_convert_fusion.1
  122.4 2.3 %collective-permute-start.25 = (bf16[2,64,3072]{2,1,0:T(8,128)(2,1)}, bf16[2,64,3072]{2,1,0:T(8,128)(2,1)}, u32[]{:S(2)}, u32[]{:S(2)}) collective-permute-start(bf16[2,64,3072]{2,1,0:T(8,128)(2,1)} %add_convert_fusion.1), channel_id=1, source_target_pairs={{0,6},{1,3},{2,4},{3,1},{4,2},{5,7},{6,0},{7,5},{8,14},{9,11},{10,... | collective-permute-start | bytes 2359304 | tf_op jit(solution)/shard_map/ppermute | solution.py:29
  124.6 0.9 fusion.13
  125.5 5.2 %all-to-all-start.2 = ((bf16[8,8,3072]{2,1,0:T(8,128)(2,1)}), bf16[8,8,3072]{2,1,0:T(8,128)(2,1)}, u32[]{:S(2)}, u32[]{:S(2)}) async-start(bf16[8,8,3072]{2,1,0:T(8,128)(2,1)} %fusion.13), calls=%async_computation.2 | async-start | bytes 786432 | tf_op jit(solution)/shard_map/all_to_all | solution.py:194
  130.7 2.4 %convert_add_fusion = f32[2,64,3072]{2,1,0:T(8,128)} fusion(f32[2,64,3072]{2,1,0:T(8,128)S(1)} %bitcast.152, bf16[1,64,3072]{2,1,0:T(8,128)(2,1)} %get-tuple-element.51, bf16[1,64,3072]{2,1,0:T(8,128)(2,1)} %get-tuple-element.52), kind=kLoop, calls=%fused_computation.7 | loop fusion | flops 1179648 | bytes 3932160 | tf_op jit(solution)/shard_map/add | solution.py:180
  133.1 2.8 %collective-permute-done.25 = bf16[2,64,3072]{2,1,0:T(8,128)(2,1)} collective-permute-done((bf16[2,64,3072]{2,1,0:T(8,128)(2,1)}, bf16[2,64,3072]{2,1,0:T(8,128)(2,1)}, u32[]{:S(2)}, u32[]{:S(2)}) %collective-permute-start.25) | collective-permute-done | bytes 786464 | tf_op jit(solution)/shard_map/ppermute | solution.py:29
  135.9 1.3 fusion.14
  137.7 6.6 %all-to-all-done.2 = bf16[8,8,3072]{2,1,0:T(8,128)(2,1)} async-done(((bf16[8,8,3072]{2,1,0:T(8,128)(2,1)}), bf16[8,8,3072]{2,1,0:T(8,128)(2,1)}, u32[]{:S(2)}, u32[]{:S(2)}) %all-to-all-start.2) | async-done | bytes 393248 | tf_op jit(solution)/shard_map/all_to_all | solution.py:194
  144.3 1.1 reduce_sum.24
  145.3 2.1 %fusion.12 = bf16[8,8,3072]{2,1,0:T(8,128)(2,1)} fusion(bf16[64,3072]{1,0:T(8,128)(2,1)S(1)} %collective-permute-done.27, f32[2,64,3072]{2,1,0:T(8,128)} %convert_add_fusion, bf16[2,64,3072]{2,1,0:T(8,128)(2,1)} %collective-permute-done.25), kind=kLoop, calls=%fused_computation.23 | loop fusion | flops 983040 | bytes 1966080 | tf_op jit(solution)/shard_map/reshape | solution.py:190
  147.5 5.1 %all-to-all-start.3 = ((bf16[8,8,3072]{2,1,0:T(8,128)(2,1)}), bf16[8,8,3072]{2,1,0:T(8,128)(2,1)S(1)}, u32[]{:S(2)}, u32[]{:S(2)}) async-start(bf16[8,8,3072]{2,1,0:T(8,128)(2,1)} %fusion.12), calls=%async_computation.3 | async-start | bytes 786432 | tf_op jit(solution)/shard_map/all_to_all | solution.py:194
  153.4 4.6 %fusion.26 = f32[3072,768]{1,0:T(8,128)S(1)} fusion(bf16[512,768]{1,0:T(8,128)(2,1)S(1)} %bitcast.141, bf16[64,8,3072]{2,1,0:T(8,128)(2,1)} %copy-done.2), kind=kOutput, calls=%fused_computation.74 | convolution fusion | flops 2415919104 | bytes 13369344 | tf_op jit(solution)/shard_map/dot_general | solution.py:199
  158.0 7.1 %add_convert_fusion = bf16[3072,768]{1,0:T(8,128)(2,1)} fusion(f32[3072,768]{1,0:T(8,128)S(1)} %fusion.26, bf16[512,768]{1,0:T(8,128)(2,1)S(1)} %bitcast.140, bf16[64,8,3072]{2,1,0:T(8,128)(2,1)} %constant_dynamic-update-slice_fusion), kind=kOutput, calls=%fused_computation | convolution fusion | flops 2420637696 | bytes 18087936 | tf_op jit(solution)/shard_map/dot_general | solution.py:199
  (87 shorter events, 14.8 us)
Async XLA Ops:
  0.6 0.9 copy-start
  2.4 21.8 %all-to-all-start = ((bf16[8,8,3072]{2,1,0:T(8,128)(2,1)}), bf16[8,8,3072]{2,1,0:T(8,128)(2,1)S(1)}, u32[]{:S(2)}, u32[]{:S(2)}) async-start(bf16[8,8,3072]{2,1,0:T(8,128)(2,1)} %get-tuple-element.22), calls=%async_computation | async-start | bytes 786432 | tf_op jit(solution)/shard_map/all_to_all | solution.py:138
  24.2 11.5 %collective-permute-start.1 = (bf16[8,8,3072]{2,1,0:T(8,128)(2,1)S(1)}, bf16[8,8,3072]{2,1,0:T(8,128)(2,1)S(1)}, u32[]{:S(2)}, u32[]{:S(2)}) collective-permute-start(bf16[8,8,3072]{2,1,0:T(8,128)(2,1)S(1)} %all-to-all-done), channel_id=1, source_target_pairs={{0,6},{1,3},{2,4},{3,1},{4,2},{5,7},{6,0},{7,5},{8,14},{9,11},{10,... | collective-permute-start | bytes 1179656 | tf_op jit(solution)/shard_map/ppermute | solution.py:29
  27.0 7.8 %collective-permute-start = (bf16[8,8,3072]{2,1,0:T(8,128)(2,1)S(1)}, bf16[8,8,3072]{2,1,0:T(8,128)(2,1)S(1)}, u32[]{:S(2)}, u32[]{:S(2)}) collective-permute-start(bf16[8,8,3072]{2,1,0:T(8,128)(2,1)S(1)} %all-to-all-done), channel_id=1, source_target_pairs={{0,2},{1,7},{2,0},{3,5},{4,6},{5,3},{6,4},{7,1},{8,10},{9,15},{10,... | collective-permute-start | bytes 1179656 | tf_op jit(solution)/shard_map/ppermute | solution.py:29
  27.4 15.9 %all-to-all-start.1 = ((bf16[8,8,3072]{2,1,0:T(8,128)(2,1)}), bf16[8,8,3072]{2,1,0:T(8,128)(2,1)S(1)}, u32[]{:S(2)}, u32[]{:S(2)}) async-start(bf16[8,8,3072]{2,1,0:T(8,128)(2,1)} %get-tuple-element.25), calls=%async_computation.1 | async-start | bytes 786432 | tf_op jit(solution)/shard_map/all_to_all | solution.py:138
  30.8 14.7 %collective-permute-start.3 = (bf16[8,8,3072]{2,1,0:T(8,128)(2,1)S(1)}, bf16[8,8,3072]{2,1,0:T(8,128)(2,1)S(1)}, u32[]{:S(2)}, u32[]{:S(2)}) collective-permute-start(bf16[8,8,3072]{2,1,0:T(8,128)(2,1)S(1)} %all-to-all-done), channel_id=1, source_target_pairs={{0,1},{1,0},{2,3},{3,2},{4,5},{5,4},{6,7},{7,6},{8,9},{9,8},{10,11... | collective-permute-start | bytes 1179656 | tf_op jit(solution)/shard_map/ppermute | solution.py:29
  34.8 13.4 %collective-permute-start.5 = (bf16[8,8,3072]{2,1,0:T(8,128)(2,1)S(1)}, bf16[8,8,3072]{2,1,0:T(8,128)(2,1)S(1)}, u32[]{:S(2)}, u32[]{:S(2)}) collective-permute-start(bf16[8,8,3072]{2,1,0:T(8,128)(2,1)S(1)} %collective-permute-done), channel_id=1, source_target_pairs={{0,1},{1,0},{2,3},{3,2},{4,5},{5,4},{6,7},{7,6},{8,9},{9,8},{10,11... | collective-permute-start | bytes 1179656 | tf_op jit(solution)/shard_map/ppermute | solution.py:29
  34.8 9.0 %collective-permute-start.2 = (bf16[8,8,3072]{2,1,0:T(8,128)(2,1)S(1)}, bf16[8,8,3072]{2,1,0:T(8,128)(2,1)S(1)}, u32[]{:S(2)}, u32[]{:S(2)}) collective-permute-start(bf16[8,8,3072]{2,1,0:T(8,128)(2,1)S(1)} %collective-permute-done), channel_id=1, source_target_pairs={{0,6},{1,3},{2,4},{3,1},{4,2},{5,7},{6,0},{7,5},{8,14},{9,11},{10,... | collective-permute-start | bytes 1179656 | tf_op jit(solution)/shard_map/ppermute | solution.py:29
  35.7 10.6 %collective-permute-start.4 = (bf16[8,8,3072]{2,1,0:T(8,128)(2,1)S(1)}, bf16[8,8,3072]{2,1,0:T(8,128)(2,1)}, u32[]{:S(2)}, u32[]{:S(2)}) collective-permute-start(bf16[8,8,3072]{2,1,0:T(8,128)(2,1)S(1)} %collective-permute-done.1), channel_id=1, source_target_pairs={{0,1},{1,0},{2,3},{3,2},{4,5},{5,4},{6,7},{7,6},{8,9},{9,8},{10,11... | collective-permute-start | bytes 1179656 | tf_op jit(solution)/shard_map/ppermute | solution.py:29
  43.3 6.4 %copy-start.1 = (bf16[3072,768]{1,0:T(8,128)(2,1)S(1)}, bf16[3072,768]{1,0:T(8,128)(2,1)}, u32[]{:S(2)}) copy-start(bf16[3072,768]{1,0:T(8,128)(2,1)} %param.4) | copy-start | bytes 14155780
  43.3 22.7 %collective-permute-start.12 = (bf16[8,8,3072]{2,1,0:T(8,128)(2,1)S(1)}, bf16[8,8,3072]{2,1,0:T(8,128)(2,1)S(1)}, u32[]{:S(2)}, u32[]{:S(2)}) collective-permute-start(bf16[8,8,3072]{2,1,0:T(8,128)(2,1)S(1)} %all-to-all-done.1), channel_id=1, source_target_pairs={{0,1},{1,0},{2,3},{3,2},{4,5},{5,4},{6,7},{7,6},{8,9},{9,8},{10,11... | collective-permute-start | bytes 1179656 | tf_op jit(solution)/shard_map/ppermute | solution.py:29
  43.7 14.0 %collective-permute-start.10 = (bf16[8,8,3072]{2,1,0:T(8,128)(2,1)S(1)}, bf16[8,8,3072]{2,1,0:T(8,128)(2,1)S(1)}, u32[]{:S(2)}, u32[]{:S(2)}) collective-permute-start(bf16[8,8,3072]{2,1,0:T(8,128)(2,1)S(1)} %all-to-all-done.1), channel_id=1, source_target_pairs={{0,6},{1,3},{2,4},{3,1},{4,2},{5,7},{6,0},{7,5},{8,14},{9,11},{10,... | collective-permute-start | bytes 1179656 | tf_op jit(solution)/shard_map/ppermute | solution.py:29
  45.5 9.7 %collective-permute-start.9 = (bf16[8,8,3072]{2,1,0:T(8,128)(2,1)S(1)}, bf16[8,8,3072]{2,1,0:T(8,128)(2,1)S(1)}, u32[]{:S(2)}, u32[]{:S(2)}) collective-permute-start(bf16[8,8,3072]{2,1,0:T(8,128)(2,1)S(1)} %all-to-all-done.1), channel_id=1, source_target_pairs={{0,2},{1,7},{2,0},{3,5},{4,6},{5,3},{6,4},{7,1},{8,10},{9,15},{10,... | collective-permute-start | bytes 1179656 | tf_op jit(solution)/shard_map/ppermute | solution.py:29
  46.3 2.7 %collective-permute-start.6 = (bf16[8,8,3072]{2,1,0:T(8,128)(2,1)S(1)}, bf16[8,8,3072]{2,1,0:T(8,128)(2,1)S(1)}, u32[]{:S(2)}, u32[]{:S(2)}) collective-permute-start(bf16[8,8,3072]{2,1,0:T(8,128)(2,1)S(1)} %collective-permute-done.2), channel_id=1, source_target_pairs={{0,1},{1,0},{2,3},{3,2},{4,5},{5,4},{6,7},{7,6},{8,9},{9,8},{10,11... | collective-permute-start | bytes 1179656 | tf_op jit(solution)/shard_map/ppermute | solution.py:29
  54.3 7.9 %collective-permute-start.7 = (bf16[2,8,16,768]{3,2,1,0:T(8,128)(2,1)S(1)}, bf16[2,8,16,768]{3,2,1,0:T(8,128)(2,1)S(1)}, u32[]{:S(2)}, u32[]{:S(2)}) collective-permute-start(bf16[2,8,16,768]{3,2,1,0:T(8,128)(2,1)S(1)} %pad_maximum_fusion), channel_id=1, source_target_pairs={{0,64},{1,193},{2,66},{3,195},{4,68},{5,197},{6,70},{7,199},{8,72}... | collective-permute-start | bytes 1179656 | tf_op jit(solution)/shard_map/ppermute | solution.py:29
  55.2 11.0 %collective-permute-start.14 = (bf16[8,8,3072]{2,1,0:T(8,128)(2,1)S(1)}, bf16[8,8,3072]{2,1,0:T(8,128)(2,1)S(1)}, u32[]{:S(2)}, u32[]{:S(2)}) collective-permute-start(bf16[8,8,3072]{2,1,0:T(8,128)(2,1)S(1)} %collective-permute-done.9), channel_id=1, source_target_pairs={{0,1},{1,0},{2,3},{3,2},{4,5},{5,4},{6,7},{7,6},{8,9},{9,8},{10,11... | collective-permute-start | bytes 1179656 | tf_op jit(solution)/shard_map/ppermute | solution.py:29
  57.0 9.0 %collective-permute-start.11 = (bf16[8,8,3072]{2,1,0:T(8,128)(2,1)S(1)}, bf16[8,8,3072]{2,1,0:T(8,128)(2,1)S(1)}, u32[]{:S(2)}, u32[]{:S(2)}) collective-permute-start(bf16[8,8,3072]{2,1,0:T(8,128)(2,1)S(1)} %collective-permute-done.9), channel_id=1, source_target_pairs={{0,6},{1,3},{2,4},{3,1},{4,2},{5,7},{6,0},{7,5},{8,14},{9,11},{10,... | collective-permute-start | bytes 1179656 | tf_op jit(solution)/shard_map/ppermute | solution.py:29
  57.8 8.3 %collective-permute-start.13 = (bf16[8,8,3072]{2,1,0:T(8,128)(2,1)S(1)}, bf16[8,8,3072]{2,1,0:T(8,128)(2,1)S(1)}, u32[]{:S(2)}, u32[]{:S(2)}) collective-permute-start(bf16[8,8,3072]{2,1,0:T(8,128)(2,1)S(1)} %collective-permute-done.10), channel_id=1, source_target_pairs={{0,1},{1,0},{2,3},{3,2},{4,5},{5,4},{6,7},{7,6},{8,9},{9,8},{10,11... | collective-permute-start | bytes 1179656 | tf_op jit(solution)/shard_map/ppermute | solution.py:29
  62.4 7.0 %collective-permute-start.8 = (bf16[8,16,768]{2,1,0:T(8,128)(2,1)S(1)}, bf16[8,16,768]{2,1,0:T(8,128)(2,1)S(1)}, u32[]{:S(2)}, u32[]{:S(2)}) collective-permute-start(bf16[8,16,768]{2,1,0:T(8,128)(2,1)S(1)} %get-tuple-element.46), channel_id=1, source_target_pairs={{0,192},{1,65},{2,194},{3,67},{4,196},{5,69},{6,198},{7,71},{8,200... | collective-permute-start | bytes 589832 | tf_op jit(solution)/shard_map/ppermute | solution.py:29
  66.0 4.5 %collective-permute-start.15 = (bf16[8,8,3072]{2,1,0:T(8,128)(2,1)S(1)}, bf16[8,8,3072]{2,1,0:T(8,128)(2,1)S(1)}, u32[]{:S(2)}, u32[]{:S(2)}) collective-permute-start(bf16[8,8,3072]{2,1,0:T(8,128)(2,1)S(1)} %collective-permute-done.11), channel_id=1, source_target_pairs={{0,1},{1,0},{2,3},{3,2},{4,5},{5,4},{6,7},{7,6},{8,9},{9,8},{10,11... | collective-permute-start | bytes 1179656 | tf_op jit(solution)/shard_map/ppermute | solution.py:29
  70.2 7.0 %collective-permute-start.18 = (bf16[8,16,768]{2,1,0:T(8,128)(2,1)S(1)}, bf16[8,16,768]{2,1,0:T(8,128)(2,1)S(1)}, u32[]{:S(2)}, u32[]{:S(2)}) collective-permute-start(bf16[8,16,768]{2,1,0:T(8,128)(2,1)S(1)} %get-tuple-element.28.a_ref), channel_id=1, source_target_pairs={{0,192},{1,65},{2,194},{3,67},{4,196},{5,69},{6,198},{7,71},{8,200... | collective-permute-start | bytes 589832 | tf_op jit(solution)/shard_map/ppermute | solution.py:29
  70.6 2.6 %copy-start.2 = (bf16[64,8,3072]{2,1,0:T(8,128)(2,1)}, bf16[64,8,3072]{2,1,0:T(8,128)(2,1)S(1)}, u32[]{:S(2)}) copy-start(bf16[64,8,3072]{2,1,0:T(8,128)(2,1)S(1)} %constant_dynamic-update-slice_fusion.8) | copy-start | bytes 9437188
  77.2 7.9 %collective-permute-start.19 = (bf16[2,8,16,768]{3,2,1,0:T(8,128)(2,1)S(1)}, bf16[2,8,16,768]{3,2,1,0:T(8,128)(2,1)S(1)}, u32[]{:S(2)}, u32[]{:S(2)}) collective-permute-start(bf16[2,8,16,768]{3,2,1,0:T(8,128)(2,1)S(1)} %pad_maximum_fusion.2), channel_id=1, source_target_pairs={{0,64},{1,193},{2,66},{3,195},{4,68},{5,197},{6,70},{7,199},{8,72}... | collective-permute-start | bytes 1179656 | tf_op jit(solution)/shard_map/ppermute | solution.py:29
  77.4 11.9 %collective-permute-start.16 = (bf16[2,8,16,768]{3,2,1,0:T(8,128)(2,1)S(1)}, bf16[2,8,16,768]{3,2,1,0:T(8,128)(2,1)S(1)}, u32[]{:S(2)}, u32[]{:S(2)}) collective-permute-start(bf16[2,8,16,768]{3,2,1,0:T(8,128)(2,1)S(1)} %pad_maximum_fusion.1), channel_id=1, source_target_pairs={{0,64},{1,193},{2,66},{3,195},{4,68},{5,197},{6,70},{7,199},{8,72}... | collective-permute-start | bytes 1179656 | tf_op jit(solution)/shard_map/ppermute | solution.py:29
  87.2 4.2 %collective-permute-start.20 = (bf16[4,64,3072]{2,1,0:T(8,128)(2,1)S(1)}, bf16[4,64,3072]{2,1,0:T(8,128)(2,1)S(1)}, u32[]{:S(2)}, u32[]{:S(2)}) collective-permute-start(bf16[4,64,3072]{2,1,0:T(8,128)(2,1)S(1)} %bitcast.163), channel_id=1, source_target_pairs={{0,1},{1,0},{2,3},{3,2},{4,5},{5,4},{6,7},{7,6},{8,9},{9,8},{10,11... | collective-permute-start | bytes 4718600 | tf_op jit(solution)/shard_map/ppermute | solution.py:29
  89.5 7.0 %collective-permute-start.17 = (bf16[8,16,768]{2,1,0:T(8,128)(2,1)S(1)}, bf16[8,16,768]{2,1,0:T(8,128)(2,1)S(1)}, u32[]{:S(2)}, u32[]{:S(2)}) collective-permute-start(bf16[8,16,768]{2,1,0:T(8,128)(2,1)S(1)} %get-tuple-element.47), channel_id=1, source_target_pairs={{0,192},{1,65},{2,194},{3,67},{4,196},{5,69},{6,198},{7,71},{8,200... | collective-permute-start | bytes 589832 | tf_op jit(solution)/shard_map/ppermute | solution.py:29
  91.8 14.4 %collective-permute-start.23 = (bf16[2,64,3072]{2,1,0:T(8,128)(2,1)S(1)}, bf16[2,64,3072]{2,1,0:T(8,128)(2,1)S(1)}, u32[]{:S(2)}, u32[]{:S(2)}) collective-permute-start(bf16[2,64,3072]{2,1,0:T(8,128)(2,1)S(1)} %add_convert_fusion.2), channel_id=1, source_target_pairs={{0,6},{1,3},{2,4},{3,1},{4,2},{5,7},{6,0},{7,5},{8,14},{9,11},{10,... | collective-permute-start | bytes 2359304 | tf_op jit(solution)/shard_map/ppermute | solution.py:29
  97.3 8.8 %collective-permute-start.21 = (bf16[8,16,768]{2,1,0:T(8,128)(2,1)S(1)}, bf16[8,16,768]{2,1,0:T(8,128)(2,1)S(1)}, u32[]{:S(2)}, u32[]{:S(2)}) collective-permute-start(bf16[8,16,768]{2,1,0:T(8,128)(2,1)S(1)} %get-tuple-element.31.a_ref), channel_id=1, source_target_pairs={{0,192},{1,65},{2,194},{3,67},{4,196},{5,69},{6,198},{7,71},{8,200... | collective-permute-start | bytes 589832 | tf_op jit(solution)/shard_map/ppermute | solution.py:29
  106.1 7.9 %collective-permute-start.22 = (bf16[2,8,16,768]{3,2,1,0:T(8,128)(2,1)S(1)}, bf16[2,8,16,768]{3,2,1,0:T(8,128)(2,1)S(1)}, u32[]{:S(2)}, u32[]{:S(2)}) collective-permute-start(bf16[2,8,16,768]{3,2,1,0:T(8,128)(2,1)S(1)} %pad_maximum_fusion.3), channel_id=1, source_target_pairs={{0,64},{1,193},{2,66},{3,195},{4,68},{5,197},{6,70},{7,199},{8,72}... | collective-permute-start | bytes 1179656 | tf_op jit(solution)/shard_map/ppermute | solution.py:29
  116.1 4.2 %collective-permute-start.24 = (bf16[4,64,3072]{2,1,0:T(8,128)(2,1)S(1)}, bf16[4,64,3072]{2,1,0:T(8,128)(2,1)S(1)}, u32[]{:S(2)}, u32[]{:S(2)}) collective-permute-start(bf16[4,64,3072]{2,1,0:T(8,128)(2,1)S(1)} %bitcast.164), channel_id=1, source_target_pairs={{0,1},{1,0},{2,3},{3,2},{4,5},{5,4},{6,7},{7,6},{8,9},{9,8},{10,11... | collective-permute-start | bytes 4718600 | tf_op jit(solution)/shard_map/ppermute | solution.py:29
  116.4 8.2 %collective-permute-start.26 = (bf16[64,3072]{1,0:T(8,128)(2,1)S(1)}, bf16[64,3072]{1,0:T(8,128)(2,1)S(1)}, u32[]{:S(2)}, u32[]{:S(2)}) collective-permute-start(bf16[64,3072]{1,0:T(8,128)(2,1)S(1)} %fusion.11), channel_id=1, source_target_pairs={{0,2},{1,7},{2,0},{3,5},{4,6},{5,3},{6,4},{7,1},{8,10},{9,15},{10,... | collective-permute-start | bytes 1179656 | tf_op jit(solution)/shard_map/ppermute | solution.py:29
  122.4 13.5 %collective-permute-start.25 = (bf16[2,64,3072]{2,1,0:T(8,128)(2,1)}, bf16[2,64,3072]{2,1,0:T(8,128)(2,1)}, u32[]{:S(2)}, u32[]{:S(2)}) collective-permute-start(bf16[2,64,3072]{2,1,0:T(8,128)(2,1)} %add_convert_fusion.1), channel_id=1, source_target_pairs={{0,6},{1,3},{2,4},{3,1},{4,2},{5,7},{6,0},{7,5},{8,14},{9,11},{10,... | collective-permute-start | bytes 2359304 | tf_op jit(solution)/shard_map/ppermute | solution.py:29
  125.5 18.8 %all-to-all-start.2 = ((bf16[8,8,3072]{2,1,0:T(8,128)(2,1)}), bf16[8,8,3072]{2,1,0:T(8,128)(2,1)}, u32[]{:S(2)}, u32[]{:S(2)}) async-start(bf16[8,8,3072]{2,1,0:T(8,128)(2,1)} %fusion.13), calls=%async_computation.2 | async-start | bytes 786432 | tf_op jit(solution)/shard_map/all_to_all | solution.py:194
  137.2 8.2 %collective-permute-start.27 = (bf16[64,3072]{1,0:T(8,128)(2,1)S(1)}, bf16[64,3072]{1,0:T(8,128)(2,1)S(1)}, u32[]{:S(2)}, u32[]{:S(2)}) collective-permute-start(bf16[64,3072]{1,0:T(8,128)(2,1)S(1)} %fusion.14), channel_id=1, source_target_pairs={{0,2},{1,7},{2,0},{3,5},{4,6},{5,3},{6,4},{7,1},{8,10},{9,15},{10,... | collective-permute-start | bytes 1179656 | tf_op jit(solution)/shard_map/ppermute | solution.py:29
  147.5 17.6 %all-to-all-start.3 = ((bf16[8,8,3072]{2,1,0:T(8,128)(2,1)}), bf16[8,8,3072]{2,1,0:T(8,128)(2,1)S(1)}, u32[]{:S(2)}, u32[]{:S(2)}) async-start(bf16[8,8,3072]{2,1,0:T(8,128)(2,1)} %fusion.12), calls=%async_computation.3 | async-start | bytes 786432 | tf_op jit(solution)/shard_map/all_to_all | solution.py:194
